TPU v7x, 32 devices: a whole 2x2x4 slice. The times are simulated.
32 devices in a mesh: dp: 4 (over y, x), ctx: 8 (over z, core).
Axes of the slice: x: 2, y: 2, z: 4, core: 2. Of those that a mesh axis runs over, the one named last changes fastest.
Arguments:
- tokens_in: bfloat16 [4, 2048, 1024], P('dp', 'ctx'), may hold values from -6 to 6
- positions: int32 [4, 2048], P('dp', 'ctx'), may hold values from 0 to 1023, as said below
- out_grad: bfloat16 [4, 2048, 1024], P('dp', 'ctx'), may hold values from -6 to 6
- w_qkv: float32 [1024, 2048], P(('dp', 'ctx')), may hold values from -0.1875 to 0.1875
- w_output: float32 [1024, 1024], P(('dp', 'ctx')), may hold values from -2 to 2
- w_gate_up: float32 [1024, 9216], P(('dp', 'ctx')), may hold values from -0.1875 to 0.1875
- w_down: float32 [1024, 4608], P(('dp', 'ctx')), may hold values from -0.09375 to 0.09375
- norm_gains: float32 [2176], P(('dp', 'ctx')), may hold values from -0.3 to 0.3
- first_qkv: float32 [1024, 2048], P(('dp', 'ctx')), may hold values from -16 to 16
- first_output: float32 [1024, 1024], P(('dp', 'ctx')), may hold values from -24 to 24
- first_gate_up: float32 [1024, 9216], P(('dp', 'ctx')), may hold values from -40 to 40
- first_down: float32 [1024, 4608], P(('dp', 'ctx')), may hold values from -96 to 96
- first_gains: float32 [2176], P(('dp', 'ctx')), may hold values from -80 to 80
- second_qkv: float32 [1024, 2048], P(('dp', 'ctx')), may hold values from 1556.48 to 6225.92
- second_output: float32 [1024, 1024], P(('dp', 'ctx')), may hold values from 62.2592 to 249.0368
- second_gate_up: float32 [1024, 9216], P(('dp', 'ctx')), may hold values from 194.56 to 778.24
- second_down: float32 [1024, 4608], P(('dp', 'ctx')), may hold values from 700.416 to 2801.664
- second_gains: float32 [2176], P(('dp', 'ctx')), may hold values from 778.24 to 3112.96
Outputs:
- block_out: bfloat16 [4, 2048, 1024], P('dp', 'ctx')
- input_grad: float32 [4, 2048, 1024], P('dp', 'ctx')
- grad_qkv: float32 [1024, 2048], P(('dp', 'ctx'))
- grad_output: float32 [1024, 1024], P(('dp', 'ctx'))
- grad_gate_up: float32 [1024, 9216], P(('dp', 'ctx'))
- grad_down: float32 [1024, 4608], P(('dp', 'ctx'))
- grad_gains: float32 [2176], P(('dp', 'ctx'))
- new_qkv: float32 [1024, 2048], P(('dp', 'ctx'))
- new_output: float32 [1024, 1024], P(('dp', 'ctx'))
- new_gate_up: float32 [1024, 9216], P(('dp', 'ctx'))
- new_down: float32 [1024, 4608], P(('dp', 'ctx'))
- new_gains: float32 [2176], P(('dp', 'ctx'))
- new_first_qkv: float32 [1024, 2048], P(('dp', 'ctx'))
- new_first_output: float32 [1024, 1024], P(('dp', 'ctx'))
- new_first_gate_up: float32 [1024, 9216], P(('dp', 'ctx'))
- new_first_down: float32 [1024, 4608], P(('dp', 'ctx'))
- new_first_gains: float32 [2176], P(('dp', 'ctx'))
- new_second_qkv: float32 [1024, 2048], P(('dp', 'ctx'))
- new_second_output: float32 [1024, 1024], P(('dp', 'ctx'))
- new_second_gate_up: float32 [1024, 9216], P(('dp', 'ctx'))
- new_second_down: float32 [1024, 4608], P(('dp', 'ctx'))
- new_second_gains: float32 [2176], P(('dp', 'ctx'))
Inputs may be any that keep to these rules, and one draw needn't show every extreme that they name: `positions`: each sequence holds four documents end to end and a token's position counts from its document's first token; one document of each sequence is 1024 tokens long, the other three shorter.
All inputs are finite; a program needn't handle non-finite values.
Results may differ from a plain program's by a relative error of at most 0.015.
The roundings to bfloat16 on the way count: a program that leaves them out, or rounds other values in their place, can miss the bound.
Values may be sent and summed in bfloat16 or wider, within the bound.
A program may use at most 256 MiB of HBM per device.

v0:
```python
import math

import jax
import jax.numpy as jnp
from jax import lax
from jax.sharding import PartitionSpec as P

D = 1024
HEADS = 16
KV_HEADS = 8
HEAD_DIM = 64
STEP = 4
HQ = 1024
HK = 512


EPS = 1e-05
THETA = 1000000.0
NEG_BIG = -1e30
BETA_ONE = 0.9
BETA_TWO = 0.95
ADAM_EPS = 1e-08
CONTRACT_LAST = (((1,), (1,)), ((), ()))
CONTRACT_ROWS = (((0,), (0,)), ((), ()))


def from_behind(block, axis, distance):
    devices = range(lax.axis_size(axis))
    route = [(i - distance, i) for i in devices if i - distance in devices]
    return lax.ppermute(block, axis, route)


def shifted(value, axis, steps):
    count = lax.axis_size(axis)
    pairs = [(source, (source + steps) % count) for source in range(count)]
    return lax.ppermute(value, axis, pairs)


def norm_forward(values, gain):
    recip = lax.rsqrt(jnp.mean(values * values, axis=-1, keepdims=True) + EPS)
    unit = values * recip
    return (unit * gain, unit, recip)


def norm_backward(grad, gain, unit, recip):
    scaled = grad * gain
    inner = jnp.mean(scaled * unit, axis=-1, keepdims=True)
    grad_in = recip * (scaled - unit * inner)
    grad_gain = jnp.sum((grad * unit).reshape(-1, unit.shape[-1]), axis=0)
    return (grad_in, grad_gain)


def rope_tables(places):
    half = HEAD_DIM // 2
    freqs = jnp.exp(-math.log(THETA) * (2.0 * jnp.arange(half, dtype=jnp.float32) / HEAD_DIM))
    angles = places.astype(jnp.float32)[:, None] * freqs[None, :]
    return (jnp.cos(angles)[:, None, :], jnp.sin(angles)[:, None, :])


def rotate(values, cosine, sine):
    half = HEAD_DIM // 2
    first_half = values[..., :half]
    second_half = values[..., half:]
    return jnp.concatenate(
        [first_half * cosine - second_half * sine, second_half * cosine + first_half * sine],
        axis=-1,
    )


def unrotate(grad, cosine, sine):
    half = HEAD_DIM // 2
    first_half = grad[..., :half]
    second_half = grad[..., half:]
    return jnp.concatenate(
        [first_half * cosine + second_half * sine, second_half * cosine - first_half * sine],
        axis=-1,
    )


def split_gains(gains_used):
    return (
        gains_used[:D],
        gains_used[D : 2 * D],
        gains_used[2 * D : 2 * D + HEAD_DIM],
        gains_used[2 * D + HEAD_DIM :],
    )


def front_pass(tokens_f, places, weight_qkv, gains_used):
    gain_attn, gain_ffn, gain_query, gain_key = split_gains(gains_used)
    normed, unit_in, recip_in = norm_forward(tokens_f, gain_attn)
    attn_in = normed.astype(jnp.bfloat16)
    projected = jnp.dot(attn_in, weight_qkv, preferred_element_type=jnp.float32)
    count = tokens_f.shape[0]
    query = projected[:, :HQ].reshape(count, HEADS, HEAD_DIM)
    key_raw = projected[:, HQ : HQ + HK].reshape(count, KV_HEADS, HEAD_DIM)
    value_b = projected[:, HQ + HK :].astype(jnp.bfloat16).reshape(count, KV_HEADS, HEAD_DIM)
    cosine, sine = rope_tables(places)
    query_n, unit_q, recip_q = norm_forward(query, gain_query)
    key_n, unit_k, recip_k = norm_forward(key_raw, gain_key)
    query_b = rotate(query_n, cosine, sine).astype(jnp.bfloat16)
    key_b = rotate(key_n, cosine, sine).astype(jnp.bfloat16)
    saved = (attn_in, unit_in, recip_in, unit_q, recip_q, unit_k, recip_k, cosine, sine)
    return (query_b, key_b, value_b, saved)


def ffn_forward(tokens_f, attn_out, weight_output, weight_gate_up, weight_down, gain_ffn):
    mixed = tokens_f + jnp.dot(attn_out, weight_output, preferred_element_type=jnp.float32)
    normed, unit_f, recip_f = norm_forward(mixed, gain_ffn)
    ffn_in = normed.astype(jnp.bfloat16)
    gate_up = jnp.dot(ffn_in, weight_gate_up, preferred_element_type=jnp.float32)
    width = gate_up.shape[1] // 2
    gate = gate_up[:, :width]
    upper = gate_up[:, width:]
    sigma = jax.nn.sigmoid(gate)
    active = gate * sigma
    middle = (active * upper).astype(jnp.bfloat16)
    block_out = (
        mixed
        + lax.dot_general(middle, weight_down, CONTRACT_LAST, preferred_element_type=jnp.float32)
    ).astype(jnp.bfloat16)
    return (block_out, (unit_f, recip_f, ffn_in, gate, upper, sigma, active, middle))


def ffn_backward(cotangent, attn_out, weight_output, weight_gate_up, weight_down, gain_ffn, kept):
    unit_f, recip_f, ffn_in, gate, upper, sigma, active, middle = kept
    grad_down = lax.dot_general(
        cotangent, middle, CONTRACT_ROWS, preferred_element_type=jnp.float32
    )
    grad_middle = jnp.dot(cotangent, weight_down, preferred_element_type=jnp.float32)
    grad_gate = grad_middle * upper * sigma * (1.0 + gate * (1.0 - sigma))
    grad_upper = grad_middle * active
    grad_pair = jnp.concatenate([grad_gate, grad_upper], axis=1).astype(jnp.bfloat16)
    grad_gate_up = lax.dot_general(
        ffn_in, grad_pair, CONTRACT_ROWS, preferred_element_type=jnp.float32
    )
    grad_normed = lax.dot_general(
        grad_pair, weight_gate_up, CONTRACT_LAST, preferred_element_type=jnp.float32
    )
    grad_from_norm, grad_gain_ffn = norm_backward(grad_normed, gain_ffn, unit_f, recip_f)
    grad_mixed = cotangent.astype(jnp.float32) + grad_from_norm
    grad_mixed_b = grad_mixed.astype(jnp.bfloat16)
    grad_output = lax.dot_general(
        attn_out, grad_mixed_b, CONTRACT_ROWS, preferred_element_type=jnp.float32
    )
    grad_attn = lax.dot_general(
        grad_mixed_b, weight_output, CONTRACT_LAST, preferred_element_type=jnp.float32
    ).astype(jnp.bfloat16)
    return (grad_mixed, grad_output, grad_gate_up, grad_down, grad_gain_ffn, grad_attn)


def tail_pass(grad_query, grad_key, grad_value, saved, gains_used, weight_qkv, grad_mixed):
    gain_attn, gain_ffn, gain_query, gain_key = split_gains(gains_used)
    attn_in, unit_in, recip_in, unit_q, recip_q, unit_k, recip_k, cosine, sine = saved
    count = attn_in.shape[0]
    grad_q, grad_gain_q = norm_backward(
        unrotate(grad_query, cosine, sine), gain_query, unit_q, recip_q
    )
    grad_k, grad_gain_k = norm_backward(unrotate(grad_key, cosine, sine), gain_key, unit_k, recip_k)
    grad_proj = jnp.concatenate(
        [grad_q.reshape(count, HQ), grad_k.reshape(count, HK), grad_value.reshape(count, HK)],
        axis=1,
    ).astype(jnp.bfloat16)
    grad_qkv = lax.dot_general(
        attn_in, grad_proj, CONTRACT_ROWS, preferred_element_type=jnp.float32
    )
    grad_normed = lax.dot_general(
        grad_proj, weight_qkv, CONTRACT_LAST, preferred_element_type=jnp.float32
    )
    grad_in, grad_gain_attn = norm_backward(grad_normed, gain_attn, unit_in, recip_in)
    return (grad_mixed + grad_in, grad_qkv, grad_gain_attn, grad_gain_q, grad_gain_k)


def adam_step(weight, grad, first, second, rate, decay):
    first_new = BETA_ONE * first + (1.0 - BETA_ONE) * grad
    second_new = BETA_TWO * second + (1.0 - BETA_TWO) * grad * grad
    first_hat = first_new / (1.0 - BETA_ONE**STEP)
    second_hat = second_new / (1.0 - BETA_TWO**STEP)
    weight_new = weight - rate * (first_hat / (jnp.sqrt(second_hat) + ADAM_EPS) + decay * weight)
    return (weight_new, first_new, second_new)


def allowed_mask(query_index, lower, key_index):
    return (key_index[None, :] <= query_index[:, None]) & (key_index[None, :] >= lower[:, None])


def forward_block(state, query_g, query_index, lower, keys, values, key_index):
    running, totals, accum = state
    scores = jnp.einsum(
        "qkgd,tkd->kgqt", query_g, keys, preferred_element_type=jnp.float32
    ) * HEAD_DIM ** (-0.5)
    allowed = allowed_mask(query_index, lower, key_index)
    peak = jnp.maximum(running, jnp.max(jnp.where(allowed, scores, NEG_BIG), axis=-1))
    weights = jnp.where(allowed, jnp.exp(scores - peak[..., None]), 0.0)
    factor = jnp.exp(running - peak)
    totals = totals * factor + jnp.sum(weights, axis=-1)
    accum = accum * factor[..., None] + jnp.einsum(
        "kgqt,tkd->kgqd", weights.astype(jnp.bfloat16), values, preferred_element_type=jnp.float32
    )
    return (peak, totals, accum)


def backward_block(query_g, grad_attn, delta, logsum, query_index, lower, keys, values, key_index):
    scale = HEAD_DIM ** (-0.5)
    scores = jnp.einsum("qkgd,tkd->kgqt", query_g, keys, preferred_element_type=jnp.float32) * scale
    allowed = allowed_mask(query_index, lower, key_index)
    probs = jnp.where(allowed, jnp.exp(scores - logsum[..., None]), 0.0)
    grad_values = jnp.einsum(
        "kgqt,qkgd->tkd", probs.astype(jnp.bfloat16), grad_attn, preferred_element_type=jnp.float32
    )
    grad_probs = jnp.einsum("qkgd,tkd->kgqt", grad_attn, values, preferred_element_type=jnp.float32)
    grad_scores = (scale * probs * (grad_probs - delta[..., None])).astype(jnp.bfloat16)
    grad_query = jnp.einsum("kgqt,tkd->qkgd", grad_scores, keys, preferred_element_type=jnp.float32)
    grad_keys = jnp.einsum(
        "kgqt,qkgd->tkd", grad_scores, query_g, preferred_element_type=jnp.float32
    )
    return (grad_query, grad_keys, grad_values)


def per_device(
    tokens_in,
    positions,
    out_grad,
    w_qkv,
    w_output,
    w_gate_up,
    w_down,
    norm_gains,
    first_qkv,
    first_output,
    first_gate_up,
    first_down,
    first_gains,
    second_qkv,
    second_output,
    second_gate_up,
    second_down,
    second_gains,
):
    qkv_b, output_b, gate_up_b, down_b, gains_b = (
        lax.all_gather(w_qkv.astype(jnp.bfloat16), ("dp", "ctx"), axis=0, tiled=True),
        lax.all_gather(w_output.astype(jnp.bfloat16), ("dp", "ctx"), axis=0, tiled=True),
        lax.all_gather(w_gate_up.astype(jnp.bfloat16), ("dp", "ctx"), axis=0, tiled=True),
        lax.all_gather(w_down.astype(jnp.bfloat16), ("dp", "ctx"), axis=0, tiled=True),
        lax.all_gather(norm_gains.astype(jnp.bfloat16), ("dp", "ctx"), axis=0, tiled=True),
    )
    gains_used = 1.0 + gains_b.astype(jnp.float32)
    gain_ffn = split_gains(gains_used)[1]
    seq_count = tokens_in.shape[0]
    count = tokens_in.shape[1]
    all_rows = seq_count * count
    group_size = HEADS // KV_HEADS
    tokens_f = tokens_in.reshape(all_rows, D).astype(jnp.float32)
    places_flat = positions.reshape(all_rows)
    cotangent = out_grad.reshape(all_rows, D)
    query_b, key_b, value_b, saved = front_pass(tokens_f, places_flat, qkv_b, gains_used)
    query_g = query_b.reshape(seq_count, count, KV_HEADS, group_size, HEAD_DIM)
    cycle_index = lax.axis_index("ctx")
    cycle_size = lax.axis_size("ctx")
    local_rows = jnp.arange(count, dtype=jnp.int32)
    query_index = cycle_index * count + local_rows
    lower = query_index[None, :] - positions
    kv_local = jnp.stack(
        [key_b.reshape(seq_count, count, HK), value_b.reshape(seq_count, count, HK)]
    )
    turns = cycle_size // 2
    forward_many = jax.vmap(forward_block, in_axes=(0, 0, None, 0, 0, 0, None))
    backward_many = jax.vmap(backward_block, in_axes=(0, 0, 0, 0, None, 0, 0, 0, None))

    def visit_forward(state, block, anchor):

        def compute_state(state_now):
            key_index = anchor % cycle_size * count + local_rows
            keys = block[0].reshape(seq_count, count, KV_HEADS, HEAD_DIM)
            values = block[1].reshape(seq_count, count, KV_HEADS, HEAD_DIM)
            return forward_many(state_now, query_g, query_index, lower, keys, values, key_index)

        def keep_state(state_now):
            return state_now

        return lax.cond(anchor >= 0, compute_state, keep_state, state)

    state = (
        jnp.full((seq_count, KV_HEADS, group_size, count), NEG_BIG, jnp.float32),
        jnp.zeros((seq_count, KV_HEADS, group_size, count), jnp.float32),
        jnp.zeros((seq_count, KV_HEADS, group_size, count, HEAD_DIM), jnp.float32),
    )

    def forward_turn(step, carry):
        state_now, block = carry
        state_now = visit_forward(state_now, block, cycle_index - step)
        block = from_behind(block, "ctx", 1)
        return (state_now, block)

    state, block = lax.fori_loop(0, turns, forward_turn, (state, kv_local))
    state = visit_forward(state, block, cycle_index - turns)
    peak, totals, accum = state
    attn_out4 = (accum / totals[..., None]).transpose(0, 3, 1, 2, 4).astype(jnp.bfloat16)
    logsum = peak + jnp.log(totals)
    attn_out = attn_out4.reshape(all_rows, HQ)
    block_out, kept = ffn_forward(tokens_f, attn_out, output_b, gate_up_b, down_b, gain_ffn)
    grad_mixed, grad_output, grad_gate_up, grad_down, grad_gain_ffn, grad_attn = ffn_backward(
        cotangent, attn_out, output_b, gate_up_b, down_b, gain_ffn, kept
    )
    grad_attn4 = grad_attn.reshape(seq_count, count, KV_HEADS, group_size, HEAD_DIM)
    delta = jnp.einsum(
        "sqkgd,sqkgd->skgq", grad_attn4, attn_out4, preferred_element_type=jnp.float32
    )
    query_zero = jnp.zeros((seq_count, count, KV_HEADS, group_size, HEAD_DIM), jnp.float32)
    kv_zero = jnp.zeros((2, seq_count, count, HK), jnp.float32)

    def visit_backward(block, anchor):

        def compute_grads(unused):
            key_index = anchor % cycle_size * count + local_rows
            keys = block[0].reshape(seq_count, count, KV_HEADS, HEAD_DIM)
            values = block[1].reshape(seq_count, count, KV_HEADS, HEAD_DIM)
            add_query, add_keys, add_values = backward_many(
                query_g, grad_attn4, delta, logsum, query_index, lower, keys, values, key_index
            )
            return (
                add_query,
                jnp.stack(
                    [
                        add_keys.reshape(seq_count, count, HK),
                        add_values.reshape(seq_count, count, HK),
                    ]
                ),
            )

        def no_grads(unused):
            return (query_zero, kv_zero)

        return lax.cond(anchor >= 0, compute_grads, no_grads, 0)

    def pass_grads(pending):
        return shifted(pending.astype(jnp.bfloat16), "ctx", 1).astype(pending.dtype)

    def backward_turn(step, carry):
        grad_query, block, pending = carry
        add_query, add_kv = visit_backward(block, cycle_index - step)
        pending = pass_grads(pending + add_kv)
        block = from_behind(block, "ctx", 1)
        return (grad_query + add_query, block, pending)

    grad_query, block, pending = lax.fori_loop(
        0, turns, backward_turn, (query_zero, kv_local, kv_zero)
    )
    add_query, add_kv = visit_backward(block, cycle_index - turns)
    grad_query = grad_query + add_query
    grad_kv = shifted((pending + add_kv).astype(jnp.bfloat16), "ctx", -turns).astype(jnp.float32)
    grad_key = grad_kv[0].reshape(all_rows, KV_HEADS, HEAD_DIM)
    grad_value = grad_kv[1].reshape(all_rows, KV_HEADS, HEAD_DIM)
    input_grad, grad_qkv, grad_gain_attn, grad_gain_q, grad_gain_k = tail_pass(
        grad_query.reshape(all_rows, HEADS, HEAD_DIM),
        grad_key,
        grad_value,
        saved,
        gains_used,
        qkv_b,
        grad_mixed,
    )
    grad_gains = jnp.concatenate([grad_gain_attn, grad_gain_ffn, grad_gain_q, grad_gain_k])
    shard_qkv, shard_output, shard_gate_up, shard_down, shard_gains = (
        lax.psum_scatter(grad_qkv, ("dp", "ctx"), scatter_dimension=0, tiled=True),
        lax.psum_scatter(grad_output, ("dp", "ctx"), scatter_dimension=0, tiled=True),
        lax.psum_scatter(grad_gate_up, ("dp", "ctx"), scatter_dimension=0, tiled=True),
        lax.psum_scatter(grad_down, ("dp", "ctx"), scatter_dimension=0, tiled=True),
        lax.psum_scatter(grad_gains, ("dp", "ctx"), scatter_dimension=0, tiled=True),
    )
    new_qkv, new_first_qkv, new_second_qkv = adam_step(
        w_qkv, shard_qkv, first_qkv, second_qkv, 0.02, 0.1
    )
    new_output, new_first_output, new_second_output = adam_step(
        w_output, shard_output, first_output, second_output, 0.2, 0.1
    )
    new_gate_up, new_first_gate_up, new_second_gate_up = adam_step(
        w_gate_up, shard_gate_up, first_gate_up, second_gate_up, 0.02, 0.1
    )
    new_down, new_first_down, new_second_down = adam_step(
        w_down, shard_down, first_down, second_down, 0.02, 0.1
    )
    new_gains, new_first_gains, new_second_gains = adam_step(
        norm_gains, shard_gains, first_gains, second_gains, 0.1, 0.0
    )
    return (
        block_out.reshape(seq_count, count, D),
        input_grad.reshape(seq_count, count, D),
        shard_qkv,
        shard_output,
        shard_gate_up,
        shard_down,
        shard_gains,
        new_qkv,
        new_output,
        new_gate_up,
        new_down,
        new_gains,
        new_first_qkv,
        new_first_output,
        new_first_gate_up,
        new_first_down,
        new_first_gains,
        new_second_qkv,
        new_second_output,
        new_second_gate_up,
        new_second_down,
        new_second_gains,
    )


def solution(mesh):
    in_specs = (
        P("dp", "ctx", None),
        P("dp", "ctx"),
        P("dp", "ctx", None),
        P(("dp", "ctx"), None),
        P(("dp", "ctx"), None),
        P(("dp", "ctx"), None),
        P(("dp", "ctx"), None),
        P(("dp", "ctx")),
        P(("dp", "ctx"), None),
        P(("dp", "ctx"), None),
        P(("dp", "ctx"), None),
        P(("dp", "ctx"), None),
        P(("dp", "ctx")),
        P(("dp", "ctx"), None),
        P(("dp", "ctx"), None),
        P(("dp", "ctx"), None),
        P(("dp", "ctx"), None),
        P(("dp", "ctx")),
    )
    out_specs = (
        P("dp", "ctx", None),
        P("dp", "ctx", None),
        P(("dp", "ctx"), None),
        P(("dp", "ctx"), None),
        P(("dp", "ctx"), None),
        P(("dp", "ctx"), None),
        P(("dp", "ctx")),
        P(("dp", "ctx"), None),
        P(("dp", "ctx"), None),
        P(("dp", "ctx"), None),
        P(("dp", "ctx"), None),
        P(("dp", "ctx")),
        P(("dp", "ctx"), None),
        P(("dp", "ctx"), None),
        P(("dp", "ctx"), None),
        P(("dp", "ctx"), None),
        P(("dp", "ctx")),
        P(("dp", "ctx"), None),
        P(("dp", "ctx"), None),
        P(("dp", "ctx"), None),
        P(("dp", "ctx"), None),
        P(("dp", "ctx")),
    )
    return jax.shard_map(
        per_device, mesh=mesh, in_specs=in_specs, out_specs=out_specs, check_vma=False
    )
```

profile of v0, /device:TPU:0, one launch (start us, length us, event | category | flops | bytes accessed | tf_op | source)
XLA Modules:
  0.0 1282.6 jit_solution(5196788909961721733)
XLA Ops:
  15.0 42.3 %all-reduce = bf16[2176]{0:T(1024)(128)(2,1)S(1)} all-reduce(bf16[2176]{0:T(1024)(128)(2,1)S(1)} %dynamic-update-slice), channel_id=1, replica_groups=mesh['dp'=4,'ctx'=8] {'dp','ctx'}, use_global_device_ids=true, to_apply=%add | all-reduce | flops 2176 | bytes 8704
  57.9 18.6 %all-gather.5.cloned.1.call-done = bf16[1024,2048]{1,0:T(8,128)(2,1)} async-done(((bf16[32,2048]{1,0:T(8,128)(2,1)}), bf16[1024,2048]{1,0:T(8,128)(2,1)}) %all-gather.5.cloned.1.call-update) | async-done | bytes 4194320 | tf_op jit(solution)/shard_map/all_gather | solution.py:241
  76.6 3.5 fusion.135
  86.9 44.4 %while.38 = (s32[]{:T(128)}, f32[1,8,2,256]{3,2,1,0:T(2,128)S(1)}, f32[1,8,2,256]{3,2,1,0:T(2,128)S(1)}, f32[1,8,2,256,64]{3,4,2,1,0:T(8,128)S(1)}, bf16[2,1,256...) while((s32[]{:T(128)}, f32[1,8,2,256]{3,2,1,0:T(2,128)S(1)}, ...), condition=%wide.region_8.9_spmd.clone, body=%wide.region_3.8_spmd.clone.sunk | while | flops 280703488 | bytes 20455864 | solution.py:295
  90.0 4.1 conditional.10
  94.9 6.3 collective-permute-start
  103.6 10.9 collective-permute-start
  117.1 12.6 collective-permute-start
  132.6 2.8 all-gather.7.cloned.1.call-done
  135.4 2.6 multiply_reduce_fusion.3
  138.0 124.7 %all-gather.9.cloned.1.call-done = bf16[1024,9216]{1,0:T(8,128)(2,1)} async-done(((bf16[32,9216]{1,0:T(8,128)(2,1)}), bf16[1024,9216]{1,0:T(8,128)(2,1)}) %all-gather.9.cloned.1.call-update) | async-done | bytes 18874384 | tf_op jit(solution)/shard_map/all_gather | solution.py:243
  262.7 14.0 %fusion.143 = f32[256,9216]{1,0:T(8,128)} fusion(bf16[1024,9216]{1,0:T(8,128)(2,1)} %all-gather.9.cloned.1.call-done, f32[256,1024]{1,0:T(8,128)S(1)} %get-tuple-element.967, f32[1024]{0:T(1024)S(1)} %get-tuple-element.958, f32[256]{0:T(256)S(1)} %add_rsqrt_fusion.2), kind=kOutput, calls=%fused_computation.226 | convolution fusion | flops 4832624640 | bytes 29365248 | tf_op jit(solution)/shard_map/dot_general | solution.py:111
  276.7 69.8 %all-gather.11.cloned.1.call-done = bf16[1024,4608]{1,0:T(8,128)(2,1)} async-done(((bf16[32,4608]{1,0:T(8,128)(2,1)}), bf16[1024,4608]{1,0:T(8,128)(2,1)}) %all-gather.11.cloned.1.call-update) | async-done | bytes 9437200 | tf_op jit(solution)/shard_map/all_gather | solution.py:244
  346.5 11.2 multiply_convert_fusion.1
  357.7 11.2 multiply_reduce_fusion
  370.2 2.7 fusion.131
  374.8 2.6 copy.204
  383.0 99.0 %while.39 = (s32[]{:T(128)}, f32[1,256,8,2,64]{1,4,3,2,0:T(8,128)}, bf16[2,1,256,512]{2,3,1,0:T(8,128)(2,1)}, f32[2,1,256,512]{2,3,1,0:T(8,128)}, s32[]{:T(128)}...) while((s32[]{:T(128)}, f32[1,256,8,2,64]{1,4,3,2,0:T(8,128)}, ...), condition=%wide.region_18.19_spmd.clone, body=%wide.region_15.18_spmd.clone.sunk | while | flops 684655104 | bytes 39838160 | solution.py:346
  384.0 6.7 conditional.11
  391.9 4.0 collective-permute-start.1
  397.1 8.3 collective-permute-done.2
  409.8 10.5 collective-permute-start.2
  420.4 5.3 collective-permute-start.1
  432.5 10.8 collective-permute-start.2
  443.3 11.8 collective-permute-start.1
  461.9 11.5 collective-permute-start.2
  473.3 5.3 collective-permute-start.1
  482.0 2.5 copy.205
  485.9 2.6 add_convert_fusion
  488.5 30.8 %collective-permute-start.3 = (bf16[2,1,256,512]{3,2,1,0:T(8,128)(2,1)}, bf16[2,1,256,512]{3,2,1,0:T(8,128)(2,1)}, u32[]{:S(2)}, u32[]{:S(2)}) collective-permute-start(bf16[2,1,256,512]{3,2,1,0:T(8,128)(2,1)} %add_convert_fusion), channel_id=1, source_target_pairs={{0,4},{1,5},{2,6},{3,7},{4,0},{5,1},{6,2},{7,3},{8,12},{9,13},{10,... | collective-permute-start | bytes 1572872 | tf_op jit(solution)/shard_map/ppermute | solution.py:36
  521.9 2.5 copy.203
  524.5 2.5 copy.201
  527.0 3.2 multiply_convert_fusion.3
  530.2 5.5 collective-permute-done.3
  546.2 5.7 fusion.127
  553.6 9.1 convolution_bitcast_fusion
  562.7 18.7 %copy.250 = f32[1024,4608]{1,0:T(8,128)} copy(f32[1024,4608]{0,1:T(8,128)} %convolution_bitcast_fusion) | data formatting | bytes 37748736
  582.7 17.5 %fusion.103 = f32[1024,9216]{1,0:T(8,128)} fusion(bf16[256,4608]{1,0:T(8,128)(2,1)} %get-tuple-element.942, bf16[256,4608]{1,0:T(8,128)(2,1)} %get-tuple-element.941, f32[256,1024]{1,0:T(8,128)S(1)} %copy-done.2, f32[1024]{0:T(1024)S(1)} %get-tuple-element.958, f32[256]{0:T(256)S(1)} %add_rsqrt_fusion.2), kind=kOutput, calls=%fused_computation.119 | convolution fusion | flops 4842061824 | bytes 43521024 | tf_op jit(solution)/shard_map/dot_general | solution.py:134
  605.6 3.5 copy.212
  611.6 3.6 fusion.105
  615.3 7.2 fusion.111
  625.3 4.8 fusion.119
  630.2 40.2 %all-reduce.1 = f32[2176]{0:T(1024)S(1)} all-reduce(f32[2176]{0:T(1024)S(1)} %concatenate.70), channel_id=6, replica_groups=mesh['dp'=4,'ctx'=8] {'dp','ctx'}, use_global_device_ids=true, to_apply=%region_32.33.clone | all-reduce | flops 2176 | bytes 17408
  675.6 29.8 %reduce-scatter.7.cloned.1.call-done = f32[32,2048]{1,0:T(8,128)} async-done(((f32[1024,2048]{1,0:T(8,128)}), f32[32,2048]{1,0:T(8,128)}) %reduce-scatter.7.cloned.1.call-update) | async-done | bytes 262160 | tf_op jit(solution)/shard_map/reduce_scatter | solution.py:365
  707.6 209.1 %reduce-scatter.13.cloned.1.call-done = f32[32,4608]{1,0:T(8,128)} async-done(((f32[1024,4608]{1,0:T(8,128)}), f32[32,4608]{1,0:T(8,128)}) %reduce-scatter.13.cloned.1.call-update) | async-done | bytes 589840
  916.7 2.9 multiply_subtract_fusion.1
  919.6 351.9 %reduce-scatter.11.cloned.1.call-done = f32[32,9216]{1,0:T(8,128)} async-done(((f32[1024,9216]{1,0:T(8,128)}), f32[32,9216]{1,0:T(8,128)}) %reduce-scatter.11.cloned.1.call-update) | async-done | bytes 1179664 | tf_op jit(solution)/shard_map/reduce_scatter | solution.py:367
  1271.5 4.0 multiply_subtract_fusion
  (283 shorter events, 107.5 us)
Async XLA Ops:
  7.2 7.6 copy-start.49
  7.2 50.2 %copy-start.10 = (bf16[1,256,1024]{2,1,0:T(8,128)(2,1)S(1)}, bf16[1,256,1024]{2,1,0:T(8,128)(2,1)}, u32[]{:S(2)}) copy-start(bf16[1,256,1024]{2,1,0:T(8,128)(2,1)} %param.30) | copy-start | bytes 1572868
  7.2 50.4 %copy-start.48 = (s32[1,256]{1,0:T(1,128)S(1)}, s32[1,256]{1,0:T(1,128)}, u32[]{:S(2)}) copy-start(s32[1,256]{1,0:T(1,128)} %param.31) | copy-start | bytes 3076
  7.2 69.3 %all-gather.5.cloned.1.call-start = ((), (), s32[]{:S(2)}) async-start(), calls=%async_computation.4 | async-start | bytes 4325376 | tf_op jit(solution)/shard_map/all_gather | solution.py:241
  9.0 126.4 %all-gather.7.cloned.1.call-start = ((), (), s32[]{:S(2)}) async-start(), calls=%async_computation.5 | async-start | bytes 2162688 | tf_op jit(solution)/shard_map/all_gather | solution.py:242
  10.6 252.1 %all-gather.9.cloned.1.call-start = ((), (), s32[]{:S(2)}) async-start(), calls=%async_computation.6 | async-start | bytes 19464192 | tf_op jit(solution)/shard_map/all_gather | solution.py:243
  12.8 333.7 %all-gather.11.cloned.1.call-start = ((), (), s32[]{:S(2)}) async-start(), calls=%async_computation.7 | async-start | bytes 9732096 | tf_op jit(solution)/shard_map/all_gather | solution.py:244
  14.7 658.9 %reduce-scatter.9.cloned.1.call-start = ((), (), s32[]{:S(2)}) async-start(), calls=%async_computation.9 | async-start | bytes 4325376 | tf_op jit(solution)/shard_map/reduce_scatter | solution.py:366
  57.4 74.0 %copy-start.45 = (s32[256]{0:T(256)}, s32[256]{0:T(256)S(1)}, u32[]{:S(2)}) copy-start(s32[256]{0:T(256)S(1)} %iota_add_fusion) | copy-start | bytes 3076
  57.6 23.9 %copy-start.38 = (f32[256]{0:T(256)}, f32[256]{0:T(256)S(1)}, u32[]{:S(2)}) copy-start(f32[256]{0:T(256)S(1)} %add_rsqrt_fusion.3) | copy-start | bytes 3076
  57.7 24.2 %copy-start.41 = (f32[64]{0:T(128)}, f32[64]{0:T(128)S(1)}, u32[]{:S(2)}) copy-start(f32[64]{0:T(128)S(1)} %get-tuple-element.961) | copy-start | bytes 772
  57.7 28.2 %copy-start.43 = (f32[64]{0:T(128)}, f32[64]{0:T(128)S(1)}, u32[]{:S(2)}) copy-start(f32[64]{0:T(128)S(1)} %get-tuple-element.960) | copy-start | bytes 772
  57.7 23.8 %copy-start.35 = (f32[1024]{0:T(1024)}, f32[1024]{0:T(1024)S(1)}, u32[]{:S(2)}) copy-start(f32[1024]{0:T(1024)S(1)} %get-tuple-element.959) | copy-start | bytes 12292
  81.9 458.9 %copy-start.34 = (f32[256,8]{0,1:T(8,128)}, f32[256,8]{0,1:T(8,128)S(1)}, u32[]{:S(2)}) copy-start(f32[256,8]{0,1:T(8,128)S(1)} %add_rsqrt_fusion.1) | copy-start | bytes 24580
  87.8 6.3 collective-permute-start
  94.9 8.0 collective-permute-start
  103.6 12.6 collective-permute-start
  117.1 14.3 %collective-permute-start = (bf16[2,1,256,512]{2,3,1,0:T(8,128)(2,1)}, bf16[2,1,256,512]{2,3,1,0:T(8,128)(2,1)S(1)}, u32[]{:S(2)}, u32[]{:S(2)}) collective-permute-start(bf16[2,1,256,512]{2,3,1,0:T(8,128)(2,1)} %copy.275), channel_id=1, source_target_pairs={{0,1},{1,2},{2,3},{3,4},{4,5},{5,6},{6,7},{8,9},{9,10},{10,11},{11... | collective-permute-start | bytes 1572872 | tf_op jit(solution)/shard_map/while/body/eval_jaxpr/ppermute | solution.py:30
  138.0 231.0 %copy-start.1 = (f32[256,1024]{1,0:T(8,128)}, f32[256,1024]{1,0:T(8,128)S(1)}, u32[]{:S(2)}) copy-start(f32[256,1024]{1,0:T(8,128)S(1)} %get-tuple-element.967) | copy-start | bytes 3145732
  262.7 83.8 %copy-start.30 = (bf16[1,256,1024]{2,1,0:T(8,128)(2,1)S(1)}, bf16[1,256,1024]{2,1,0:T(8,128)(2,1)}, u32[]{:S(2)}) copy-start(bf16[1,256,1024]{2,1,0:T(8,128)(2,1)} %param.32) | copy-start | bytes 1572868
  357.7 12.5 copy-start.24
  373.0 332.5 %reduce-scatter.7.cloned.1.call-start = ((), (), s32[]{:S(2)}) async-start(), calls=%async_computation.8 | async-start | bytes 8650752 | tf_op jit(solution)/shard_map/reduce_scatter | solution.py:365
  383.0 101.6 %copy-start.46 = (s32[256]{0:T(256)S(1)}, s32[256]{0:T(256)}, u32[]{:S(2)}) copy-start(s32[256]{0:T(256)} %copy-done.45) | copy-start | bytes 3076
  391.7 13.7 %collective-permute-start.2 = (bf16[2,1,256,512]{2,3,1,0:T(8,128)(2,1)}, bf16[2,1,256,512]{2,3,1,0:T(8,128)(2,1)S(1)}, u32[]{:S(2)}, u32[]{:S(2)}) collective-permute-start(bf16[2,1,256,512]{2,3,1,0:T(8,128)(2,1)} %fusion.178), channel_id=1, source_target_pairs={{0,1},{1,2},{2,3},{3,4},{4,5},{5,6},{6,7},{7,0},{8,9},{9,10},{10,1... | collective-permute-start | bytes 1572872 | tf_op jit(solution)/shard_map/while/body/eval_jaxpr/ppermute | solution.py:36
  391.9 14.5 %collective-permute-start.1 = (bf16[2,1,256,512]{2,3,1,0:T(8,128)(2,1)S(1)}, bf16[2,1,256,512]{2,3,1,0:T(8,128)(2,1)}, u32[]{:S(2)}, u32[]{:S(2)}) collective-permute-start(bf16[2,1,256,512]{2,3,1,0:T(8,128)(2,1)S(1)} %copy.293), channel_id=1, source_target_pairs={{0,1},{1,2},{2,3},{3,4},{4,5},{5,6},{6,7},{8,9},{9,10},{10,11},{11... | collective-permute-start | bytes 1572872 | tf_op jit(solution)/shard_map/while/body/eval_jaxpr/ppermute | solution.py:30
  409.8 18.2 %collective-permute-start.2 = (bf16[2,1,256,512]{2,3,1,0:T(8,128)(2,1)}, bf16[2,1,256,512]{2,3,1,0:T(8,128)(2,1)S(1)}, u32[]{:S(2)}, u32[]{:S(2)}) collective-permute-start(bf16[2,1,256,512]{2,3,1,0:T(8,128)(2,1)} %fusion.178), channel_id=1, source_target_pairs={{0,1},{1,2},{2,3},{3,4},{4,5},{5,6},{6,7},{7,0},{8,9},{9,10},{10,1... | collective-permute-start | bytes 1572872 | tf_op jit(solution)/shard_map/while/body/eval_jaxpr/ppermute | solution.py:36
  420.4 8.7 collective-permute-start.1
  432.5 24.9 %collective-permute-start.2 = (bf16[2,1,256,512]{2,3,1,0:T(8,128)(2,1)}, bf16[2,1,256,512]{2,3,1,0:T(8,128)(2,1)S(1)}, u32[]{:S(2)}, u32[]{:S(2)}) collective-permute-start(bf16[2,1,256,512]{2,3,1,0:T(8,128)(2,1)} %fusion.178), channel_id=1, source_target_pairs={{0,1},{1,2},{2,3},{3,4},{4,5},{5,6},{6,7},{7,0},{8,9},{9,10},{10,1... | collective-permute-start | bytes 1572872 | tf_op jit(solution)/shard_map/while/body/eval_jaxpr/ppermute | solution.py:36
  443.3 15.2 %collective-permute-start.1 = (bf16[2,1,256,512]{2,3,1,0:T(8,128)(2,1)S(1)}, bf16[2,1,256,512]{2,3,1,0:T(8,128)(2,1)}, u32[]{:S(2)}, u32[]{:S(2)}) collective-permute-start(bf16[2,1,256,512]{2,3,1,0:T(8,128)(2,1)S(1)} %copy.293), channel_id=1, source_target_pairs={{0,1},{1,2},{2,3},{3,4},{4,5},{5,6},{6,7},{8,9},{9,10},{10,11},{11... | collective-permute-start | bytes 1572872 | tf_op jit(solution)/shard_map/while/body/eval_jaxpr/ppermute | solution.py:30
  461.9 19.1 %collective-permute-start.2 = (bf16[2,1,256,512]{2,3,1,0:T(8,128)(2,1)}, bf16[2,1,256,512]{2,3,1,0:T(8,128)(2,1)S(1)}, u32[]{:S(2)}, u32[]{:S(2)}) collective-permute-start(bf16[2,1,256,512]{2,3,1,0:T(8,128)(2,1)} %fusion.178), channel_id=1, source_target_pairs={{0,1},{1,2},{2,3},{3,4},{4,5},{5,6},{6,7},{7,0},{8,9},{9,10},{10,1... | collective-permute-start | bytes 1572872 | tf_op jit(solution)/shard_map/while/body/eval_jaxpr/ppermute | solution.py:36
  473.3 8.7 collective-permute-start.1
  484.5 34.8 %copy-start = (f32[1,256,8,2,64]{1,4,3,2,0:T(8,128)S(1)}, f32[1,256,8,2,64]{1,4,3,2,0:T(8,128)}, u32[]{:S(2)}) copy-start(f32[1,256,8,2,64]{1,4,3,2,0:T(8,128)} %get-tuple-element.538) | copy-start | bytes 3145732
  485.9 33.7 %copy-start.4 = (f32[256,1024]{0,1:T(8,128)S(1)}, f32[256,1024]{0,1:T(8,128)}, u32[]{:S(2)}) copy-start(f32[256,1024]{0,1:T(8,128)} %copy-done.3) | copy-start | bytes 3145732
  488.5 47.1 %collective-permute-start.3 = (bf16[2,1,256,512]{3,2,1,0:T(8,128)(2,1)}, bf16[2,1,256,512]{3,2,1,0:T(8,128)(2,1)}, u32[]{:S(2)}, u32[]{:S(2)}) collective-permute-start(bf16[2,1,256,512]{3,2,1,0:T(8,128)(2,1)} %add_convert_fusion), channel_id=1, source_target_pairs={{0,4},{1,5},{2,6},{3,7},{4,0},{5,1},{6,2},{7,3},{8,12},{9,13},{10,... | collective-permute-start | bytes 1572872 | tf_op jit(solution)/shard_map/ppermute | solution.py:36
  519.6 7.4 copy-start.21
  527.0 13.8 %copy-start.15 = (f32[256,512]{0,1:T(8,128)S(1)}, f32[256,512]{0,1:T(8,128)}, u32[]{:S(2)}) copy-start(f32[256,512]{0,1:T(8,128)} %copy-done.14) | copy-start | bytes 1572868
  537.6 8.6 copy-start.12
  537.6 8.6 copy-start.36
  537.6 8.6 copy-start.39
  551.9 364.8 %reduce-scatter.13.cloned.1.call-start = ((), (), s32[]{:S(2)}) async-start(), calls=%async_computation.11 | async-start | bytes 19464192
  581.5 690.0 %reduce-scatter.11.cloned.1.call-start = ((), (), s32[]{:S(2)}) async-start(), calls=%async_computation.10 | async-start | bytes 38928384 | tf_op jit(solution)/shard_map/reduce_scatter | solution.py:367
  625.3 45.2 %copy-start.50 = (f32[68]{0:T(128)S(1)}, f32[68]{0:T(128)}, u32[]{:S(2)}) copy-start(f32[68]{0:T(128)} %param.37) | copy-start | bytes 820
  625.3 45.2 %copy-start.51 = (f32[68]{0:T(128)S(1)}, f32[68]{0:T(128)}, u32[]{:S(2)}) copy-start(f32[68]{0:T(128)} %param.42) | copy-start | bytes 820
  625.3 45.1 %copy-start.52 = (f32[68]{0:T(128)S(1)}, f32[68]{0:T(128)}, u32[]{:S(2)}) copy-start(f32[68]{0:T(128)} %param.47) | copy-start | bytes 820
  625.3 45.8 %copy-start.7 = (f32[256,1024]{1,0:T(8,128)S(1)}, f32[256,1024]{1,0:T(8,128)}, u32[]{:S(2)}) copy-start(f32[256,1024]{1,0:T(8,128)} %copy-done.5) | copy-start | bytes 3145732
  630.2 286.6 %copy-start.27 = (f32[32,4608]{1,0:T(8,128)S(1)}, f32[32,4608]{1,0:T(8,128)}, u32[]{:S(2)}) copy-start(f32[32,4608]{1,0:T(8,128)} %param.36) | copy-start | bytes 1769476
  673.6 597.9 %copy-start.20 = (f32[32,9216]{1,0:T(8,128)S(1)}, f32[32,9216]{1,0:T(8,128)}, u32[]{:S(2)}) copy-start(f32[32,9216]{1,0:T(8,128)} %param.35) | copy-start | bytes 3538948
  673.6 597.9 %copy-start.32 = (f32[32,9216]{1,0:T(8,128)S(1)}, f32[32,9216]{1,0:T(8,128)}, u32[]{:S(2)}) copy-start(f32[32,9216]{1,0:T(8,128)} %param.40) | copy-start | bytes 3538948
  (25 other events, 78.9 us)
Sparse Core Ops, SparseCore 0:
  11.6 64.8 all-gather.4
  80.1 55.1 all-gather.6
  139.0 123.7 all-gather.8
  266.2 80.2 all-gather.10
  373.1 144.3 reduce-scatter.8
  552.1 153.3 reduce-scatter.6
  712.4 204.2 reduce-scatter.12
  923.7 347.7 reduce-scatter.10
where the time goes:
time: 1290 us; the launch traced here: 1280 us
  waiting for transfers between devices  826 us (64%)
  starting transfers between devices  123 us (10%)
  matrix products  100 us (8%)
  blocking collectives  82.5 us (6%)
  local copies, waits for them, and re-layouts  70.5 us (5%)
  other arithmetic  64.3 us (5%)
  between operations  15.2 us (1%)
    reduce_scatter x1, waiting for transfers between devices, per_device(): lax.psum_scatter(grad_gate_up, ('dp', 'ctx'), scatter_dimension=0, tiled=...  352 us
    unnamed x9, waiting for transfers between devices  209 us
    all_gather x1, waiting for transfers between devices, per_device(): lax.all_gather(w_gate_up.astype(jnp.bfloat16), ('dp', 'ctx'), axis=0, til...  125 us
    unnamed x2, blocking collectives  82.5 us
    all_gather x1, waiting for transfers between devices, per_device(): lax.all_gather(w_down.astype(jnp.bfloat16), ('dp', 'ctx'), axis=0, tiled=...  69.8 us
    ppermute x5, starting transfers between devices, shifted(): return lax.ppermute(value, axis, pairs)  63.9 us
    ppermute x8, starting transfers between devices, from_behind(): return lax.ppermute(block, axis, route)  58.4 us
    reduce_scatter x1, waiting for transfers between devices, per_device(): lax.psum_scatter(grad_qkv, ('dp', 'ctx'), scatter_dimension=0, tiled=True)  29.8 us
  transfers between devices with their start and end apart: 21, of which 12 were waited for; matrix products, arithmetic and copies ran while one was open for 15% of the time, Pallas kernels for 0%

commit v1 on v0

v1 whole, which is shorter than its diff:
```python
import functools
import math

import jax
import jax.numpy as jnp
from jax import lax
from jax.experimental import pallas as pl
from jax.experimental.pallas import tpu as pltpu
from jax.sharding import PartitionSpec as P

D = 1024
HEADS = 16
KV_HEADS = 8
HEAD_DIM = 64
STEP = 4
HQ = 1024
HK = 512


EPS = 1e-05
THETA = 1000000.0
NEG_BIG = -1e30
BETA_ONE = 0.9
BETA_TWO = 0.95
ADAM_EPS = 1e-08
CONTRACT_LAST = (((1,), (1,)), ((), ()))
CONTRACT_ROWS = (((0,), (0,)), ((), ()))


def norm_forward(values, gain):
    recip = lax.rsqrt(jnp.mean(values * values, axis=-1, keepdims=True) + EPS)
    unit = values * recip
    return (unit * gain, unit, recip)


def norm_backward(grad, gain, unit, recip):
    scaled = grad * gain
    inner = jnp.mean(scaled * unit, axis=-1, keepdims=True)
    grad_in = recip * (scaled - unit * inner)
    grad_gain = jnp.sum((grad * unit).reshape(-1, unit.shape[-1]), axis=0)
    return (grad_in, grad_gain)


def rope_tables(places):
    half = HEAD_DIM // 2
    freqs = jnp.exp(-math.log(THETA) * (2.0 * jnp.arange(half, dtype=jnp.float32) / HEAD_DIM))
    angles = places.astype(jnp.float32)[:, None] * freqs[None, :]
    return (jnp.cos(angles)[:, None, :], jnp.sin(angles)[:, None, :])


def rotate(values, cosine, sine):
    half = HEAD_DIM // 2
    first_half = values[..., :half]
    second_half = values[..., half:]
    return jnp.concatenate(
        [first_half * cosine - second_half * sine, second_half * cosine + first_half * sine],
        axis=-1,
    )


def unrotate(grad, cosine, sine):
    half = HEAD_DIM // 2
    first_half = grad[..., :half]
    second_half = grad[..., half:]
    return jnp.concatenate(
        [first_half * cosine + second_half * sine, second_half * cosine - first_half * sine],
        axis=-1,
    )


def split_gains(gains_used):
    return (
        gains_used[:D],
        gains_used[D : 2 * D],
        gains_used[2 * D : 2 * D + HEAD_DIM],
        gains_used[2 * D + HEAD_DIM :],
    )


def front_pass(tokens_f, places, weight_qkv, gains_used):
    gain_attn, gain_ffn, gain_query, gain_key = split_gains(gains_used)
    normed, unit_in, recip_in = norm_forward(tokens_f, gain_attn)
    attn_in = normed.astype(jnp.bfloat16)
    projected = jnp.dot(attn_in, weight_qkv, preferred_element_type=jnp.float32)
    count = tokens_f.shape[0]
    query = projected[:, :HQ].reshape(count, HEADS, HEAD_DIM)
    key_raw = projected[:, HQ : HQ + HK].reshape(count, KV_HEADS, HEAD_DIM)
    value_b = projected[:, HQ + HK :].astype(jnp.bfloat16).reshape(count, KV_HEADS, HEAD_DIM)
    cosine, sine = rope_tables(places)
    query_n, unit_q, recip_q = norm_forward(query, gain_query)
    key_n, unit_k, recip_k = norm_forward(key_raw, gain_key)
    query_b = rotate(query_n, cosine, sine).astype(jnp.bfloat16)
    key_b = rotate(key_n, cosine, sine).astype(jnp.bfloat16)
    saved = (attn_in, unit_in, recip_in, unit_q, recip_q, unit_k, recip_k, cosine, sine)
    return (query_b, key_b, value_b, saved)


def tail_pass(grad_query, grad_key, grad_value, saved, gains_used, weight_qkv, grad_mixed):
    gain_attn, gain_ffn, gain_query, gain_key = split_gains(gains_used)
    attn_in, unit_in, recip_in, unit_q, recip_q, unit_k, recip_k, cosine, sine = saved
    count = attn_in.shape[0]
    grad_q, grad_gain_q = norm_backward(
        unrotate(grad_query, cosine, sine), gain_query, unit_q, recip_q
    )
    grad_k, grad_gain_k = norm_backward(unrotate(grad_key, cosine, sine), gain_key, unit_k, recip_k)
    grad_proj = jnp.concatenate(
        [grad_q.reshape(count, HQ), grad_k.reshape(count, HK), grad_value.reshape(count, HK)],
        axis=1,
    ).astype(jnp.bfloat16)
    grad_qkv = lax.dot_general(
        attn_in, grad_proj, CONTRACT_ROWS, preferred_element_type=jnp.float32
    )
    grad_normed = lax.dot_general(
        grad_proj, weight_qkv, CONTRACT_LAST, preferred_element_type=jnp.float32
    )
    grad_in, grad_gain_attn = norm_backward(grad_normed, gain_attn, unit_in, recip_in)
    return (grad_mixed + grad_in, grad_qkv, grad_gain_attn, grad_gain_q, grad_gain_k)


def adam_step(weight, grad, first, second, rate, decay):
    first_new = BETA_ONE * first + (1.0 - BETA_ONE) * grad
    second_new = BETA_TWO * second + (1.0 - BETA_TWO) * grad * grad
    first_hat = first_new / (1.0 - BETA_ONE**STEP)
    second_hat = second_new / (1.0 - BETA_TWO**STEP)
    weight_new = weight - rate * (first_hat / (jnp.sqrt(second_hat) + ADAM_EPS) + decay * weight)
    return (weight_new, first_new, second_new)


BF = jnp.bfloat16
F32 = jnp.float32
MESH_ID = pl.DeviceIdType.MESH
ANY = pl.BlockSpec(memory_space=pl.ANY)
VMEM = pl.BlockSpec(memory_space=pltpu.VMEM)
DMA = pltpu.SemaphoreType.DMA
NN = (((1,), (0,)), ((), ()))
NT = (((1,), (1,)), ((), ()))
TN = (((0,), (0,)), ((), ()))
VMEM_BYTES = 60 << 20


def dot(a, b, dims):
    return lax.dot_general(a, b, dims, preferred_element_type=F32)


class Place:
    def __init__(self, planes, depth):
        self.planes, self.depth = planes, depth
        self.dp = lax.axis_index("dp")
        self.ctx = lax.axis_index("ctx")
        self.z = self.ctx // 2
        self.core = self.ctx % 2

    def sibling(self):
        return {"dp": self.dp, "ctx": self.z * 2 + 1 - self.core}

    def across(self, o):
        return {"dp": self.dp ^ o, "ctx": self.ctx}

    def behind(self, k):
        return lax.rem(self.z + self.depth - k, self.depth)

    def ahead(self, k):
        return lax.rem(self.z + k, self.depth)

    def along(self, z):
        return {"dp": self.dp, "ctx": z * 2 + self.core}


def greet(devices):
    barrier = pltpu.get_barrier_semaphore()
    for device in devices:
        pl.semaphore_signal(barrier, inc=1, device_id=device, device_id_type=MESH_ID)
    pl.semaphore_wait(barrier, len(devices))


def remote(src, dst, send, recv, device):
    return pltpu.make_async_remote_copy(
        src_ref=src, dst_ref=dst, send_sem=send, recv_sem=recv, device_id=device, device_id_type=MESH_ID
    )


def params(collective_id=None):
    if collective_id is None:
        return pltpu.CompilerParams(vmem_limit_bytes=VMEM_BYTES)
    return pltpu.CompilerParams(
        vmem_limit_bytes=VMEM_BYTES, collective_id=collective_id, has_side_effects=True
    )


def plane_exchange_kernel(planes, depth, w_ref, a_ref, send, recv, local):
    me = Place(planes, depth)
    own = pltpu.make_async_copy(w_ref.at[me.dp], a_ref.at[me.dp], local)
    own.start()
    greet([me.across(o) for o in range(1, planes)])
    copies = []
    for o in range(1, planes):
        copy = remote(
            w_ref.at[me.dp ^ o], a_ref.at[me.dp], send.at[o], recv.at[o], me.across(o)
        )
        copy.start()
        copies.append(copy)
    own.wait()
    for o in range(1, planes):
        copies[o - 1].wait_send()
        remote(
            w_ref.at[me.dp], a_ref.at[me.dp ^ o], send.at[o], recv.at[o], me.across(o)
        ).wait_recv()


def plane_exchange(blocks, planes, depth, collective_id):
    return pl.pallas_call(
        functools.partial(plane_exchange_kernel, planes, depth),
        out_shape=jax.ShapeDtypeStruct(blocks.shape, blocks.dtype),
        in_specs=[ANY],
        out_specs=ANY,
        scratch_shapes=[DMA((planes,)), DMA((planes,)), DMA(())],
        compiler_params=params(collective_id),
    )(blocks)


class Gather:
    def __init__(self, me, x_ref, g_ref, sems):
        self.me, self.x, self.g, self.sems = me, x_ref, g_ref, sems
        self.sent = []

    def push(self, src, dst, kind, o, k, device):
        copy = remote(src, dst, self.sems.at[2 * kind, o, k], self.sems.at[2 * kind + 1, o, k], device)
        copy.start()
        self.sent.append(copy)

    def expect(self, dst, kind, o, k):
        remote(dst, dst, self.sems.at[2 * kind, o, k], self.sems.at[2 * kind + 1, o, k], self.me.sibling()).wait_recv()

    def start(self):
        me = self.me
        here = self.g.at[me.dp, me.z, me.core]
        self.own = pltpu.make_async_copy(self.x, here, self.sems.at[6, 0, 0])
        self.own.start()

    def first(self):
        me = self.me
        here = self.g.at[me.dp, me.z, me.core]
        for k in range(1, me.depth):
            self.push(self.x, here, 0, 0, k, me.along(me.ahead(k)))
        for o in range(1, me.planes):
            self.push(self.x, here, 1, o, 0, me.across(o))
        self.push(self.x, here, 2, 0, 0, me.sibling())

    def second(self):
        me = self.me
        for k in range(1, me.depth):
            block = self.g.at[me.dp, me.behind(k), me.core]
            self.expect(block, 0, 0, k)
            for o in range(1, me.planes):
                self.push(block, block, 1, o, k, me.across(o))
            self.push(block, block, 2, 0, k, me.sibling())
        for k in range(me.depth):
            for o in range(1, me.planes):
                block = self.g.at[me.dp ^ o, me.behind(k), me.core]
                self.expect(block, 1, o, k)
                self.push(block, block, 2, o, k, me.sibling())

    def finish(self):
        me = self.me
        for o in range(me.planes):
            for k in range(me.depth):
                block = self.g.at[me.dp ^ o, me.behind(k), 1 - me.core]
                self.expect(block, 2, o, k)
        for copy in self.sent:
            copy.wait_send()
        self.own.wait()


def gather_kernel(planes, depth, x_ref, g_ref, sems):
    me = Place(planes, depth)
    work = Gather(me, x_ref, g_ref, sems)
    work.start()
    greet(
        [me.across(o) for o in range(1, planes)]
        + [me.along(me.ahead(k)) for k in range(1, depth)]
        + [me.sibling()]
    )
    work.first()
    work.second()
    work.finish()


def gather_all(block, planes, depth, collective_id):
    return pl.pallas_call(
        functools.partial(gather_kernel, planes, depth),
        out_shape=jax.ShapeDtypeStruct((planes, depth, 2) + block.shape, block.dtype),
        in_specs=[ANY],
        out_specs=ANY,
        scratch_shapes=[DMA((7, planes, depth))],
        compiler_params=params(collective_id),
    )(block)


def halo_kernel(planes, depth, turns, kv_ref, og_ref, wo_ref, kv_all, og_all, wo_all, local, zs, cs, ps, wsem):
    me = Place(planes, depth)
    half = turns // 2
    weights = Gather(me, wo_ref, wo_all, wsem)
    weights.start()
    own_kv = pltpu.make_async_copy(kv_ref, kv_all.at[0], local.at[0])
    own_kv.start()
    own_og = pltpu.make_async_copy(og_ref, og_all.at[0], local.at[1])
    own_og.start()
    greet(
        [me.across(o) for o in range(1, planes)]
        + [me.along(me.ahead(k)) for k in range(1, depth)]
        + [me.sibling()]
    )

    def z_copy(k):
        return remote(kv_ref, kv_all.at[2 * k], zs.at[0, k], zs.at[1, k], me.along(me.ahead(k)))

    def c_copy(i):
        return remote(
            kv_all.at[2 * i + 2 * me.core], kv_all.at[2 * i + 1], cs.at[0, i], cs.at[1, i], me.sibling()
        )

    for k in range(1, half + 1):
        @pl.when(me.z + k < depth)
        def _():
            z_copy(k).start()

    weights.first()
    shares = []
    for o in range(1, planes):
        share = remote(og_ref, og_all.at[o], ps.at[0, o], ps.at[1, o], me.across(o))
        share.start()
        shares.append(share)
    own_kv.wait()

    @pl.when(me.core == 0)
    def _():
        c_copy(0).start()

    for k in range(1, half + 1):
        there = me.z - k >= 0

        @pl.when(there)
        def _():
            z_copy(k).wait_recv()

        @pl.when(there & (me.core == 1))
        def _():
            c_copy(k - 1).start()

        if k < half:
            @pl.when(there & (me.core == 0))
            def _():
                c_copy(k).start()

        @pl.when(me.z - k < 0)
        def _():
            fill = pltpu.make_async_copy(kv_ref, kv_all.at[2 * k], local.at[2])
            fill.start()
            fill.wait()

    for i in range(half):
        @pl.when(me.z - i - 1 + me.core >= 0)
        def _():
            c_copy(i).wait_recv()

        @pl.when(me.z - i - 1 + me.core < 0)
        def _():
            fill = pltpu.make_async_copy(kv_ref, kv_all.at[2 * i + 1], local.at[2])
            fill.start()
            fill.wait()

        @pl.when(me.z - i - me.core >= 0)
        def _():
            c_copy(i).wait_send()

    for k in range(1, half + 1):
        @pl.when(me.z + k < depth)
        def _():
            z_copy(k).wait_send()

    weights.second()
    for share in shares:
        share.wait()
    weights.finish()
    own_og.wait()


def halo(kv, cotangent, w_output_b, planes, depth, turns, collective_id):
    half = turns // 2
    return pl.pallas_call(
        functools.partial(halo_kernel, planes, depth, turns),
        out_shape=(
            jax.ShapeDtypeStruct((turns + 1,) + kv.shape, kv.dtype),
            jax.ShapeDtypeStruct((planes,) + cotangent.shape, cotangent.dtype),
            jax.ShapeDtypeStruct((planes, depth, 2) + w_output_b.shape, w_output_b.dtype),
        ),
        in_specs=[ANY, ANY, ANY],
        out_specs=(ANY, ANY, ANY),
        scratch_shapes=[
            DMA((3,)),
            DMA((2, half + 1)),
            DMA((2, half)),
            DMA((2, planes)),
            DMA((7, planes, depth)),
        ],
        compiler_params=params(collective_id),
    )(kv, cotangent, w_output_b)


def fill_bias(bias, lower_ref, slots, count):
    query = lax.broadcasted_iota(jnp.int32, (count, count), 1)
    lower = lower_ref[...]
    for s in range(slots):
        key = lax.broadcasted_iota(jnp.int32, (count, count), 0) - s * count
        allowed = (key <= query) & (key >= lower)
        bias[pl.ds(s * count, count), :] = jnp.where(allowed, 0.0, NEG_BIG)


def attend_kernel(slots, count, q_ref, kv_ref, lower_ref, o_ref, lse_ref, bias):
    fill_bias(bias, lower_ref, slots, count)

    def four_heads(t, carry):
        keys = kv_ref[:, pl.ds(t * 128, 128)]
        values = kv_ref[:, pl.ds(HK + t * 128, 128)]
        queries = q_ref[:, pl.ds(t * 256, 256)]
        sums = []
        for u in range(2):
            key = keys[:, u * 64 : u * 64 + 64]
            value = values[:, u * 64 : u * 64 + 64]
            for g in range(2):
                at = u * 128 + g * 64
                query = queries[:, at : at + 64]
                scores = dot(key, query, NT) * (HEAD_DIM ** (-0.5)) + bias[...]
                weights = jnp.exp(scores)
                total = jnp.sum(weights, axis=0, keepdims=True)
                out = dot(value, weights.astype(BF), TN) / total
                o_ref[pl.ds(t * 256 + at, 64), :] = out.astype(BF)
                sums.append(jnp.log(total))
        lse_ref[t] = jnp.concatenate(sums, axis=0)
        return carry

    lax.fori_loop(0, HEADS // 4, four_heads, 0)


def attend(query, kv, lower):
    count = query.shape[0]
    slots = kv.shape[0]
    flops = 4 * HEADS * slots * count * count * HEAD_DIM
    return pl.pallas_call(
        functools.partial(attend_kernel, slots, count),
        out_shape=(
            jax.ShapeDtypeStruct((HQ, count), BF),
            jax.ShapeDtypeStruct((HEADS // 4, 4, count), F32),
        ),
        in_specs=[VMEM, VMEM, VMEM],
        out_specs=(VMEM, VMEM),
        scratch_shapes=[pltpu.VMEM((slots * count, count), F32)],
        compiler_params=params(),
        cost_estimate=pl.CostEstimate(flops=flops * 4, bytes_accessed=4 << 20, transcendentals=0),
    )(query, kv.reshape(slots * count, 2 * HK), lower)


def attend_back_kernel(slots, count, q_ref, kv_ref, lower_ref, gob_ref, lse_ref, delta_ref, gq_ref, gkv_ref, bias):
    scale = HEAD_DIM ** (-0.5)
    fill_bias(bias, lower_ref, slots, count)

    def four_heads(t, carry):
        keys = kv_ref[:, pl.ds(t * 128, 128)]
        values = kv_ref[:, pl.ds(HK + t * 128, 128)]
        queries = q_ref[:, pl.ds(t * 256, 256)]
        lse = lse_ref[t]
        delta = delta_ref[t]
        grad_keys, grad_values = [], []
        for u in range(2):
            key = keys[:, u * 64 : u * 64 + 64]
            value = values[:, u * 64 : u * 64 + 64]
            grad_key, grad_value = 0.0, 0.0
            for g in range(2):
                at, h = u * 128 + g * 64, 2 * u + g
                query = queries[:, at : at + 64]
                gob = gob_ref[pl.ds(t * 256 + at, 64), :]
                probs = jnp.exp(dot(key, query, NT) * scale + bias[...] - lse[h : h + 1, :])
                grad_value = grad_value + dot(probs.astype(BF), gob, NT)
                grad_probs = dot(value, gob, NN)
                grad_scores = (scale * probs * (grad_probs - delta[h : h + 1, :])).astype(BF)
                grad_key = grad_key + dot(grad_scores, query, NN)
                gq_ref[pl.ds(t * 256 + at, 64), :] = dot(key, grad_scores, TN)
            grad_keys.append(grad_key)
            grad_values.append(grad_value)
        gkv_ref[:, pl.ds(t * 128, 128)] = jnp.concatenate(grad_keys, axis=1).astype(BF)
        gkv_ref[:, pl.ds(HK + t * 128, 128)] = jnp.concatenate(grad_values, axis=1).astype(BF)
        return carry

    lax.fori_loop(0, HEADS // 4, four_heads, 0)


def attend_back(query, kv, lower, gob, lse, delta):
    count = query.shape[0]
    slots = kv.shape[0]
    flops = 10 * HEADS * slots * count * count * HEAD_DIM
    gq, gkv = pl.pallas_call(
        functools.partial(attend_back_kernel, slots, count),
        out_shape=(
            jax.ShapeDtypeStruct((HQ, count), F32),
            jax.ShapeDtypeStruct((slots * count, 2 * HK), BF),
        ),
        in_specs=[VMEM] * 6,
        out_specs=(VMEM, VMEM),
        scratch_shapes=[pltpu.VMEM((slots * count, count), F32)],
        compiler_params=params(),
        cost_estimate=pl.CostEstimate(flops=flops * 4, bytes_accessed=8 << 20, transcendentals=0),
    )(query, kv.reshape(slots * count, 2 * HK), lower, gob, lse, delta)
    return gq, gkv.reshape(slots, count, 2 * HK)


def ffn_kernel(
    planes, depth, hn_ref, og_ref, w_any, gn_out, parts_out, grads_out,
    w, hns, hnt, ogt, mid, pair, send_gn, recv_gn, own_gn, stage, wsem, hsem, gsem, osem,
):
    me = Place(planes, depth)
    count, width = hn_ref.shape
    full = w.shape[2]
    ctxs, dps, rows = w_any.shape[0], w_any.shape[1], w_any.shape[3]
    chunk = 384 if full % 384 == 0 else full

    def load(i, carry):
        c, d = i // dps, i % dps
        for m in range(3):
            pltpu.make_async_copy(
                w_any.at[c, d, m], w.at[m, pl.ds((d * ctxs + c) * rows, rows), :], wsem.at[m, i]
            ).start()
        return carry

    lax.fori_loop(0, ctxs * dps, load, 0)
    greet([me.across(o) for o in range(1, planes)])

    def hn_copy(o):
        return remote(hn_ref, hns.at[o], hsem.at[0, o], hsem.at[1, o], {"dp": me.dp ^ o, "ctx": me.ctx})

    def gn_copy(o):
        return remote(send_gn.at[o], recv_gn.at[o], gsem.at[0, o], gsem.at[1, o], {"dp": me.dp ^ o, "ctx": me.ctx})

    for o in range(1, planes):
        hn_copy(o).start()
    hns[0] = hn_ref[...]

    def loaded(i, carry):
        c, d = i // dps, i % dps
        for m in range(3):
            pltpu.make_async_copy(
                w_any.at[c, d, m], w.at[m, pl.ds((d * ctxs + c) * rows, rows), :], wsem.at[m, i]
            ).wait()
        return carry

    lax.fori_loop(0, ctxs * dps, loaded, 0)

    def block(o, carry):
        @pl.when(o > 0)
        def _():
            hn_copy(o).wait_recv()

        hn = hns[o]
        og = og_ref[o]
        hnt[:, pl.ds(pl.multiple_of(o * count, 128), count)] = hn.T
        ogt[:, pl.ds(pl.multiple_of(o * count, 128), count)] = og.T
        own_gn[0] = jnp.zeros((count, width), F32)
        own_gn[1] = jnp.zeros((count, width), F32)
        at = pl.ds(pl.multiple_of(o * count, 128), count)

        def part(j, inner):
            cols = pl.ds(pl.multiple_of(j * chunk, 128), chunk)
            w_gate, w_up, w_down = w[0, :, cols], w[1, :, cols], w[2, :, cols]
            gate = dot(hn, w_gate, NN)
            upper = dot(hn, w_up, NN)
            sigma = 1.0 / (1.0 + jnp.exp(-gate))
            active = gate * sigma
            middle = (active * upper).astype(BF)
            gmid = dot(og, w_down, NN)
            ggate = (gmid * upper * sigma * (1.0 + gate * (1.0 - sigma))).astype(BF)
            gupper = (gmid * active).astype(BF)
            mid[at, cols] = middle
            pair[0, at, cols] = ggate
            pair[1, at, cols] = gupper
            own_gn[0] += dot(ggate, w_gate, NT) + dot(gupper, w_up, NT)
            own_gn[1] += dot(middle, w_down, NT)
            return inner

        lax.fori_loop(0, full // chunk, part, 0)
        parts_out[o] = own_gn[1].astype(BF)

        @pl.when(o > 0)
        def _():
            send_gn[o] = own_gn[0].astype(BF)
            gn_copy(o).start()

        @pl.when(o == 0)
        def _():
            gn_out[...] = own_gn[0]

        return carry

    lax.fori_loop(0, planes, block, 0)

    strip = ctxs * rows

    def out_copy(m, d):
        return pltpu.make_async_copy(stage.at[m], grads_out.at[d, m], osem.at[m])

    def weight_grads(d, carry):
        left = pl.ds(pl.multiple_of(d * strip, 128), strip)
        for m in range(3):
            @pl.when(d > 0)
            def _():
                out_copy(m, d - 1).wait()

            if m == 2:
                total = dot(ogt[left, :], mid[...], NN)
            else:
                total = dot(hnt[left, :], pair[m], NN)
            stage[m] = total.astype(BF)
            out_copy(m, d).start()
        return carry

    lax.fori_loop(0, dps, weight_grads, 0)
    for m in range(3):
        out_copy(m, dps - 1).wait()
    total = gn_out[...]
    for o in range(1, planes):
        gn_copy(o).wait_recv()
        total = total + recv_gn[o].astype(F32)
    gn_out[...] = total
    for o in range(1, planes):
        gn_copy(o).wait_send()
        hn_copy(o).wait_send()


def ffn(hn, og_all, w_all, planes, depth, collective_id):
    count, width = hn.shape
    ctxs, dps, _, rows, full = w_all.shape
    tokens = planes * count
    strip = ctxs * rows
    flops = 18 * tokens * width * full
    return pl.pallas_call(
        functools.partial(ffn_kernel, planes, depth),
        out_shape=(
            jax.ShapeDtypeStruct((count, width), F32),
            jax.ShapeDtypeStruct((planes, count, width), BF),
            jax.ShapeDtypeStruct((dps, 3, strip, full), BF),
        ),
        in_specs=[VMEM, VMEM, ANY],
        out_specs=(VMEM, VMEM, ANY),
        scratch_shapes=[
            pltpu.VMEM((3, width, full), BF),
            pltpu.VMEM((planes, count, width), BF),
            pltpu.VMEM((width, tokens), BF),
            pltpu.VMEM((width, tokens), BF),
            pltpu.VMEM((tokens, full), BF),
            pltpu.VMEM((2, tokens, full), BF),
            pltpu.VMEM((planes, count, width), BF),
            pltpu.VMEM((planes, count, width), BF),
            pltpu.VMEM((2, count, width), F32),
            pltpu.VMEM((3, strip, full), BF),
            DMA((3, ctxs * dps)),
            DMA((2, planes)),
            DMA((2, planes)),
            DMA((3,)),
        ],
        compiler_params=params(collective_id),
        cost_estimate=pl.CostEstimate(flops=flops, bytes_accessed=20 << 20, transcendentals=0),
    )(hn, og_all, w_all)


def give_back_kernel(
    planes, depth, turns, d_ref, parts_ref, mixed_ref, kv_out, block_out, dsum, from_core, from_z, from_plane, cs, zs, ps
):
    me = Place(planes, depth)
    half = turns // 2
    greet(
        [me.across(o) for o in range(1, planes)]
        + [me.along(me.ahead(k)) for k in range(1, depth)]
        + [me.sibling()]
    )

    def c_copy(i):
        return remote(d_ref.at[2 * i + 1], from_core.at[i], cs.at[0, i], cs.at[1, i], me.sibling())

    def z_copy(k):
        return remote(dsum.at[k], from_z.at[k], zs.at[0, k], zs.at[1, k], me.along(me.behind(k)))

    def p_copy(o):
        return remote(parts_ref.at[o], from_plane.at[o], ps.at[0, o], ps.at[1, o], me.across(o))

    for i in range(half):
        @pl.when(me.z - i - 1 + me.core >= 0)
        def _():
            c_copy(i).start()

    for o in range(1, planes):
        p_copy(o).start()

    for k in range(half, 0, -1):
        @pl.when(me.z - k >= 0)
        def _():
            @pl.when(me.core == 0)
            def _():
                if k < half:
                    c_copy(k).wait_recv()
                    dsum[k] = (d_ref[2 * k].astype(F32) + from_core[min(k, half - 1)].astype(F32)).astype(BF)
                else:
                    dsum[k] = d_ref[2 * k]

            @pl.when(me.core == 1)
            def _():
                c_copy(k - 1).wait_recv()
                dsum[k] = (d_ref[2 * k].astype(F32) + from_core[k - 1].astype(F32)).astype(BF)

            z_copy(k).start()

    kv_out[...] = d_ref[0].astype(F32)

    @pl.when(me.core == 0)
    def _():
        c_copy(0).wait_recv()
        kv_out[...] += from_core[0].astype(F32)

    for k in range(1, half + 1):
        @pl.when(me.z + k < depth)
        def _():
            z_copy(k).wait_recv()
            kv_out[...] += from_z[k].astype(F32)

    total = mixed_ref[...] + parts_ref[0].astype(F32)
    for o in range(1, planes):
        p_copy(o).wait_recv()
        total = total + from_plane[o].astype(F32)
    block_out[...] = total.astype(BF)

    for o in range(1, planes):
        p_copy(o).wait_send()
    for i in range(half):
        @pl.when(me.z - i - 1 + me.core >= 0)
        def _():
            c_copy(i).wait_send()
    for k in range(1, half + 1):
        @pl.when(me.z - k >= 0)
        def _():
            z_copy(k).wait_send()


def give_back(gkv, parts, mixed, planes, depth, collective_id):
    slots, count, width = gkv.shape
    half = (slots - 1) // 2
    return pl.pallas_call(
        functools.partial(give_back_kernel, planes, depth, slots - 1),
        out_shape=(
            jax.ShapeDtypeStruct((count, width), F32),
            jax.ShapeDtypeStruct((count, D), BF),
        ),
        in_specs=[VMEM, VMEM, VMEM],
        out_specs=(VMEM, VMEM),
        scratch_shapes=[
            pltpu.VMEM((half + 1, count, width), BF),
            pltpu.VMEM((half, count, width), BF),
            pltpu.VMEM((half + 1, count, width), BF),
            pltpu.VMEM((planes, count, D), BF),
            DMA((2, half)),
            DMA((2, half + 1)),
            DMA((2, planes)),
        ],
        compiler_params=params(collective_id),
    )(gkv, parts, mixed)


def scatter_kernel(planes, depth, p_ref, out_ref, from_core, sums, from_plane, total, from_z, cs, ps, zs):
    me = Place(planes, depth)
    greet(
        [me.across(o) for o in range(1, planes)]
        + [me.along(me.ahead(k)) for k in range(1, depth)]
        + [me.sibling()]
    )

    def c_copy(o):
        return remote(
            p_ref.at[me.dp ^ o, 1 - me.core], from_core.at[o], cs.at[0, o], cs.at[1, o], me.sibling()
        )

    def p_copy(o):
        return remote(sums.at[o], from_plane.at[o], ps.at[0, o], ps.at[1, o], me.across(o))

    def z_copy(k):
        return remote(total.at[me.ahead(k)], from_z.at[k], zs.at[0, k], zs.at[1, k], me.along(me.ahead(k)))

    order = list(range(1, planes)) + [0]
    for o in order:
        c_copy(o).start()
    for o in order:
        c_copy(o).wait_recv()
        sums[o] = (p_ref[me.dp ^ o, me.core].astype(F32) + from_core[o].astype(F32)).astype(BF)
        if o > 0:
            p_copy(o).start()
    for o in range(1, planes):
        p_copy(o).wait_recv()
    for k in range(depth):
        z = me.ahead(k)
        value = sums[0, z].astype(F32)
        for o in range(1, planes):
            value = value + from_plane[o, z].astype(F32)
        total[z] = value.astype(BF)
        if k > 0:
            z_copy(k).start()
        else:
            out_ref[...] = value
    for k in range(1, depth):
        z_copy(k).wait_recv()
        out_ref[...] += from_z[k].astype(F32)
    for o in range(planes):
        c_copy(o).wait_send()
    for o in range(1, planes):
        p_copy(o).wait_send()
    for k in range(1, depth):
        z_copy(k).wait_send()


def scatter_all(partial, planes, depth, collective_id):
    rows, columns = partial.shape[3:]
    return pl.pallas_call(
        functools.partial(scatter_kernel, planes, depth),
        out_shape=jax.ShapeDtypeStruct((rows, columns), F32),
        in_specs=[VMEM],
        out_specs=VMEM,
        scratch_shapes=[
            pltpu.VMEM((planes, depth, rows, columns), BF),
            pltpu.VMEM((planes, depth, rows, columns), BF),
            pltpu.VMEM((planes, depth, rows, columns), BF),
            pltpu.VMEM((depth, rows, columns), BF),
            pltpu.VMEM((depth, rows, columns), BF),
            DMA((2, planes)),
            DMA((2, planes)),
            DMA((2, depth)),
        ],
        compiler_params=params(collective_id),
    )(partial)


def per_device(
    tokens_in,
    positions,
    out_grad,
    w_qkv,
    w_output,
    w_gate_up,
    w_down,
    norm_gains,
    first_qkv,
    first_output,
    first_gate_up,
    first_down,
    first_gains,
    second_qkv,
    second_output,
    second_gate_up,
    second_down,
    second_gains,
):
    planes, ctxs = lax.axis_size("dp"), lax.axis_size("ctx")
    depth = ctxs // 2
    turns = ctxs // 2
    rows = w_qkv.shape[0]
    full = w_down.shape[1] // planes
    n_gains = norm_gains.shape[0]
    count = tokens_in.shape[0] * tokens_in.shape[1]

    w_blocks = jnp.concatenate(
        [
            w_gate_up.astype(BF).reshape(rows, 2, planes, full).transpose(2, 1, 0, 3),
            w_down.astype(BF).reshape(rows, 1, planes, full).transpose(2, 1, 0, 3),
        ],
        axis=1,
    )
    w_mine = plane_exchange(w_blocks, planes, depth, 0)
    w_all = lax.all_gather(w_mine, "ctx", axis=0, tiled=False)

    gains_row = jnp.pad(norm_gains.astype(BF)[None, :], ((0, rows - 1), (0, 128 - n_gains)))
    front = gather_all(
        jnp.concatenate([w_qkv.astype(BF), gains_row], axis=1), planes, depth, 1
    )
    qkv_b = front.reshape(D, 2 * HQ + 128)[:, : 2 * HQ]
    gains_b = front[:, :, :, 0, 2 * HQ : 2 * HQ + n_gains].reshape(-1)
    gains_used = 1.0 + gains_b.astype(F32)
    gain_ffn = split_gains(gains_used)[1]
    tokens_f = tokens_in.reshape(count, D).astype(F32)
    places = positions.reshape(count)
    cotangent = out_grad.reshape(count, D)
    query_b, key_b, value_b, saved = front_pass(tokens_f, places, qkv_b, gains_used)
    query = query_b.reshape(count, HQ)
    kv = jnp.concatenate([key_b.reshape(count, HK), value_b.reshape(count, HK)], axis=1)
    kv_all, og_all, wo_all = halo(kv, cotangent, w_output.astype(BF), planes, depth, turns, 2)
    output_b = wo_all.reshape(HQ, D)
    lower = (jnp.arange(count, dtype=jnp.int32) - places)[None, :]
    attn_t, lse = attend(query, kv_all, lower)
    mixed = tokens_f + dot(attn_t, output_b, TN)
    normed, unit_f, recip_f = norm_forward(mixed, gain_ffn)
    ffn_in = normed.astype(BF)
    if rows % 16 == 0:
        w_used = w_all
    else:
        w_used = w_all.transpose(2, 1, 0, 3, 4).reshape(1, 1, 3, D, full)
    grad_normed, parts, grads = ffn(ffn_in, og_all, w_used, planes, depth, 3)
    grads = grads.reshape(planes, 3, ctxs, rows, full) if rows % 16 == 0 else grads.reshape(3, planes, ctxs, rows, full).transpose(1, 0, 2, 3, 4)
    grads_mine = lax.psum_scatter(
        grads.transpose(2, 0, 1, 3, 4), "ctx", scatter_dimension=0, tiled=False
    )

    grad_from_norm, grad_gain_ffn = norm_backward(grad_normed, gain_ffn, unit_f, recip_f)
    grad_mixed = cotangent.astype(F32) + grad_from_norm
    grad_mixed_b = grad_mixed.astype(BF)
    grad_output = dot(attn_t, grad_mixed_b, NN)
    gob_t = dot(output_b, grad_mixed_b, NT).astype(BF)
    delta = jnp.sum(
        (gob_t.astype(F32) * attn_t.astype(F32)).reshape(HEADS // 4, 4, HEAD_DIM, count), axis=2
    )
    gq_t, gkv_all = attend_back(query, kv_all, lower, gob_t, lse, delta)
    grad_kv, block_out = give_back(gkv_all, parts, mixed, planes, depth, 4)
    input_grad, grad_qkv, grad_gain_attn, grad_gain_q, grad_gain_k = tail_pass(
        gq_t.T.reshape(count, HEADS, HEAD_DIM),
        grad_kv[:, :HK].reshape(count, KV_HEADS, HEAD_DIM),
        grad_kv[:, HK:].reshape(count, KV_HEADS, HEAD_DIM),
        saved,
        gains_used,
        qkv_b,
        grad_mixed,
    )
    grad_gains = jnp.concatenate([grad_gain_attn, grad_gain_ffn, grad_gain_q, grad_gain_k])
    gains_block = jnp.pad(
        grad_gains.astype(BF).reshape(planes * ctxs, 1, n_gains), ((0, 0), (0, rows - 1), (0, 128 - n_gains))
    ).reshape(D, 128)
    partial = jnp.concatenate([grad_qkv.astype(BF), grad_output.astype(BF), gains_block], axis=1)
    partial = partial.reshape(planes, depth, 2, rows, 3 * D + 128).transpose(0, 2, 1, 3, 4)
    mine = scatter_all(partial, planes, depth, 5)
    shard_qkv = mine[:, : 2 * D]
    shard_output = mine[:, 2 * D : 3 * D]
    shard_gains = mine[0, 3 * D : 3 * D + n_gains]

    ffn_shards = plane_exchange(grads_mine, planes, depth, 6).astype(F32)
    shard_gate_up = ffn_shards[:, :2].transpose(2, 1, 0, 3).reshape(rows, 2 * planes * full)
    shard_down = ffn_shards[:, 2].transpose(1, 0, 2).reshape(rows, planes * full)

    new_qkv, new_first_qkv, new_second_qkv = adam_step(
        w_qkv, shard_qkv, first_qkv, second_qkv, 0.02, 0.1
    )
    new_output, new_first_output, new_second_output = adam_step(
        w_output, shard_output, first_output, second_output, 0.2, 0.1
    )
    new_gate_up, new_first_gate_up, new_second_gate_up = adam_step(
        w_gate_up, shard_gate_up, first_gate_up, second_gate_up, 0.02, 0.1
    )
    new_down, new_first_down, new_second_down = adam_step(
        w_down, shard_down, first_down, second_down, 0.02, 0.1
    )
    new_gains, new_first_gains, new_second_gains = adam_step(
        norm_gains, shard_gains, first_gains, second_gains, 0.1, 0.0
    )
    return (
        block_out.reshape(tokens_in.shape),
        input_grad.reshape(tokens_in.shape),
        shard_qkv,
        shard_output,
        shard_gate_up,
        shard_down,
        shard_gains,
        new_qkv,
        new_output,
        new_gate_up,
        new_down,
        new_gains,
        new_first_qkv,
        new_first_output,
        new_first_gate_up,
        new_first_down,
        new_first_gains,
        new_second_qkv,
        new_second_output,
        new_second_gate_up,
        new_second_down,
        new_second_gains,
    )


def solution(mesh):
    in_specs = (
        P("dp", "ctx", None),
        P("dp", "ctx"),
        P("dp", "ctx", None),
        P(("dp", "ctx"), None),
        P(("dp", "ctx"), None),
        P(("dp", "ctx"), None),
        P(("dp", "ctx"), None),
        P(("dp", "ctx")),
        P(("dp", "ctx"), None),
        P(("dp", "ctx"), None),
        P(("dp", "ctx"), None),
        P(("dp", "ctx"), None),
        P(("dp", "ctx")),
        P(("dp", "ctx"), None),
        P(("dp", "ctx"), None),
        P(("dp", "ctx"), None),
        P(("dp", "ctx"), None),
        P(("dp", "ctx")),
    )
    out_specs = (
        P("dp", "ctx", None),
        P("dp", "ctx", None),
        P(("dp", "ctx"), None),
        P(("dp", "ctx"), None),
        P(("dp", "ctx"), None),
        P(("dp", "ctx"), None),
        P(("dp", "ctx")),
        P(("dp", "ctx"), None),
        P(("dp", "ctx"), None),
        P(("dp", "ctx"), None),
        P(("dp", "ctx"), None),
        P(("dp", "ctx")),
        P(("dp", "ctx"), None),
        P(("dp", "ctx"), None),
        P(("dp", "ctx"), None),
        P(("dp", "ctx"), None),
        P(("dp", "ctx")),
        P(("dp", "ctx"), None),
        P(("dp", "ctx"), None),
        P(("dp", "ctx"), None),
        P(("dp", "ctx"), None),
        P(("dp", "ctx")),
    )
    return jax.shard_map(
        per_device, mesh=mesh, in_specs=in_specs, out_specs=out_specs, check_vma=False
    )
```

time: 1290 us -> 508 us (0.39)
  waiting for transfers between devices: 826 us -> 0.04 us
  Pallas kernels: 0 us -> 391 us
  starting transfers between devices: 123 us -> 0.08 us
  matrix products: 100 us -> 15.1 us
  blocking collectives: 82.5 us -> 0 us
  other arithmetic: 64.3 us -> 33.2 us
  local copies, waits for them, and re-layouts: 70.5 us -> 45.6 us
    pallas_call x0 -> x9, Pallas kernels: none -> 391 us  [the longest x1 111 us: halo(): pl.pallas_call(functools.partial(halo_kernel, planes, depth, turns), out_...]
    reduce_scatter x3 -> x1, waiting for transfers between devices: 382 us -> 0.01 us  [per_device(): lax.psum_scatter(grads.transpose(2, 0, 1, 3, 4), 'ctx', scatter_dimension...]
    all_gather x4 -> x1, waiting for transfers between devices: 216 us -> 0.01 us  [per_device(): w_all = lax.all_gather(w_mine, 'ctx', axis=0, tiled=False)]
    unnamed x9 -> x2, waiting for transfers between devices: 209 us -> 0.03 us
    ppermute x13 -> x0, starting transfers between devices: 122 us -> none  [the longest x5 63.9 us: shifted(): return lax.ppermute(value, axis, pairs)]
    unnamed x2 -> x0, blocking collectives: 82.5 us -> none
    dot_general x16 -> x3, matrix products: 86.2 us -> 5.46 us  [dot(): return lax.dot_general(a, b, dims, preferred_element_type=F32)]
    unnamed x109 -> x110, local copies, waits for them, and re-layouts: 28.3 us -> 6.65 us
  transfers between devices with their start and end apart: 21 -> 2, of which waited for: 12 -> 0; matrix products, arithmetic and copies ran while one was open for 15% -> 14% of each run, Pallas kernels for 0% -> 61%
where the time goes in v1:
time: 508 us; the launch traced here: 501 us
  Pallas kernels  391 us (77%)
  local copies, waits for them, and re-layouts  45.6 us (9%)
  other arithmetic  33.2 us (7%)
  between operations  15.5 us (3%)
  matrix products  15.1 us (3%)
    pallas_call x1, Pallas kernels, halo(): pl.pallas_call(functools.partial(halo_kernel, planes, depth, turns), out_...  111 us
    pallas_call x1, Pallas kernels, scatter_all(): pl.pallas_call(functools.partial(scatter_kernel, planes, depth), out_shap...  84.7 us
    pallas_call x1, Pallas kernels, ffn(): pl.pallas_call(functools.partial(ffn_kernel, planes, depth), out_shape=(j...  57.1 us
    pallas_call x1, Pallas kernels, give_back(): pl.pallas_call(functools.partial(give_back_kernel, planes, depth, slots -...  46.7 us
    pallas_call x1, Pallas kernels, gather_all(): pl.pallas_call(functools.partial(gather_kernel, planes, depth), out_shape...  32.2 us
    pallas_call x2, Pallas kernels, plane_exchange(): pl.pallas_call(functools.partial(plane_exchange_kernel, planes, depth), o...  26.6 us
    pallas_call x1, Pallas kernels, attend_back(): pl.pallas_call(functools.partial(attend_back_kernel, slots, count), out_s...  21.1 us
    pallas_call x1, Pallas kernels, attend(): pl.pallas_call(functools.partial(attend_kernel, slots, count), out_shape=...  11.8 us
  transfers between devices with their start and end apart: 2, of which 0 were waited for; matrix products, arithmetic and copies ran while one was open for 14% of the time, Pallas kernels for 61%

profile of v1, /device:TPU:0, one launch (start us, length us, event | category | flops | bytes accessed | tf_op | source)
XLA Modules:
  0.0 500.5 jit_solution(1965393738223436102)
XLA Ops:
  7.2 1.4 convert_element_type.105
  9.4 1.0 pad_maximum_fusion.2.w_ref
  10.4 14.7 %shard_map.348 = bf16[4,3,32,1152]{3,2,1,0:T(8,128)(2,1)} custom-call(bf16[4,3,32,1152]{3,2,1,0:T(8,128)(2,1)} %pad_maximum_fusion.2.w_ref), custom_call_target="tpu_custom_call" | custom-call | tf_op jit(solution)/shard_map/pallas_call | solution.py:211
  25.9 32.2 %shard_map.345 = bf16[4,4,2,32,2176]{4,3,2,1,0:T(8,128)(2,1)} custom-call(bf16[32,2176]{1,0:T(8,128)(2,1)} %fusion.26.x_ref), custom_call_target="tpu_custom_call" | custom-call | tf_op jit(solution)/shard_map/pallas_call | solution.py:289
  59.3 3.6 fusion.2
  63.1 1.2 copy-done.6
  68.3 1.0 copy.106.q_ref
  70.2 110.9 %shard_map.346 = (bf16[5,256,1024]{2,1,0:T(8,128)(2,1)}, bf16[4,256,1024]{2,1,0:T(8,128)(2,1)}, bf16[4,4,2,32,1024]{4,3,2,1,0:T(8,128)(2,1)}) custom-call(bf16[256,1024]{1,0:T(8,128)(2,1)} %pad_maximum_fusion.4.kv_ref, bf16[256,1024]{1,0:T(8,128)(2,1)} %bitcast.104, bf16[32,1024]{1,0:T(8,128)(2,1)} %convert_element_type.102.wo_ref), custom_call_target="tpu_custom_call" | custom-call | tf_op jit(solution)/shard_map/pallas_call | solution.py:390
  181.1 11.8 %shard_map.347 = (bf16[1024,256]{1,0:T(8,128)(2,1)}, f32[4,4,256]{2,1,0:T(4,128)}) custom-call(bf16[256,1024]{1,0:T(8,128)(2,1)} %copy.106.q_ref, bf16[1280,1024]{1,0:T(8,128)(2,1)} %bitcast.113, s32[1,256]{1,0:T(1,128)} %get-tuple-element.86.lower_ref), custom_call_target="tpu_custom_call" | custom-call | flops 5368709120 | bytes 4194304 | tf_op jit(solution)/shard_map/pallas_call | solution.py:449
  192.9 2.6 multiply_reduce_fusion.3
  195.5 1.1 multiply_convert_fusion.1.hn_ref
  196.6 57.1 %shard_map.349 = (f32[256,1024]{1,0:T(8,128)}, bf16[4,256,1024]{2,1,0:T(8,128)(2,1)}, bf16[4,3,256,1152]{3,2,1,0:T(8,128)(2,1)}) custom-call(bf16[256,1024]{1,0:T(8,128)(2,1)} %multiply_convert_fusion.1.hn_ref, bf16[4,256,1024]{2,1,0:T(8,128)(2,1)} %get-tuple-element.37.og_ref, bf16[8,4,3,32,1152]{4,3,2,1,0:T(8,128)(2,1)} %bitcast.112), custom_call_target="tpu_custom_call" | custom-call | flops 21743271936 | bytes 20971520 | tf_op jit(solution)/shard_map/pallas_call | solution.py:643
  253.7 6.7 %copy.139 = bf16[4,3,8,32,1152]{4,3,1,0,2:T(8,128)(2,1)} copy(bf16[4,3,8,32,1152]{4,3,2,1,0:T(8,128)(2,1)} %bitcast.86) | data formatting | bytes 14155776 | tf_op jit(solution)/shard_map/reshape | solution.py:909
  260.5 2.2 reshape.293
  262.8 1.9 reshape.292
  264.8 1.3 copy.110
  267.0 2.0 copy.115
  271.6 2.2 bitcast_reduce_fusion
  273.7 21.1 %shard_map.350 = (f32[1024,256]{1,0:T(8,128)}, bf16[1280,1024]{1,0:T(8,128)(2,1)}) custom-call(bf16[256,1024]{1,0:T(8,128)(2,1)} %copy.106.q_ref, bf16[1280,1024]{1,0:T(8,128)(2,1)} %bitcast.114, s32[1,256]{1,0:T(1,128)} %get-tuple-element.86.lower_ref, bf16[1024,256]{1,0:T(8,128)(2,1)} %get-tuple-element.91.gob_ref, ...), custom_call_target="tpu_custom_call" | custom-call | flops 13421772800 | bytes 8388608 | tf_op jit(solution)/shard_map/pallas_call | solution.py:501
  294.9 46.7 %shard_map.351 = (f32[256,1024]{1,0:T(8,128)}, bf16[256,1024]{1,0:T(8,128)(2,1)}) custom-call(bf16[5,256,1024]{2,1,0:T(8,128)(2,1)} %bitcast.95, bf16[4,256,1024]{2,1,0:T(8,128)(2,1)} %get-tuple-element.41.parts_ref, f32[256,1024]{1,0:T(8,128)} %copy-done), custom_call_target="tpu_custom_call" | custom-call | tf_op jit(solution)/shard_map/pallas_call | solution.py:753
  341.6 2.0 slice.92
  343.6 1.1 slice.148
  344.8 2.5 copy.116
  347.3 2.5 copy.117
  349.8 1.2 pad_maximum_fusion
  351.1 1.3 copy.109
  352.4 1.3 copy.107
  354.0 1.3 copy.119
  355.4 1.3 copy.120
  356.7 0.9 pad_maximum_fusion.5
  357.6 1.0 copy.114
  358.6 2.2 copy.112
  360.8 2.6 fusion.18
  363.5 2.9 fusion.4
  366.7 0.9 copy-done.17
  369.1 4.6 fusion.16
  374.9 1.4 convolution_convert_fusion
  376.3 3.3 maximum_bitcast_fusion.p_ref
  379.7 84.7 %shard_map.352 = f32[32,3200]{1,0:T(8,128)} custom-call(bf16[4,2,4,32,3200]{4,3,2,1,0:T(8,128)(2,1)} %maximum_bitcast_fusion.p_ref), custom_call_target="tpu_custom_call" | custom-call | tf_op jit(solution)/shard_map/pallas_call | solution.py:826
  464.4 1.2 multiply_subtract_fusion.6
  465.6 1.7 multiply_subtract_fusion.5
  467.4 1.3 fusion.15
  468.6 1.0 multiply_subtract_fusion.3
  469.7 11.8 %shard_map.353 = bf16[4,3,32,1152]{3,2,1,0:T(8,128)(2,1)} custom-call(bf16[4,3,32,1152]{3,2,1,0:T(8,128)(2,1)} %bitcast.109), custom_call_target="tpu_custom_call" | custom-call | tf_op jit(solution)/shard_map/pallas_call | solution.py:211
  481.5 1.3 convert_element_type.114
  485.1 1.5 copy.131
  486.7 4.2 multiply_subtract_fusion
  490.9 1.5 multiply_subtract_fusion.1
  (181 shorter events, 17.7 us)
Async XLA Ops:
  7.2 2.0 copy-start.22
  7.2 189.4 %all-gather.3.cloned.1.call-start = ((), (), s32[]{:S(2)}) async-start(), calls=%async_computation.2 | async-start | bytes 7962624 | tf_op jit(solution)/shard_map/all_gather | solution.py:881
  9.3 15.8 %copy-start.34 = (f32[32,2048]{1,0:T(8,128)S(1)}, f32[32,2048]{1,0:T(8,128)}, u32[]{:S(2)}) copy-start(f32[32,2048]{1,0:T(8,128)} %param.21) | copy-start | bytes 786436
  9.3 15.9 %copy-start.50 = (f32[68]{0:T(128)S(1)}, f32[68]{0:T(128)}, u32[]{:S(2)}) copy-start(f32[68]{0:T(128)} %param.25) | copy-start | bytes 820
  25.1 444.5 %reduce-scatter.2.cloned.1.call-start = ((), (), s32[]{:S(2)}) async-start(), calls=%async_computation.1 | async-start | bytes 7962624 | tf_op jit(solution)/shard_map/reduce_scatter | solution.py:910
  25.9 33.2 %copy-start.9 = (bf16[1,256,1024]{2,1,0:T(8,128)(2,1)S(1)}, bf16[1,256,1024]{2,1,0:T(8,128)(2,1)}, u32[]{:S(2)}) copy-start(bf16[1,256,1024]{2,1,0:T(8,128)(2,1)} %param.18) | copy-start | bytes 1572868
  59.3 3.7 copy-start.47
  63.0 1.4 copy-start.6
  63.0 5.0 %copy-start.8 = (f32[256,512]{1,0:T(8,128)}, f32[256,512]{1,0:T(8,128)S(1)}, u32[]{:S(2)}) copy-start(f32[256,512]{1,0:T(8,128)S(1)} %slice.107) | copy-start | bytes 1572868
  63.0 1.7 copy-start.49
  64.4 2.3 copy-start.39
  64.6 3.1 copy-start.4
  181.1 11.8 %copy-start.10 = (bf16[1,256,1024]{2,1,0:T(8,128)(2,1)S(1)}, bf16[1,256,1024]{2,1,0:T(8,128)(2,1)}, u32[]{:S(2)}) copy-start(bf16[1,256,1024]{2,1,0:T(8,128)(2,1)} %param.18) | copy-start | bytes 1572868
  195.5 74.3 %copy-start = (f32[256,1024]{1,0:T(8,128)}, f32[256,1024]{1,0:T(8,128)S(1)}, u32[]{:S(2)}) copy-start(f32[256,1024]{1,0:T(8,128)S(1)} %get-tuple-element.89.mixed_ref) | copy-start | bytes 3145732
  266.1 3.3 copy-start.20
  269.3 1.3 copy-start.26
  269.7 1.8 copy-start.3
  269.7 1.8 copy-start.14
  341.6 3.1 copy-start.31
  351.0 1.4 copy-start.16
  352.4 1.3 copy-start.25
  354.0 2.7 copy-start.5
  358.6 4.8 copy-start.1
  360.8 2.6 copy-start.2
  363.5 3.0 copy-start.7
  363.5 3.0 copy-start.27
  363.5 2.9 copy-start.28
  363.5 2.9 copy-start.29
  363.5 3.2 copy-start.19
  366.5 1.5 copy-start.18
  369.1 5.0 copy-start.15
  379.6 84.8 %copy-start.51 = (f32[68]{0:T(128)S(1)}, f32[68]{0:T(128)}, u32[]{:S(2)}) copy-start(f32[68]{0:T(128)} %param.25) | copy-start | bytes 820
  379.6 84.8 %copy-start.52 = (f32[68]{0:T(128)S(1)}, f32[68]{0:T(128)}, u32[]{:S(2)}) copy-start(f32[68]{0:T(128)} %param.30) | copy-start | bytes 820
  379.6 84.8 %copy-start.53 = (f32[68]{0:T(128)S(1)}, f32[68]{0:T(128)}, u32[]{:S(2)}) copy-start(f32[68]{0:T(128)} %param.35) | copy-start | bytes 820
  379.6 86.0 %copy-start.40 = (f32[32,1024]{1,0:T(8,128)S(1)}, f32[32,1024]{1,0:T(8,128)}, u32[]{:S(2)}) copy-start(f32[32,1024]{1,0:T(8,128)} %param.22) | copy-start | bytes 393220
  379.6 86.0 %copy-start.45 = (f32[32,1024]{1,0:T(8,128)S(1)}, f32[32,1024]{1,0:T(8,128)}, u32[]{:S(2)}) copy-start(f32[32,1024]{1,0:T(8,128)} %param.27) | copy-start | bytes 393220
  379.6 86.0 %copy-start.46 = (f32[32,1024]{1,0:T(8,128)S(1)}, f32[32,1024]{1,0:T(8,128)}, u32[]{:S(2)}) copy-start(f32[32,1024]{1,0:T(8,128)} %param.32) | copy-start | bytes 393220
  379.7 87.7 %copy-start.33 = (f32[256,1024]{1,0:T(8,128)S(1)}, f32[256,1024]{1,0:T(8,128)}, u32[]{:S(2)}) copy-start(f32[256,1024]{1,0:T(8,128)} %get-tuple-element.92) | copy-start | bytes 3145732
  467.3 1.3 copy-start.35
  467.4 1.3 copy-start.41
  467.4 1.3 copy-start.42
  484.5 2.1 copy-start.12
  485.1 5.8 %copy-start.13 = (f32[32,9216]{1,0:T(8,128)}, f32[32,9216]{1,0:T(8,128)S(1)}, u32[]{:S(2)}) copy-start(f32[32,9216]{1,0:T(8,128)S(1)} %reshape.295) | copy-start | bytes 3538948
  486.6 4.3 copy-start.24
  486.7 4.3 copy-start.23
  486.7 4.3 copy-start.36
  486.7 4.3 copy-start.37
  490.9 1.5 copy-start.38
  (8 other events, 8.7 us)
Sparse Core Ops, SparseCore 0:
  25.3 83.6 all-gather.2
  260.5 97.2 reduce-scatter.1

commit v2 on v1

v2 whole, which is shorter than its diff:
```python
import functools
import math

import jax
import jax.numpy as jnp
from jax import lax
from jax.experimental import pallas as pl
from jax.experimental.pallas import tpu as pltpu
from jax.sharding import PartitionSpec as P

D = 1024
HEADS = 16
KV_HEADS = 8
HEAD_DIM = 64
STEP = 4
HQ = 1024
HK = 512


EPS = 1e-05
THETA = 1000000.0
NEG_BIG = -1e30
BETA_ONE = 0.9
BETA_TWO = 0.95
ADAM_EPS = 1e-08


def rope_tables(places):
    half = HEAD_DIM // 2
    freqs = jnp.exp(-math.log(THETA) * (2.0 * jnp.arange(half, dtype=jnp.float32) / HEAD_DIM))
    angles = freqs[:, None] * places.astype(jnp.float32)[None, :]
    return (jnp.cos(angles), jnp.sin(angles))


def adam_step(weight, grad, first, second, rate, decay):
    first_new = BETA_ONE * first + (1.0 - BETA_ONE) * grad
    second_new = BETA_TWO * second + (1.0 - BETA_TWO) * grad * grad
    first_hat = first_new / (1.0 - BETA_ONE**STEP)
    second_hat = second_new / (1.0 - BETA_TWO**STEP)
    weight_new = weight - rate * (first_hat / (jnp.sqrt(second_hat) + ADAM_EPS) + decay * weight)
    return (weight_new, first_new, second_new)


BF = jnp.bfloat16
F32 = jnp.float32
MESH_ID = pl.DeviceIdType.MESH
ANY = pl.BlockSpec(memory_space=pl.ANY)
VMEM = pl.BlockSpec(memory_space=pltpu.VMEM)
DMA = pltpu.SemaphoreType.DMA
NN = (((1,), (0,)), ((), ()))
NT = (((1,), (1,)), ((), ()))
TN = (((0,), (0,)), ((), ()))
VMEM_BYTES = 60 << 20
GROUPS = HEADS // 4


def dot(a, b, dims):
    return lax.dot_general(a, b, dims, preferred_element_type=F32)


class Place:
    def __init__(self, planes, depth):
        self.planes, self.depth = planes, depth
        self.dp = lax.axis_index("dp")
        self.ctx = lax.axis_index("ctx")
        self.z = self.ctx // 2
        self.core = self.ctx % 2

    def sibling(self):
        return {"dp": self.dp, "ctx": self.z * 2 + 1 - self.core}

    def across(self, o):
        return {"dp": self.dp ^ o, "ctx": self.ctx}

    def behind(self, k):
        return lax.rem(self.z + self.depth - k, self.depth)

    def ahead(self, k):
        return lax.rem(self.z + k, self.depth)

    def along(self, z):
        return {"dp": self.dp, "ctx": z * 2 + self.core}

    def plane(self):
        return [self.across(o) for o in range(1, self.planes)]

    def line(self):
        return [self.along(self.ahead(k)) for k in range(1, self.depth)]


def greet(devices):
    barrier = pltpu.get_barrier_semaphore()
    for device in devices:
        pl.semaphore_signal(barrier, inc=1, device_id=device, device_id_type=MESH_ID)
    pl.semaphore_wait(barrier, len(devices))


def remote(src, dst, send, recv, device):
    return pltpu.make_async_remote_copy(
        src_ref=src, dst_ref=dst, send_sem=send, recv_sem=recv, device_id=device, device_id_type=MESH_ID
    )


def params(collective_id):
    return pltpu.CompilerParams(
        vmem_limit_bytes=VMEM_BYTES, collective_id=collective_id, has_side_effects=True
    )


def exchange_kernel(planes, depth, counts, *refs):
    n_plane, n_line = counts
    n = n_plane + n_line
    ins, outs, (send, recv, local) = refs[:n], refs[n : 2 * n], refs[2 * n :]
    me = Place(planes, depth)
    owns, copies, waits = [], [], []
    for i in range(n):
        if i < n_plane:
            own = pltpu.make_async_copy(ins[i].at[me.dp], outs[i].at[me.dp], local.at[i])
        else:
            own = pltpu.make_async_copy(ins[i], outs[i].at[me.z], local.at[i])
        own.start()
        owns.append(own)
    greet(me.plane() + (me.line() if n_line else []))
    for i in range(n_plane, n):
        for k in range(1, depth):
            sems = (send.at[i, k], recv.at[i, k])
            copies.append(remote(ins[i], outs[i].at[me.z], *sems, me.along(me.ahead(k))))
            waits.append(remote(ins[i], outs[i].at[me.behind(k)], *sems, me.along(me.ahead(k))))
    for o in range(1, planes):
        for i in range(n_plane):
            sems = (send.at[i, o], recv.at[i, o])
            copies.append(remote(ins[i].at[me.dp ^ o], outs[i].at[me.dp], *sems, me.across(o)))
            waits.append(remote(ins[i].at[me.dp], outs[i].at[me.dp ^ o], *sems, me.across(o)))
    for copy in copies:
        copy.start()
    for own in owns:
        own.wait()
    for copy in copies:
        copy.wait_send()
    for wait in waits:
        wait.wait_recv()


def exchange(plane_arrays, line_arrays, planes, depth, collective_id):
    counts = (len(plane_arrays), len(line_arrays))
    n = sum(counts)
    most = max(planes, depth)
    shapes = [jax.ShapeDtypeStruct(a.shape, a.dtype) for a in plane_arrays]
    shapes += [jax.ShapeDtypeStruct((depth,) + a.shape, a.dtype) for a in line_arrays]
    return pl.pallas_call(
        functools.partial(exchange_kernel, planes, depth, counts),
        out_shape=tuple(shapes),
        in_specs=[ANY] * n,
        out_specs=(ANY,) * n,
        scratch_shapes=[DMA((n, most)), DMA((n, most)), DMA((n,))],
        compiler_params=params(collective_id),
    )(*plane_arrays, *line_arrays)


class Spread:
    def __init__(self, me, x_ref, g_ref, sems):
        self.me, self.x, self.g, self.sems = me, x_ref, g_ref, sems
        self.sent = []

    def push(self, src, dst, kind, o, device):
        copy = remote(src, dst, self.sems.at[kind, o], self.sems.at[kind + 1, o], device)
        copy.start()
        self.sent.append(copy)

    def mine(self, o, core):
        return self.g.at[self.me.dp ^ o, :, core]

    def start(self):
        me = self.me
        self.own = pltpu.make_async_copy(self.x, self.mine(0, me.core), self.sems.at[4, 0])
        self.own.start()

    def first(self):
        me = self.me
        for o in range(1, me.planes):
            self.push(self.x, self.mine(0, me.core), 0, o, me.across(o))
        self.push(self.x, self.mine(0, me.core), 2, 0, me.sibling())

    def relay(self, o):
        block = self.mine(o, self.me.core)
        remote(block, block, self.sems.at[0, o], self.sems.at[1, o], self.me.sibling()).wait_recv()
        self.push(block, block, 2, o, self.me.sibling())

    def arrive(self, o):
        block = self.mine(o, 1 - self.me.core)
        remote(block, block, self.sems.at[2, o], self.sems.at[3, o], self.me.sibling()).wait_recv()
        if o == 0:
            self.own.wait()

    def finish(self):
        for copy in self.sent:
            copy.wait_send()


def spread_sems(planes):
    return DMA((5, planes))


class Collect:
    def __init__(self, me, p_ref, scratch):
        self.me, self.p = me, p_ref
        self.from_core, self.sums, self.from_plane, self.total, self.from_z, self.cs, self.ps, self.zs = scratch

    def c_copy(self, o):
        me = self.me
        return remote(
            self.p.at[me.dp ^ o, :, 1 - me.core], self.from_core.at[o], self.cs.at[0, o], self.cs.at[1, o], me.sibling()
        )

    def p_copy(self, o):
        return remote(
            self.sums.at[o], self.from_plane.at[o], self.ps.at[0, o], self.ps.at[1, o], self.me.across(o)
        )

    def z_copy(self, k):
        me = self.me
        return remote(
            self.total.at[me.ahead(k)], self.from_z.at[k], self.zs.at[0, k], self.zs.at[1, k], me.along(me.ahead(k))
        )

    def first(self, o):
        self.c_copy(o).start()

    def second(self, o):
        me = self.me
        self.c_copy(o).wait_recv()
        own = self.p[me.dp ^ o, :, me.core].astype(F32)
        self.sums[o] = (own + self.from_core[o].astype(F32)).astype(self.sums.dtype)
        if o > 0:
            self.p_copy(o).start()

    def third(self):
        me = self.me
        for o in range(1, me.planes):
            self.p_copy(o).wait_recv()
        for k in list(range(1, me.depth)) + [0]:
            z = me.ahead(k)
            value = self.sums[0, z].astype(F32)
            for o in range(1, me.planes):
                value = value + self.from_plane[o, z].astype(F32)
            self.total[z] = value.astype(self.total.dtype)
            if k > 0:
                self.z_copy(k).start()
        return value

    def last(self, value):
        for k in range(1, self.me.depth):
            self.z_copy(k).wait_recv()
            value = value + self.from_z[k].astype(F32)
        return value

    def finish(self):
        for o in range(self.me.planes):
            self.c_copy(o).wait_send()
        for o in range(1, self.me.planes):
            self.p_copy(o).wait_send()
        for k in range(1, self.me.depth):
            self.z_copy(k).wait_send()


def collect_scratch(planes, depth, rows, columns, kind):
    return [
        pltpu.VMEM((planes, depth, rows, columns), kind),
        pltpu.VMEM((planes, depth, rows, columns), kind),
        pltpu.VMEM((planes, depth, rows, columns), kind),
        pltpu.VMEM((depth, rows, columns), kind),
        pltpu.VMEM((depth, rows, columns), kind),
        DMA((2, planes)),
        DMA((2, planes)),
        DMA((2, depth)),
    ]


COLLECT = 8


def unit_of(values, axis):
    recip = lax.rsqrt(jnp.mean(values * values, axis=axis, keepdims=True) + EPS)
    return values * recip, recip


def column_of(row, start):
    lane = lax.broadcasted_iota(jnp.int32, (HEAD_DIM, 128), 1)
    entry = lax.broadcasted_iota(jnp.int32, (HEAD_DIM, 128), 0)
    return jnp.sum(jnp.where(lane == entry + start, row, 0.0), axis=1, keepdims=True)


def turned(values, cosine, sine):
    half = HEAD_DIM // 2
    a, b = values[:half], values[half:]
    return jnp.concatenate([a * cosine - b * sine, b * cosine + a * sine], axis=0)


def front_kernel(
    planes, depth, n_gains, tok_ref, cos_ref, sin_ref, x_ref, gain_ref,
    q_out, kv_out, w_out, xat_out, unit_out, recip_out, gains_out,
    gains_g, xa, xa_plain, proj, wsem, gsem,
):
    me = Place(planes, depth)
    count = tok_ref.shape[0]
    half = D // planes
    gains = Spread(me, gain_ref, gains_g, gsem)
    weights = Spread(me, x_ref, w_out, wsem)
    gains.start()
    weights.start()
    greet(me.plane() + [me.sibling()])
    gains.first()
    weights.first()
    unit, _ = unit_of(tok_ref[...].astype(F32), 1)
    xa_plain[...] = unit
    for o in range(1, planes):
        gains.relay(o)
    for o in range(planes):
        gains.arrive(o)
    devices = planes * depth * 2
    table = gains_g[...].reshape(devices, 8, 128)[:, 0, :].astype(BF)
    entries = devices * n_gains
    index = lax.broadcasted_iota(jnp.int32, (128, entries), 1)
    pick = jnp.where(
        index % n_gains == lax.broadcasted_iota(jnp.int32, (128, entries), 0), 1.0, 0.0
    ).astype(BF)
    spread = dot(table, pick, NN)
    owner = lax.broadcasted_iota(jnp.int32, (devices, entries), 1) // n_gains
    device = lax.broadcasted_iota(jnp.int32, (devices, entries), 0)
    gains_row = 1.0 + jnp.sum(jnp.where(owner == device, spread, 0.0), axis=0, keepdims=True)
    gains_out[...] = gains_row
    normed = (xa_plain[...] * gains_row[:, :D]).astype(BF)
    xat_out[...] = normed.T
    for d in range(planes):
        xa[d] = normed[:, d * half : (d + 1) * half]
    proj[...] = jnp.zeros_like(proj)
    for o in [0] + list(range(1, planes)):
        if o > 0:
            weights.relay(o)
        weights.arrive(o)
        rows = w_out[me.dp ^ o].reshape(half, 2 * HQ)
        piece = xa[me.dp ^ o]
        proj[...] += dot(piece, rows, NN)
    tail_row = gains_row[:, 2 * D : 2 * D + 128]
    gain_q, gain_k = column_of(tail_row, 0), column_of(tail_row, HEAD_DIM)
    cosine, sine = cos_ref[...], sin_ref[...]
    for h in range(0, HEADS + KV_HEADS, 4):
        four = proj[:, h * HEAD_DIM : (h + 4) * HEAD_DIM].T
        results, recips = [], []
        for i in range(4):
            value, recip = unit_of(four[i * HEAD_DIM : (i + 1) * HEAD_DIM], 0)
            unit_out[pl.ds((h + i) * HEAD_DIM, HEAD_DIM), :] = value
            recips.append(recip)
            results.append(turned(value * (gain_q if h < HEADS else gain_k), cosine, sine))
        recip_out[h // 4] = jnp.concatenate(recips, axis=0)
        block = jnp.concatenate(results, axis=0)
        if h < HEADS:
            q_out[pl.ds(h * HEAD_DIM, 4 * HEAD_DIM), :] = (block * HEAD_DIM ** (-0.5)).astype(BF)
        else:
            kv_out[:, pl.ds((h - HEADS) * HEAD_DIM, 4 * HEAD_DIM)] = block.T.astype(BF)
    kv_out[:, pl.ds(HK, HK)] = proj[:, HQ + HK :].astype(BF)
    gains.finish()
    weights.finish()


def front(tokens, cosine, sine, x_line, gains_line, n_gains, planes, depth, collective_id):
    count = tokens.shape[0]
    rows, columns = x_line.shape[1:]
    return pl.pallas_call(
        functools.partial(front_kernel, planes, depth, n_gains),
        out_shape=(
            jax.ShapeDtypeStruct((HQ, count), BF),
            jax.ShapeDtypeStruct((count, 2 * HK), BF),
            jax.ShapeDtypeStruct((planes, depth, 2, rows, columns), BF),
            jax.ShapeDtypeStruct((D, count), BF),
            jax.ShapeDtypeStruct((HQ + HK, count), F32),
            jax.ShapeDtypeStruct(((HEADS + KV_HEADS) // 4, 4, count), F32),
            jax.ShapeDtypeStruct((1, planes * depth * 2 * n_gains), F32),
        ),
        in_specs=[VMEM] * 5,
        out_specs=(VMEM,) * 7,
        scratch_shapes=[
            pltpu.VMEM((planes, depth, 2, 8, 128), F32),
            pltpu.VMEM((planes, count, D // planes), BF),
            pltpu.VMEM((count, D), F32),
            pltpu.VMEM((count, 2 * HQ), F32),
            spread_sems(planes),
            spread_sems(planes),
        ],
        compiler_params=params(collective_id),
        cost_estimate=pl.CostEstimate(flops=40 << 30, bytes_accessed=8 << 20, transcendentals=0),
    )(tokens, cosine, sine, x_line, gains_line)


def fill_bias(bias, lower, slot):
    count = bias.shape[0]
    query = lax.broadcasted_iota(jnp.int32, (count, count), 1)
    key = lax.broadcasted_iota(jnp.int32, (count, count), 0) - slot * count
    bias[...] = jnp.where((key <= query) & (key >= lower), 0.0, NEG_BIG)


def attend_kernel(
    planes, depth, turns, kv_ref, og_ref, wo_ref, q_ref, lower_ref, tok_ref, gains_ref,
    kv_all, og_all, wo_all, o_out, lse_out, mixed_out, hn_out,
    bias, accum, sums, local, zs, cs, ps, wsem,
):
    me = Place(planes, depth)
    half = turns // 2
    count = kv_ref.shape[0]
    weights = Spread(me, wo_ref, wo_all, wsem)
    weights.start()
    own_kv = pltpu.make_async_copy(kv_ref, kv_all.at[0], local.at[0])
    own_kv.start()
    own_og = pltpu.make_async_copy(og_ref, og_all.at[0], local.at[1])
    own_og.start()
    greet(me.plane() + me.line() + [me.sibling()])

    def z_copy(k):
        return remote(kv_ref, kv_all.at[2 * k], zs.at[0, k], zs.at[1, k], me.along(me.ahead(k)))

    def c_copy(i):
        return remote(
            kv_all.at[2 * i + 2 * me.core], kv_all.at[2 * i + 1], cs.at[0, i], cs.at[1, i], me.sibling()
        )

    for k in range(1, half + 1):
        @pl.when(me.z + k < depth)
        def _():
            z_copy(k).start()

    own_kv.wait()

    @pl.when(me.core == 0)
    def _():
        c_copy(0).start()

    weights.first()
    shares = []
    for o in range(1, planes):
        share = remote(og_ref, og_all.at[o], ps.at[0, o], ps.at[1, o], me.across(o))
        share.start()
        shares.append(share)
    accum[...] = jnp.zeros_like(accum)
    sums[...] = jnp.zeros_like(sums)

    def visit(slot):
        fill_bias(bias, lower_ref[...], slot)

        def four_heads(t, carry):
            keys = kv_all[slot, :, pl.ds(pl.multiple_of(t * 128, 128), 128)]
            values = kv_all[slot, :, pl.ds(pl.multiple_of(HK + t * 128, 128), 128)]
            totals = []
            for u in range(2):
                key = keys[:, u * 64 : u * 64 + 64]
                value = values[:, u * 64 : u * 64 + 64]
                for g in range(2):
                    at = pl.ds(pl.multiple_of(t * 256 + u * 128 + g * 64, 64), 64)
                    weight = jnp.exp(dot(key, q_ref[at, :], NN) + bias[...])
                    totals.append(jnp.sum(weight, axis=0, keepdims=True))
                    accum[at, :] += dot(value, weight.astype(BF), TN)
            sums[t] += jnp.concatenate(totals, axis=0)
            return carry

        lax.fori_loop(0, GROUPS, four_heads, 0)

    visit(0)
    for k in range(1, half + 1):
        there = me.z - k >= 0

        @pl.when(there)
        def _():
            z_copy(k).wait_recv()

        @pl.when(there & (me.core == 1))
        def _():
            c_copy(k - 1).start()

        if k < half:
            @pl.when(there & (me.core == 0))
            def _():
                c_copy(k).start()

        @pl.when(there)
        def _():
            visit(2 * k)

        @pl.when(me.z - k < 0)
        def _():
            fill = pltpu.make_async_copy(kv_ref, kv_all.at[2 * k], local.at[2])
            fill.start()
            fill.wait()

    for i in range(half):
        @pl.when(me.z - i - 1 + me.core >= 0)
        def _():
            c_copy(i).wait_recv()
            visit(2 * i + 1)

        @pl.when(me.z - i - 1 + me.core < 0)
        def _():
            fill = pltpu.make_async_copy(kv_ref, kv_all.at[2 * i + 1], local.at[2])
            fill.start()
            fill.wait()

    for o in range(1, planes):
        weights.relay(o)
    for t in range(GROUPS):
        total = sums[t]
        lse_out[t] = jnp.log(total)
        for h in range(4):
            at = pl.ds(t * 256 + h * 64, 64)
            o_out[at, :] = (accum[at, :] / total[h : h + 1, :]).astype(BF)
    for o in range(planes):
        weights.arrive(o)
    mixed = tok_ref[...].astype(F32) + dot(o_out[...].T, wo_all[...].reshape(HQ, D), NN)
    mixed_out[...] = mixed
    unit, _ = unit_of(mixed, 1)
    hn_out[...] = (unit * gains_ref[:, D : 2 * D]).astype(BF)

    for i in range(half):
        @pl.when(me.z - i - me.core >= 0)
        def _():
            c_copy(i).wait_send()

    for k in range(1, half + 1):
        @pl.when(me.z + k < depth)
        def _():
            z_copy(k).wait_send()

    for share in shares:
        share.wait()
    weights.finish()
    own_og.wait()


def attend(kv, cotangent, wo_line, query, lower, tokens, gains_row, planes, depth, turns, collective_id):
    half = turns // 2
    count = kv.shape[0]
    rows, columns = wo_line.shape[1:]
    return pl.pallas_call(
        functools.partial(attend_kernel, planes, depth, turns),
        out_shape=(
            jax.ShapeDtypeStruct((turns + 1,) + kv.shape, BF),
            jax.ShapeDtypeStruct((planes,) + cotangent.shape, BF),
            jax.ShapeDtypeStruct((planes, depth, 2, rows, columns), BF),
            jax.ShapeDtypeStruct((HQ, count), BF),
            jax.ShapeDtypeStruct((GROUPS, 4, count), F32),
            jax.ShapeDtypeStruct((count, D), F32),
            jax.ShapeDtypeStruct((count, D), BF),
        ),
        in_specs=[VMEM] * 7,
        out_specs=(VMEM,) * 7,
        scratch_shapes=[
            pltpu.VMEM((count, count), F32),
            pltpu.VMEM((HQ, count), F32),
            pltpu.VMEM((GROUPS, 4, count), F32),
            DMA((3,)),
            DMA((2, half + 1)),
            DMA((2, half)),
            DMA((2, planes)),
            spread_sems(planes),
        ],
        compiler_params=params(collective_id),
        cost_estimate=pl.CostEstimate(flops=40 << 30, bytes_accessed=8 << 20, transcendentals=0),
    )(kv, cotangent, wo_line, query, lower, tokens, gains_row)


def ffn_kernel(
    planes, depth, hn_ref, og_ref, w_any, gn_out, parts_out, down_out, pair_out,
    w, hns, hnt, ogt, mid, pair, send_gn, recv_gn, own_gn, stage, wsem, hsem, gsem, osem,
):
    me = Place(planes, depth)
    count, width = hn_ref.shape
    full = w.shape[2]
    ctxs, dps, rows = w_any.shape[0], w_any.shape[1], w_any.shape[3]
    chunk = 384 if full % 384 == 0 else full

    def w_copy(i, m):
        c, d = i // dps, i % dps
        return pltpu.make_async_copy(
            w_any.at[c, d, m], w.at[m, pl.ds((d * ctxs + c) * rows, rows), :], wsem.at[m, i]
        )

    def load(i, carry):
        for m in range(3):
            w_copy(i, m).start()
        return carry

    lax.fori_loop(0, ctxs * dps, load, 0)
    greet(me.plane())

    def hn_copy(o):
        return remote(hn_ref, hns.at[o], hsem.at[0, o], hsem.at[1, o], me.across(o))

    def gn_copy(o):
        return remote(send_gn.at[o], recv_gn.at[o], gsem.at[0, o], gsem.at[1, o], me.across(o))

    for o in range(1, planes):
        hn_copy(o).start()
    hns[0] = hn_ref[...]

    def loaded(i, carry):
        for m in range(3):
            w_copy(i, m).wait()
        return carry

    lax.fori_loop(0, ctxs * dps, loaded, 0)

    def block(o, carry):
        @pl.when(o > 0)
        def _():
            hn_copy(o).wait_recv()

        hn = hns[o]
        og = og_ref[o]
        at = pl.ds(pl.multiple_of(o * count, 128), count)
        hnt[:, at] = hn.T
        ogt[:, at] = og.T
        own_gn[0] = jnp.zeros((count, width), F32)
        own_gn[1] = jnp.zeros((count, width), F32)

        def part(j, inner):
            cols = pl.ds(pl.multiple_of(j * chunk, 128), chunk)
            w_gate, w_up, w_down = w[0, :, cols], w[1, :, cols], w[2, :, cols]
            gate = dot(hn, w_gate, NN)
            upper = dot(hn, w_up, NN)
            sigma = 1.0 / (1.0 + jnp.exp(-gate))
            active = gate * sigma
            middle = (active * upper).astype(BF)
            gmid = dot(og, w_down, NN)
            ggate = (gmid * upper * sigma * (1.0 + gate * (1.0 - sigma))).astype(BF)
            gupper = (gmid * active).astype(BF)
            mid[at, cols] = middle
            pair[0, at, cols] = ggate
            pair[1, at, cols] = gupper
            own_gn[0] += dot(ggate, w_gate, NT) + dot(gupper, w_up, NT)
            own_gn[1] += dot(middle, w_down, NT)
            return inner

        lax.fori_loop(0, full // chunk, part, 0)
        parts_out[o] = own_gn[1].astype(BF)

        @pl.when(o > 0)
        def _():
            send_gn[o] = own_gn[0].astype(BF)
            gn_copy(o).start()

        @pl.when(o == 0)
        def _():
            gn_out[...] = own_gn[0]

        return carry

    lax.fori_loop(0, planes, block, 0)

    strip = ctxs * rows

    def out_copy(m, d):
        into = down_out.at[:, d] if m == 2 else pair_out.at[:, d, m]
        return pltpu.make_async_copy(stage.at[m], into, osem.at[m])

    def weight_grads(d, carry):
        left = pl.ds(pl.multiple_of(d * strip, 128), strip)
        for m in (2, 0, 1):
            @pl.when(d > 0)
            def _():
                out_copy(m, d - 1).wait()

            if m == 2:
                total = dot(ogt[left, :], mid[...], NN)
            else:
                total = dot(hnt[left, :], pair[m], NN)
            stage[m] = total.astype(BF).reshape(ctxs, rows, full)
            out_copy(m, d).start()
        return carry

    lax.fori_loop(0, dps, weight_grads, 0)
    for m in range(3):
        out_copy(m, dps - 1).wait()
    total = gn_out[...]
    for o in range(1, planes):
        gn_copy(o).wait_recv()
        total = total + recv_gn[o].astype(F32)
    gn_out[...] = total
    for o in range(1, planes):
        gn_copy(o).wait_send()
        hn_copy(o).wait_send()


def ffn(hn, og_all, w_all, planes, depth, collective_id):
    count, width = hn.shape
    ctxs, dps, _, rows, full = w_all.shape
    tokens = planes * count
    flops = 18 * tokens * width * full
    return pl.pallas_call(
        functools.partial(ffn_kernel, planes, depth),
        out_shape=(
            jax.ShapeDtypeStruct((count, width), F32),
            jax.ShapeDtypeStruct((planes, count, width), BF),
            jax.ShapeDtypeStruct((ctxs, dps, rows, full), BF),
            jax.ShapeDtypeStruct((ctxs, dps, 2, rows, full), BF),
        ),
        in_specs=[VMEM, VMEM, ANY],
        out_specs=(VMEM, VMEM, ANY, ANY),
        scratch_shapes=[
            pltpu.VMEM((3, width, full), BF),
            pltpu.VMEM((planes, count, width), BF),
            pltpu.VMEM((width, tokens), BF),
            pltpu.VMEM((width, tokens), BF),
            pltpu.VMEM((tokens, full), BF),
            pltpu.VMEM((2, tokens, full), BF),
            pltpu.VMEM((planes, count, width), BF),
            pltpu.VMEM((planes, count, width), BF),
            pltpu.VMEM((2, count, width), F32),
            pltpu.VMEM((3, ctxs, rows, full), BF),
            DMA((3, ctxs * dps)),
            DMA((2, planes)),
            DMA((2, planes)),
            DMA((3,)),
        ],
        compiler_params=params(collective_id),
        cost_estimate=pl.CostEstimate(flops=flops, bytes_accessed=20 << 20, transcendentals=0),
    )(hn, og_all, w_all)


def back_kernel(
    planes, depth, turns, gn_ref, mixed_ref, og_ref, gains_ref, wo_ref, o_ref, lse_ref, q_ref, kv_ref, lower_ref, parts_ref,
    gq_out, kv_out, gmixed_out, dgain_out, block_out, shard_out,
    bias, gob, delta, gkv, dsum, from_core, from_z, from_plane, partial, *rest,
):
    collect = Collect(Place(planes, depth), partial, rest[:COLLECT])
    cs, zs, ps = rest[COLLECT:]
    me = collect.me
    half = turns // 2
    count = gn_ref.shape[0]
    greet(me.plane() + me.line() + [me.sibling()])

    def c_copy(i):
        return remote(gkv.at[2 * i + 1], from_core.at[i], cs.at[0, i], cs.at[1, i], me.sibling())

    def z_copy(k):
        return remote(dsum.at[k], from_z.at[k], zs.at[0, k], zs.at[1, k], me.along(me.behind(k)))

    def p_copy(o):
        return remote(parts_ref.at[o], from_plane.at[o], ps.at[0, o], ps.at[1, o], me.across(o))

    unit, recip = unit_of(mixed_ref[...], 1)
    grad = gn_ref[...]
    scaled = grad * gains_ref[:, D : 2 * D]
    inner = jnp.mean(scaled * unit, axis=1, keepdims=True)
    gmixed = og_ref[...].astype(F32) + recip * (scaled - unit * inner)
    gmixed_out[...] = gmixed
    dgain_out[...] = jnp.sum(grad * unit, axis=0, keepdims=True)
    gmixed_b = gmixed.astype(BF)
    gob[...] = dot(wo_ref[...].reshape(HQ, D), gmixed_b, NT).astype(BF)
    for t in range(GROUPS):
        rows = []
        for h in range(4):
            at = pl.ds(t * 256 + h * 64, 64)
            rows.append(
                jnp.sum(gob[at, :].astype(F32) * o_ref[at, :].astype(F32), axis=0, keepdims=True)
            )
        delta[t] = jnp.concatenate(rows, axis=0)
    gq_out[...] = jnp.zeros_like(gq_out)

    def visit(slot):
        fill_bias(bias, lower_ref[...], slot)

        def four_heads(t, carry):
            key_at = pl.ds(pl.multiple_of(t * 128, 128), 128)
            value_at = pl.ds(pl.multiple_of(HK + t * 128, 128), 128)
            keys, values = kv_ref[slot, :, key_at], kv_ref[slot, :, value_at]
            lse_t, delta_t = lse_ref[t], delta[t]
            grad_keys, grad_values = [], []
            for u in range(2):
                key = keys[:, u * 64 : u * 64 + 64]
                value = values[:, u * 64 : u * 64 + 64]
                grad_key, grad_value = 0.0, 0.0
                for g in range(2):
                    h = 2 * u + g
                    at = pl.ds(pl.multiple_of(t * 256 + h * 64, 64), 64)
                    query, gob_h = q_ref[at, :], gob[at, :]
                    probs = jnp.exp(dot(key, query, NN) + bias[...] - lse_t[h : h + 1, :])
                    grad_value = grad_value + dot(probs.astype(BF), gob_h, NT)
                    grad_scores = (probs * (dot(value, gob_h, NN) - delta_t[h : h + 1, :])).astype(BF)
                    grad_key = grad_key + dot(grad_scores, query, NT)
                    gq_out[at, :] += dot(key, grad_scores, TN)
                grad_keys.append(grad_key)
                grad_values.append(grad_value)
            gkv[slot, :, key_at] = jnp.concatenate(grad_keys, axis=1).astype(BF)
            gkv[slot, :, value_at] = jnp.concatenate(grad_values, axis=1).astype(BF)
            return carry

        lax.fori_loop(0, GROUPS, four_heads, 0)

    for i in range(half - 1, -1, -1):
        @pl.when(me.z - i - 1 + me.core >= 0)
        def _():
            visit(2 * i + 1)
            c_copy(i).start()

    for k in range(half, 0, -1):
        @pl.when(me.z - k >= 0)
        def _():
            visit(2 * k)

            @pl.when(me.core == 0)
            def _():
                if k < half:
                    c_copy(k).wait_recv()
                    dsum[k] = (gkv[2 * k].astype(F32) + from_core[min(k, half - 1)].astype(F32)).astype(BF)
                else:
                    dsum[k] = gkv[2 * k]

            @pl.when(me.core == 1)
            def _():
                c_copy(k - 1).wait_recv()
                dsum[k] = (gkv[2 * k].astype(F32) + from_core[k - 1].astype(F32)).astype(BF)

            z_copy(k).start()

    visit(0)
    gq_out[...] *= HEAD_DIM ** (-0.5)
    half_rows = D // planes
    shape = partial.shape[1:]
    order = list(range(1, planes)) + [0]
    for o in order:
        d = me.dp ^ o
        rows = o_ref[pl.ds(pl.multiple_of(d * half_rows, 128), half_rows), :]
        partial[d] = dot(rows, gmixed_b, NN).astype(BF).reshape(shape)
        collect.first(o)
    for o in order:
        collect.second(o)
    for o in range(1, planes):
        p_copy(o).start()
    value = collect.third()
    shard_out[...] = collect.last(value)

    kv_out[...] = gkv[0].astype(F32)

    @pl.when(me.core == 0)
    def _():
        c_copy(0).wait_recv()
        kv_out[...] += from_core[0].astype(F32)

    for k in range(1, half + 1):
        @pl.when(me.z + k < depth)
        def _():
            z_copy(k).wait_recv()
            kv_out[...] += from_z[k].astype(F32)

    total = mixed_ref[...] + parts_ref[0].astype(F32)
    for o in range(1, planes):
        p_copy(o).wait_recv()
        total = total + from_plane[o].astype(F32)
    block_out[...] = total.astype(BF)

    for o in range(1, planes):
        p_copy(o).wait_send()
    for i in range(half):
        @pl.when(me.z - i - 1 + me.core >= 0)
        def _():
            c_copy(i).wait_send()
    for k in range(1, half + 1):
        @pl.when(me.z - k >= 0)
        def _():
            z_copy(k).wait_send()
    collect.finish()


def back(gn, mixed, cotangent, gains_row, wo_all, o_t, lse, query, kv_all, lower, parts, planes, depth, turns, collective_id):
    half = turns // 2
    count = gn.shape[0]
    rows = wo_all.shape[3]
    return pl.pallas_call(
        functools.partial(back_kernel, planes, depth, turns),
        out_shape=(
            jax.ShapeDtypeStruct((HQ, count), F32),
            jax.ShapeDtypeStruct((count, 2 * HK), F32),
            jax.ShapeDtypeStruct((count, D), F32),
            jax.ShapeDtypeStruct((1, D), F32),
            jax.ShapeDtypeStruct((count, D), BF),
            jax.ShapeDtypeStruct((rows, D), F32),
        ),
        in_specs=[VMEM] * 11,
        out_specs=(VMEM,) * 6,
        scratch_shapes=[
            pltpu.VMEM((count, count), F32),
            pltpu.VMEM((HQ, count), BF),
            pltpu.VMEM((GROUPS, 4, count), F32),
            pltpu.VMEM((turns + 1, count, 2 * HK), BF),
            pltpu.VMEM((half + 1, count, 2 * HK), BF),
            pltpu.VMEM((half, count, 2 * HK), BF),
            pltpu.VMEM((half + 1, count, 2 * HK), BF),
            pltpu.VMEM((planes, count, D), BF),
            pltpu.VMEM((planes, depth, 2, rows, D), BF),
        ]
        + collect_scratch(planes, depth, rows, D, BF)
        + [DMA((2, half)), DMA((2, half + 1)), DMA((2, planes))],
        compiler_params=params(collective_id),
        cost_estimate=pl.CostEstimate(flops=60 << 30, bytes_accessed=8 << 20, transcendentals=0),
    )(gn, mixed, cotangent, gains_row, wo_all, o_t, lse, query, kv_all, lower, parts)


def tail_kernel(
    planes, depth, n_gains, gq_ref, gkv_ref, unit_ref, recip_ref, cos_ref, sin_ref, gains_ref, w_ref, xat_ref, tok_ref, gmixed_ref, dgf_ref,
    grad_out, shard_out, gains_out, gproj, partial, gains_p, *rest,
):
    me = Place(planes, depth)
    collect = Collect(me, partial, rest[:COLLECT])
    small = Collect(me, gains_p, rest[COLLECT:])
    count = tok_ref.shape[0]
    tail_row = gains_ref[:, 2 * D : 2 * D + 128]
    gain_q, gain_k = column_of(tail_row, 0), column_of(tail_row, HEAD_DIM)
    cosine, sine = cos_ref[...], -sin_ref[...]
    gained = [0.0, 0.0]
    for h in range(0, HEADS + KV_HEADS, 4):
        kind = 0 if h < HEADS else 1
        if kind == 0:
            four = gq_ref[pl.ds(h * HEAD_DIM, 4 * HEAD_DIM), :]
        else:
            four = gkv_ref[:, pl.ds((h - HEADS) * HEAD_DIM, 4 * HEAD_DIM)].T
        recips = recip_ref[h // 4]
        results = []
        for i in range(4):
            unit = unit_ref[pl.ds((h + i) * HEAD_DIM, HEAD_DIM), :]
            grad = turned(four[i * HEAD_DIM : (i + 1) * HEAD_DIM], cosine, sine)
            scaled = grad * (gain_k if kind else gain_q)
            inner = jnp.mean(scaled * unit, axis=0, keepdims=True)
            results.append(recips[i : i + 1, :] * (scaled - unit * inner))
            gained[kind] = gained[kind] + grad * unit
        gproj[:, pl.ds(h * HEAD_DIM, 4 * HEAD_DIM)] = jnp.concatenate(results, axis=0).T.astype(BF)
    gproj[:, pl.ds(HQ + HK, HK)] = gkv_ref[:, pl.ds(HK, HK)].astype(BF)
    greet(me.plane() + me.line() + [me.sibling()])
    half_rows = D // planes
    shape = partial.shape[1:]
    order = list(range(1, planes)) + [0]
    for o in order:
        d = me.dp ^ o
        rows = xat_ref[pl.ds(pl.multiple_of(d * half_rows, 128), half_rows), :]
        partial[d] = dot(rows, gproj[...], NN).astype(BF).reshape(shape)
        collect.first(o)
        if o != order[0]:
            collect.second(order[order.index(o) - 1])
    collect.second(0)
    grad = dot(gproj[...], w_ref[...].reshape(D, 2 * HQ), NT)
    unit, recip = unit_of(tok_ref[...].astype(F32), 1)
    scaled = grad * gains_ref[:, :D]
    inner = jnp.mean(scaled * unit, axis=1, keepdims=True)
    grad_out[...] = gmixed_ref[...] + recip * (scaled - unit * inner)
    dga = jnp.sum(grad * unit, axis=0, keepdims=True)
    lane = lax.broadcasted_iota(jnp.int32, (HEAD_DIM, 128), 1)
    entry = lax.broadcasted_iota(jnp.int32, (HEAD_DIM, 128), 0)
    sums = [jnp.sum(g, axis=1, keepdims=True) for g in gained]
    last = jnp.sum(
        jnp.where(lane == entry, sums[0], 0.0) + jnp.where(lane == entry + HEAD_DIM, sums[1], 0.0),
        axis=0,
        keepdims=True,
    )
    whole = jnp.concatenate([dga, dgf_ref[...], last], axis=1)
    devices = planes * depth * 2
    entries = devices * n_gains
    index = lax.broadcasted_iota(jnp.int32, (devices, entries), 1)
    device = lax.broadcasted_iota(jnp.int32, (devices, entries), 0)
    apart = jnp.where(index // n_gains == device, whole, 0.0)
    pick = jnp.where(
        lax.broadcasted_iota(jnp.int32, (128, entries), 1) % n_gains
        == lax.broadcasted_iota(jnp.int32, (128, entries), 0),
        1.0,
        0.0,
    )
    table = lax.dot_general(
        apart, pick, NT, preferred_element_type=F32, precision=lax.Precision.HIGHEST
    )
    gains_p[...] = jnp.broadcast_to(table[:, None, :], (devices, 8, 128)).reshape(gains_p.shape)
    for o in order:
        small.first(o)
    for o in order:
        small.second(o)
    value = collect.third()
    little = small.third()
    shard_out[...] = collect.last(value)
    gains_out[...] = small.last(little)
    collect.finish()
    small.finish()


def tail(gq, gkv, unit, recip, cosine, sine, gains_row, w_all, xat, tokens, gmixed, dgf, n_gains, planes, depth, collective_id):
    count = tokens.shape[0]
    rows, columns = w_all.shape[3:]
    return pl.pallas_call(
        functools.partial(tail_kernel, planes, depth, n_gains),
        out_shape=(
            jax.ShapeDtypeStruct((count, D), F32),
            jax.ShapeDtypeStruct((rows, columns), F32),
            jax.ShapeDtypeStruct((8, 128), F32),
        ),
        in_specs=[VMEM] * 12,
        out_specs=(VMEM,) * 3,
        scratch_shapes=[
            pltpu.VMEM((count, columns), BF),
            pltpu.VMEM((planes, depth, 2, rows, columns), BF),
            pltpu.VMEM((planes, depth, 2, 8, 128), F32),
        ]
        + collect_scratch(planes, depth, rows, columns, BF)
        + collect_scratch(planes, depth, 8, 128, F32),
        compiler_params=params(collective_id),
        cost_estimate=pl.CostEstimate(flops=40 << 30, bytes_accessed=8 << 20, transcendentals=0),
    )(gq, gkv, unit, recip, cosine, sine, gains_row, w_all, xat, tokens, gmixed, dgf)


def per_device(
    tokens_in,
    positions,
    out_grad,
    w_qkv,
    w_output,
    w_gate_up,
    w_down,
    norm_gains,
    first_qkv,
    first_output,
    first_gate_up,
    first_down,
    first_gains,
    second_qkv,
    second_output,
    second_gate_up,
    second_down,
    second_gains,
):
    planes, ctxs = lax.axis_size("dp"), lax.axis_size("ctx")
    depth = ctxs // 2
    turns = ctxs // 2
    rows = w_qkv.shape[0]
    full = w_down.shape[1] // planes
    n_gains = norm_gains.shape[0]
    count = tokens_in.shape[0] * tokens_in.shape[1]
    tokens = tokens_in.reshape(count, D)
    places = positions.reshape(count)
    cotangent = out_grad.reshape(count, D)

    w_blocks = jnp.concatenate(
        [
            w_gate_up.astype(BF).reshape(rows, 2, planes, full).transpose(2, 1, 0, 3),
            w_down.astype(BF).reshape(rows, 1, planes, full).transpose(2, 1, 0, 3),
        ],
        axis=1,
    )
    gains_block = jnp.pad(norm_gains.astype(BF).astype(F32)[None, :], ((0, 7), (0, 128 - n_gains)))
    w_mine, qkv_line, output_line, gains_line = exchange(
        [w_blocks], [w_qkv.astype(BF), w_output.astype(BF), gains_block], planes, depth, 0
    )
    w_all = lax.all_gather(w_mine, "ctx", axis=0, tiled=False)

    cosine, sine = rope_tables(places)
    query, kv, qkv_all, xat, unit_heads, recip_heads, gains_row = front(
        tokens, cosine, sine, qkv_line, gains_line, n_gains, planes, depth, 1
    )
    lower = (jnp.arange(count, dtype=jnp.int32) - places)[None, :]
    kv_all, og_all, output_all, attn_t, lse, mixed, hn = attend(
        kv, cotangent, output_line, query, lower, tokens, gains_row, planes, depth, turns, 2
    )
    w_used = w_all if rows % 16 == 0 else w_all.transpose(2, 1, 0, 3, 4).reshape(1, 1, 3, D, full)
    grad_normed, parts, down_grads, pair_grads = ffn(hn, og_all, w_used, planes, depth, 3)
    if rows % 16 != 0:
        down_grads = down_grads.reshape(planes, ctxs, rows, full).transpose(1, 0, 2, 3)
        pair_grads = pair_grads.reshape(2, planes, ctxs, rows, full).transpose(2, 1, 0, 3, 4)
    down_mine = lax.psum_scatter(down_grads, "ctx", scatter_dimension=0, tiled=False)
    grad_query, grad_kv, grad_mixed, grad_gain_ffn, block_out, shard_output = back(
        grad_normed, mixed, cotangent, gains_row, output_all, attn_t, lse, query, kv_all, lower, parts,
        planes, depth, turns, 4,
    )
    pair_grads, grad_kv = lax.optimization_barrier((pair_grads, grad_kv))
    pair_mine = lax.psum_scatter(pair_grads, "ctx", scatter_dimension=0, tiled=False)
    input_grad, shard_qkv, gains_tile = tail(
        grad_query, grad_kv, unit_heads, recip_heads, cosine, sine, gains_row, qkv_all, xat, tokens, grad_mixed,
        grad_gain_ffn, n_gains, planes, depth, 5,
    )
    shard_gains = gains_tile[0, :n_gains]

    down_shards, pair_shards = exchange([down_mine, pair_mine], [], planes, depth, 6)
    shard_gate_up = pair_shards.transpose(2, 1, 0, 3).reshape(rows, 2 * planes * full).astype(F32)
    shard_down = down_shards.transpose(1, 0, 2).reshape(rows, planes * full).astype(F32)

    new_qkv, new_first_qkv, new_second_qkv = adam_step(
        w_qkv, shard_qkv, first_qkv, second_qkv, 0.02, 0.1
    )
    new_output, new_first_output, new_second_output = adam_step(
        w_output, shard_output, first_output, second_output, 0.2, 0.1
    )
    new_gate_up, new_first_gate_up, new_second_gate_up = adam_step(
        w_gate_up, shard_gate_up, first_gate_up, second_gate_up, 0.02, 0.1
    )
    new_down, new_first_down, new_second_down = adam_step(
        w_down, shard_down, first_down, second_down, 0.02, 0.1
    )
    new_gains, new_first_gains, new_second_gains = adam_step(
        norm_gains, shard_gains, first_gains, second_gains, 0.1, 0.0
    )
    return (
        block_out.reshape(tokens_in.shape),
        input_grad.reshape(tokens_in.shape),
        shard_qkv,
        shard_output,
        shard_gate_up,
        shard_down,
        shard_gains,
        new_qkv,
        new_output,
        new_gate_up,
        new_down,
        new_gains,
        new_first_qkv,
        new_first_output,
        new_first_gate_up,
        new_first_down,
        new_first_gains,
        new_second_qkv,
        new_second_output,
        new_second_gate_up,
        new_second_down,
        new_second_gains,
    )


def solution(mesh):
    in_specs = (
        P("dp", "ctx", None),
        P("dp", "ctx"),
        P("dp", "ctx", None),
        P(("dp", "ctx"), None),
        P(("dp", "ctx"), None),
        P(("dp", "ctx"), None),
        P(("dp", "ctx"), None),
        P(("dp", "ctx")),
        P(("dp", "ctx"), None),
        P(("dp", "ctx"), None),
        P(("dp", "ctx"), None),
        P(("dp", "ctx"), None),
        P(("dp", "ctx")),
        P(("dp", "ctx"), None),
        P(("dp", "ctx"), None),
        P(("dp", "ctx"), None),
        P(("dp", "ctx"), None),
        P(("dp", "ctx")),
    )
    out_specs = (
        P("dp", "ctx", None),
        P("dp", "ctx", None),
        P(("dp", "ctx"), None),
        P(("dp", "ctx"), None),
        P(("dp", "ctx"), None),
        P(("dp", "ctx"), None),
        P(("dp", "ctx")),
        P(("dp", "ctx"), None),
        P(("dp", "ctx"), None),
        P(("dp", "ctx"), None),
        P(("dp", "ctx"), None),
        P(("dp", "ctx")),
        P(("dp", "ctx"), None),
        P(("dp", "ctx"), None),
        P(("dp", "ctx"), None),
        P(("dp", "ctx"), None),
        P(("dp", "ctx")),
        P(("dp", "ctx"), None),
        P(("dp", "ctx"), None),
        P(("dp", "ctx"), None),
        P(("dp", "ctx"), None),
        P(("dp", "ctx")),
    )
    return jax.shard_map(
        per_device, mesh=mesh, in_specs=in_specs, out_specs=out_specs, check_vma=False
    )
```

time: 508 us -> 387 us (0.76); the launches traced: 501 us -> 387 us
  Pallas kernels: 391 us -> 346 us
  local copies, waits for them, and re-layouts: 45.6 us -> 8.96 us
  other arithmetic: 33.2 us -> 17.1 us
  matrix products: 15.1 us -> 0 us
    pallas_call x8 -> x6, Pallas kernels: 334 us -> 290 us  [the longest x1 106 us: back(): pl.pallas_call(functools.partial(back_kernel, planes, depth, turns), out_...]
    dot_general x6 -> x0, matrix products: 15.1 us -> none  [the longest x3 5.46 us: dot(): return lax.dot_general(a, b, dims, preferred_element_type=F32)]
    reshape x5 -> x0, local copies, waits for them, and re-layouts: 12.8 us -> none  [the longest x1 6.7 us: per_device(): grads.reshape(planes, 3, ctxs, rows, full)]
    mul x12 -> x0, local copies, waits for them, and re-layouts: 6.82 us -> none  [the longest x4 4.25 us: norm_forward(): unit = values * recip]
    reduce_sum x6 -> x0, other arithmetic: 6.23 us -> none  [the longest x3 5.89 us: norm_backward(): grad_gain = jnp.sum((grad * unit).reshape(-1, unit.shape[-1]), axis=0)]
  transfers between devices with their start and end apart: 2 -> 3, of which waited for: 0 -> 0; matrix products, arithmetic and copies ran while one was open for 14% -> 1% of each run, Pallas kernels for 61% -> 65%
where the time goes in v2:
time: 387 us
  Pallas kernels  346 us (89%)
  other arithmetic  17.1 us (4%)
  between operations  14.1 us (4%)
  local copies, waits for them, and re-layouts  8.96 us (2%)
    pallas_call x1, Pallas kernels, back(): pl.pallas_call(functools.partial(back_kernel, planes, depth, turns), out_...  106 us
    pallas_call x1, Pallas kernels, tail(): pl.pallas_call(functools.partial(tail_kernel, planes, depth, n_gains), ou...  59 us
    pallas_call x1, Pallas kernels, ffn(): pl.pallas_call(functools.partial(ffn_kernel, planes, depth), out_shape=(j...  55.9 us
    pallas_call x1, Pallas kernels, attend(): pl.pallas_call(functools.partial(attend_kernel, planes, depth, turns), ou...  54.3 us
    pallas_call x2, Pallas kernels, exchange(): pl.pallas_call(functools.partial(exchange_kernel, planes, depth, counts),...  38.7 us
    pallas_call x1, Pallas kernels, front(): pl.pallas_call(functools.partial(front_kernel, planes, depth, n_gains), o...  32.3 us
    sub x5, other arithmetic, adam_step(): weight - rate * (first_hat / (jnp.sqrt(second_hat) + ADAM_EPS) + decay *...  7.82 us
  transfers between devices with their start and end apart: 3, of which 0 were waited for; matrix products, arithmetic and copies ran while one was open for 1% of the time, Pallas kernels for 65%

profile of v2, /device:TPU:0, one launch (start us, length us, event | category | flops | bytes accessed | tf_op | source)
XLA Modules:
  0.0 386.7 jit_solution(957088378331540629)
XLA Ops:
  7.2 0.0 all-gather.3.cloned.1.call-start
  7.2 0.7 convert_bitcast_fusion.2
  7.9 0.6 pad_convert_fusion.refs_3_
  8.5 1.5 convert_element_type.44.refs_2_
  10.0 1.7 convert_element_type.43.refs_1_
  11.8 1.1 convert_element_type.42
  12.9 0.1 reshape.77
  13.0 0.1 convert_element_type.41
  13.1 0.5 reshape.76
  13.5 0.1 copy.51
  13.6 1.0 pad_maximum_fusion.refs_0_
  14.6 24.8 %shard_map.345 = (bf16[4,3,32,1152]{3,2,1,0:T(8,128)(2,1)}, bf16[4,32,2048]{2,1,0:T(8,128)(2,1)}, bf16[4,32,1024]{2,1,0:T(8,128)(2,1)}, f32[4,8,128]{2,1,0:T(8,128)}) custom-call(bf16[4,3,32,1152]{3,2,1,0:T(8,128)(2,1)} %pad_maximum_fusion.refs_0_, bf16[32,2048]{1,0:T(8,128)(2,1)} %convert_element_type.43.refs_1_, ...), custom_call_target="tpu_custom_call" | custom-call | tf_op jit(solution)/shard_map/pallas_call | solution.py:150
  39.4 0.0 all-gather.3.cloned.1.call-update
  39.4 0.0 reduce-scatter.3.cloned.1.call-start
  39.5 0.6 iota_subtract_fusion
  40.0 0.8 multiply_sine_fusion
  40.9 32.3 %shard_map.346 = (bf16[1024,256]{1,0:T(8,128)(2,1)}, bf16[256,1024]{1,0:T(8,128)(2,1)}, bf16[4,4,2,32,2048]{4,3,2,1,0:T(8,128)(2,1)}, bf16[1024,256]{1,0:T(8,128...) custom-call(bf16[256,1024]{1,0:T(8,128)(2,1)} %bitcast.37, ...), custom_call_target="tpu_custom_call" | custom-call | flops 42949672960 | bytes 8388608 | tf_op jit(solution)/shard_map/pallas_call | solution.py:369
  73.2 54.3 %shard_map.347 = (bf16[5,256,1024]{2,1,0:T(8,128)(2,1)}, bf16[4,256,1024]{2,1,0:T(8,128)(2,1)}, bf16[4,4,2,32,1024]{4,3,2,1,0:T(8,128)(2,1)}, bf16[1024,256]{1,0...) custom-call(bf16[256,1024]{1,0:T(8,128)(2,1)} %get-tuple-element.59.kv_ref, ...), custom_call_target="tpu_custom_call" | custom-call | flops 42949672960 | bytes 8388608 | tf_op jit(solution)/shard_map/pallas_call | solution.py:540
  127.5 0.0 all-gather.3.cloned.1.call-done
  127.5 55.9 %shard_map.348 = (f32[256,1024]{1,0:T(8,128)}, bf16[4,256,1024]{2,1,0:T(8,128)(2,1)}, bf16[8,4,32,1152]{3,2,1,0:T(8,128)(2,1)}, bf16[8,4,2,32,1152]{4,3,2,1,0:T(8,128)(2,1)}) custom-call(bf16[256,1024]{1,0:T(8,128)(2,1)} %get-tuple-element.63.hn_ref, bf16[4,256,1024]{2,1,0:T(8,128)(2,1)} %get-tuple-element.64.og_ref, bf16[8,4,3,32,1152]{4,3,2,1,0:T(8,128)(2,1)} %bitcast.34), custom_call_target="tpu_custom_call" | custom-call | flops 21743271936 | bytes 20971520 | tf_op jit(solution)/shard_map/pallas_call | solution.py:695
  183.4 0.0 reduce-scatter.3.cloned.1.call-update
  183.4 0.0 reduce-scatter.5.cloned.1.call-start
  183.5 106.2 %shard_map.349 = (f32[1024,256]{1,0:T(8,128)}, f32[256,1024]{1,0:T(8,128)}, f32[256,1024]{1,0:T(8,128)}, f32[1,1024]{1,0:T(1,128)}, bf16[256,1024]{1,0:T(8,128)(2,1)}, /*index=5*/f32[32,1024]{1,0:T(8,128)}) custom-call(f32[256,1024]{1,0:T(8,128)} %get-tuple-element.66.gn_ref, f32[256,1024]{1,0:T(8,128)} %get-tuple-element.67.mixed_ref, ...), custom_call_target="tpu_custom_call" | custom-call | flops 64424509440 | bytes 8388608 | tf_op jit(solution)/shard_map/pallas_call | solution.py:875
  289.7 0.0 reduce-scatter.5.cloned.1.call-update
  289.8 59.0 %shard_map.350 = (f32[256,1024]{1,0:T(8,128)}, f32[32,2048]{1,0:T(8,128)}, f32[8,128]{1,0:T(8,128)}) custom-call(f32[1024,256]{1,0:T(8,128)} %get-tuple-element.74.gq_ref, f32[256,1024]{1,0:T(8,128)} %get-tuple-element.77.gkv_ref, f32[1536,256]{1,0:T(8,128)} %get-tuple-element.78.unit_ref, f32[6,4,256]{2,1,0:T(4,128)} %get-tuple-element.79.recip_ref, ...), custom_call_target="tpu_custom_call" | custom-call | flops 42949672960 | bytes 8388608 | tf_op jit(solution)/shard_map/pallas_call | solution.py:991
  348.8 1.2 multiply_subtract_fusion.4
  350.1 0.8 multiply_subtract_fusion.3
  350.9 1.9 multiply_subtract_fusion.2
  352.8 13.9 %shard_map.351 = (bf16[4,32,1152]{2,1,0:T(8,128)(2,1)}, bf16[4,2,32,1152]{3,2,1,0:T(8,128)(2,1)}) custom-call(bf16[4,32,1152]{2,1,0:T(8,128)(2,1)} %bitcast.32, bf16[4,2,32,1152]{3,2,1,0:T(8,128)(2,1)} %bitcast.30), custom_call_target="tpu_custom_call" | custom-call | tf_op jit(solution)/shard_map/pallas_call | solution.py:150
  366.7 1.1 convert_bitcast_fusion
  367.9 0.8 copy.46
  368.7 0.5 reshape.81
  369.2 0.0 copy-start.2
  369.3 0.4 copy-done.15
  369.7 1.0 copy-done.3
  370.7 0.4 copy-done.10
  371.1 0.2 copy-done.11
  371.3 1.5 multiply_subtract_fusion.1
  372.8 0.1 copy-done.1
  372.9 0.7 copy-done.5
  373.6 0.4 copy-done.6
  373.9 2.3 multiply_subtract_fusion
  376.3 0.8 copy.57
  377.1 0.6 copy-done.9
  377.7 1.0 copy.58
  378.7 0.1 copy-done.8
  378.8 0.7 copy.59
  379.5 0.7 copy.60
  (44 shorter events, 0.2 us)
Async XLA Ops:
  7.2 120.3 %all-gather.3.cloned.1.call-start = ((), (), s32[]{:S(2)}) async-start(), calls=%async_computation.4 | async-start | bytes 7962624 | tf_op jit(solution)/shard_map/all_gather | solution.py:1054
  10.0 2.9 copy-start
  14.6 24.9 %copy-start.20 = (s32[1,256]{1,0:T(1,128)S(1)}, s32[1,256]{1,0:T(1,128)}, u32[]{:S(2)}) copy-start(s32[1,256]{1,0:T(1,128)} %param.19) | copy-start | bytes 3076
  39.4 313.4 %reduce-scatter.3.cloned.1.call-start = ((), (), s32[]{:S(2)}) async-start(), calls=%async_computation.2 | async-start | bytes 2654208 | tf_op jit(solution)/shard_map/reduce_scatter | solution.py:1069
  183.4 169.4 %reduce-scatter.5.cloned.1.call-start = ((), (), s32[]{:S(2)}) async-start(), calls=%async_computation.3 | async-start | bytes 5308416 | tf_op jit(solution)/shard_map/reduce_scatter | solution.py:1075
  289.7 59.1 %copy-start.21 = (f32[68]{0:T(128)S(1)}, f32[68]{0:T(128)}, u32[]{:S(2)}) copy-start(f32[68]{0:T(128)} %param.25) | copy-start | bytes 820
  289.7 59.1 %copy-start.22 = (f32[68]{0:T(128)S(1)}, f32[68]{0:T(128)}, u32[]{:S(2)}) copy-start(f32[68]{0:T(128)} %param.30) | copy-start | bytes 820
  289.7 59.1 %copy-start.23 = (f32[68]{0:T(128)S(1)}, f32[68]{0:T(128)}, u32[]{:S(2)}) copy-start(f32[68]{0:T(128)} %param.35) | copy-start | bytes 820
  289.7 60.3 %copy-start.12 = (f32[32,1024]{1,0:T(8,128)S(1)}, f32[32,1024]{1,0:T(8,128)}, u32[]{:S(2)}) copy-start(f32[32,1024]{1,0:T(8,128)} %param.22) | copy-start | bytes 393220
  289.8 60.3 %copy-start.13 = (f32[32,1024]{1,0:T(8,128)S(1)}, f32[32,1024]{1,0:T(8,128)}, u32[]{:S(2)}) copy-start(f32[32,1024]{1,0:T(8,128)} %get-tuple-element.137) | copy-start | bytes 393220
  289.8 60.3 %copy-start.18 = (f32[32,1024]{1,0:T(8,128)S(1)}, f32[32,1024]{1,0:T(8,128)}, u32[]{:S(2)}) copy-start(f32[32,1024]{1,0:T(8,128)} %param.27) | copy-start | bytes 393220
  289.8 60.3 %copy-start.19 = (f32[32,1024]{1,0:T(8,128)S(1)}, f32[32,1024]{1,0:T(8,128)}, u32[]{:S(2)}) copy-start(f32[32,1024]{1,0:T(8,128)} %param.32) | copy-start | bytes 393220
  289.8 61.1 %copy-start.7 = (f32[32,2048]{1,0:T(8,128)S(1)}, f32[32,2048]{1,0:T(8,128)}, u32[]{:S(2)}) copy-start(f32[32,2048]{1,0:T(8,128)} %param.21) | copy-start | bytes 786436
  289.8 61.1 %copy-start.16 = (f32[32,2048]{1,0:T(8,128)S(1)}, f32[32,2048]{1,0:T(8,128)}, u32[]{:S(2)}) copy-start(f32[32,2048]{1,0:T(8,128)} %param.26) | copy-start | bytes 786436
  289.8 61.1 %copy-start.17 = (f32[32,2048]{1,0:T(8,128)S(1)}, f32[32,2048]{1,0:T(8,128)}, u32[]{:S(2)}) copy-start(f32[32,2048]{1,0:T(8,128)} %param.31) | copy-start | bytes 786436
  368.7 1.0 copy-start.15
  369.2 3.6 copy-start.2
  369.2 1.5 copy-start.3
  369.2 1.9 copy-start.10
  369.2 2.1 copy-start.11
  369.7 3.1 copy-start.4
  371.3 1.6 copy-start.1
  371.3 2.3 copy-start.5
  371.3 2.6 copy-start.6
  373.9 2.4 copy-start.14
  376.3 1.4 copy-start.9
  377.7 1.1 copy-start.8
Sparse Core Ops, SparseCore 0:
  39.5 87.4 all-gather.2
  183.6 74.3 reduce-scatter.2
  289.8 62.4 reduce-scatter.4

commit v3 on v2

v3 whole, which is shorter than its diff:
```python
import functools
import math

import jax
import jax.numpy as jnp
from jax import lax
from jax.experimental import pallas as pl
from jax.experimental.pallas import tpu as pltpu
from jax.sharding import PartitionSpec as P

D = 1024
HEADS = 16
KV_HEADS = 8
HEAD_DIM = 64
STEP = 4
HQ = 1024
HK = 512


EPS = 1e-05
THETA = 1000000.0
NEG_BIG = -1e30
BETA_ONE = 0.9
BETA_TWO = 0.95
ADAM_EPS = 1e-08


def rope_tables(places):
    half = HEAD_DIM // 2
    freqs = jnp.exp(-math.log(THETA) * (2.0 * jnp.arange(half, dtype=jnp.float32) / HEAD_DIM))
    angles = freqs[:, None] * places.astype(jnp.float32)[None, :]
    return (jnp.cos(angles), jnp.sin(angles))


def adam_step(weight, grad, first, second, rate, decay):
    first_new = BETA_ONE * first + (1.0 - BETA_ONE) * grad
    second_new = BETA_TWO * second + (1.0 - BETA_TWO) * grad * grad
    first_hat = first_new / (1.0 - BETA_ONE**STEP)
    second_hat = second_new / (1.0 - BETA_TWO**STEP)
    weight_new = weight - rate * (first_hat / (jnp.sqrt(second_hat) + ADAM_EPS) + decay * weight)
    return (weight_new, first_new, second_new)


BF = jnp.bfloat16
F32 = jnp.float32
MESH_ID = pl.DeviceIdType.MESH
ANY = pl.BlockSpec(memory_space=pl.ANY)
VMEM = pl.BlockSpec(memory_space=pltpu.VMEM)
DMA = pltpu.SemaphoreType.DMA
NN = (((1,), (0,)), ((), ()))
NT = (((1,), (1,)), ((), ()))
TN = (((0,), (0,)), ((), ()))
VMEM_BYTES = 60 << 20
GROUPS = HEADS // 4


def dot(a, b, dims):
    return lax.dot_general(a, b, dims, preferred_element_type=F32)


class Place:
    def __init__(self, planes, depth):
        self.planes, self.depth = planes, depth
        self.dp = lax.axis_index("dp")
        self.ctx = lax.axis_index("ctx")
        self.z = self.ctx // 2
        self.core = self.ctx % 2

    def sibling(self):
        return {"dp": self.dp, "ctx": self.z * 2 + 1 - self.core}

    def across(self, o):
        return {"dp": self.dp ^ o, "ctx": self.ctx}

    def behind(self, k):
        return lax.rem(self.z + self.depth - k, self.depth)

    def ahead(self, k):
        return lax.rem(self.z + k, self.depth)

    def along(self, z):
        return {"dp": self.dp, "ctx": z * 2 + self.core}

    def plane(self):
        return [self.across(o) for o in range(1, self.planes)]

    def line(self):
        return [self.along(self.ahead(k)) for k in range(1, self.depth)]


def greet(devices):
    barrier = pltpu.get_barrier_semaphore()
    for device in devices:
        pl.semaphore_signal(barrier, inc=1, device_id=device, device_id_type=MESH_ID)
    pl.semaphore_wait(barrier, len(devices))


def remote(src, dst, send, recv, device):
    return pltpu.make_async_remote_copy(
        src_ref=src, dst_ref=dst, send_sem=send, recv_sem=recv, device_id=device, device_id_type=MESH_ID
    )


def params(collective_id):
    return pltpu.CompilerParams(
        vmem_limit_bytes=VMEM_BYTES, collective_id=collective_id, has_side_effects=True
    )


class Spread:
    def __init__(self, me, g_ref, line_sems, sems):
        self.me, self.g, self.line_sems, self.sems = me, g_ref, line_sems, sems
        self.sent = []

    def push(self, src, dst, kind, o, device):
        copy = remote(src, dst, self.sems.at[kind, o], self.sems.at[kind + 1, o], device)
        copy.start()
        self.sent.append(copy)

    def mine(self, o, core):
        return self.g.at[self.me.dp ^ o, :, core]

    def line(self):
        me = self.me
        block = self.g.at[me.dp, me.z, me.core]
        for k in range(1, me.depth):
            copy = remote(
                block, block, self.line_sems.at[0, k], self.line_sems.at[1, k], me.along(me.ahead(k))
            )
            copy.start()
            self.sent.append(copy)

    def first(self):
        me = self.me
        for k in range(1, me.depth):
            block = self.g.at[me.dp, me.behind(k), me.core]
            remote(
                block, block, self.line_sems.at[0, k], self.line_sems.at[1, k], me.along(me.ahead(k))
            ).wait_recv()
        for o in range(1, me.planes):
            self.push(self.mine(0, me.core), self.mine(0, me.core), 0, o, me.across(o))
        self.push(self.mine(0, me.core), self.mine(0, me.core), 2, 0, me.sibling())

    def relay(self, o):
        block = self.mine(o, self.me.core)
        remote(block, block, self.sems.at[0, o], self.sems.at[1, o], self.me.sibling()).wait_recv()
        self.push(block, block, 2, o, self.me.sibling())

    def arrive(self, o):
        block = self.mine(o, 1 - self.me.core)
        remote(block, block, self.sems.at[2, o], self.sems.at[3, o], self.me.sibling()).wait_recv()

    def finish(self):
        for copy in self.sent:
            copy.wait_send()


def spread_sems(planes, depth):
    return [DMA((2, depth)), DMA((4, planes))]


class Collect:
    def __init__(self, me, p_ref, scratch):
        self.me, self.p = me, p_ref
        self.sums, self.from_plane, self.total, self.from_z, self.cs, self.ps, self.zs = scratch

    def c_copy(self, o):
        me = self.me
        return remote(
            self.p.at[me.dp ^ o, :, 1 - me.core], self.sums.at[o], self.cs.at[0, o], self.cs.at[1, o], me.sibling()
        )

    def p_copy(self, o):
        return remote(
            self.sums.at[o], self.from_plane.at[o - 1], self.ps.at[0, o], self.ps.at[1, o], self.me.across(o)
        )

    def z_copy(self, k):
        me = self.me
        return remote(
            self.total.at[me.ahead(k)], self.from_z.at[k], self.zs.at[0, k], self.zs.at[1, k], me.along(me.ahead(k))
        )

    def first(self, o):
        self.c_copy(o).start()

    def second(self, o):
        me = self.me
        self.c_copy(o).wait_recv()
        own = self.p[me.dp ^ o, :, me.core].astype(F32)
        self.sums[o] = (own + self.sums[o].astype(F32)).astype(self.sums.dtype)
        if o > 0:
            self.p_copy(o).start()

    def third(self):
        me = self.me
        for o in range(1, me.planes):
            self.p_copy(o).wait_recv()
        for k in list(range(1, me.depth)) + [0]:
            z = me.ahead(k)
            value = self.sums[0, z].astype(F32)
            for o in range(1, me.planes):
                value = value + self.from_plane[o - 1, z].astype(F32)
            self.total[z] = value.astype(self.total.dtype)
            if k > 0:
                self.z_copy(k).start()
        return value

    def last(self, value):
        for k in range(1, self.me.depth):
            self.z_copy(k).wait_recv()
            value = value + self.from_z[k].astype(F32)
        return value

    def finish(self):
        for o in range(self.me.planes):
            self.c_copy(o).wait_send()
        for o in range(1, self.me.planes):
            self.p_copy(o).wait_send()
        for k in range(1, self.me.depth):
            self.z_copy(k).wait_send()


def collect_scratch(planes, depth, rows, columns, kind):
    return [
        pltpu.VMEM((planes, depth, rows, columns), kind),
        pltpu.VMEM((planes - 1, depth, rows, columns), kind),
        pltpu.VMEM((depth, rows, columns), kind),
        pltpu.VMEM((depth, rows, columns), kind),
        DMA((2, planes)),
        DMA((2, planes)),
        DMA((2, depth)),
    ]


COLLECT = 7


def unit_of(values, axis):
    recip = lax.rsqrt(jnp.mean(values * values, axis=axis, keepdims=True) + EPS)
    return values * recip, recip


def column_of(row, start):
    lane = lax.broadcasted_iota(jnp.int32, (HEAD_DIM, 128), 1)
    entry = lax.broadcasted_iota(jnp.int32, (HEAD_DIM, 128), 0)
    return jnp.sum(jnp.where(lane == entry + start, row, 0.0), axis=1, keepdims=True)


def turned(values, cosine, sine):
    half = HEAD_DIM // 2
    a, b = values[:half], values[half:]
    return jnp.concatenate([a * cosine - b * sine, b * cosine + a * sine], axis=0)


def fill_bias(bias, lower, slot):
    count = bias.shape[0]
    query = lax.broadcasted_iota(jnp.int32, (count, count), 1)
    key = lax.broadcasted_iota(jnp.int32, (count, count), 0) - slot * count
    bias[...] = jnp.where((key <= query) & (key >= lower), 0.0, NEG_BIG)


class Pass:
    def __init__(self, me, w_ref, sems):
        self.me, self.w, self.sems = me, w_ref, sems

    def copy(self, kind, s, down, core=None, device=None):
        me = self.me
        z = me.z + s - 1 if down else me.z - s + 1
        block = self.w.at[z * 2 + (me.core if core is None else core)]
        device = me.sibling() if device is None else device
        return remote(block, block, self.sems.at[kind, s], self.sems.at[kind + 1, s], device)

    def held(self, s, down):
        me = self.me
        return me.z + s - 1 < me.depth if down else me.z - s + 1 >= 0

    def on(self, s, down):
        me = self.me
        return self.held(s, down) & (me.z >= 1 if down else me.z + 1 < me.depth)

    def line_copy(self, s, down):
        me = self.me
        return self.copy(2 if down else 0, s, down, None, me.along(me.z - 1 if down else me.z + 1))

    def step(self, s):
        for down in (False, True):
            if s > 1:
                @pl.when(self.held(s, down))
                def _():
                    me = self.me
                    z = me.z + s - 1 if down else me.z - s + 1
                    block = self.w.at[z * 2 + me.core]
                    kind = 2 if down else 0
                    remote(
                        block, block, self.sems.at[kind, s - 1], self.sems.at[kind + 1, s - 1], me.sibling()
                    ).wait_recv()

            @pl.when(self.on(s, down))
            def _():
                self.line_copy(s, down).start()

            if s > 1 or not down:
                @pl.when(self.held(s, down))
                def _():
                    self.copy(6 if down else 4, s, down).start()

    def finish(self):
        for s in range(1, self.me.depth + 1):
            for down in (False, True):
                @pl.when(self.on(s, down))
                def _():
                    self.line_copy(s, down).wait_send()

                if s > 1 or not down:
                    @pl.when(self.held(s, down))
                    def _():
                        self.copy(6 if down else 4, s, down).wait_send()
                        self.copy(6 if down else 4, s, down, 1 - self.me.core).wait_recv()


def ahead_kernel(
    planes, depth, turns, n_gains,
    tok_ref, cos_ref, sin_ref, lower_ref, gain_ref, wqkv_ref, wout_ref, wpair_ref, wdown_ref, og_ref,
    q_any, kv_any, wqkv_any, xat_any, unit_any, recip_any, og_all, wo_any, w_any,
    gains_out, o_out, lse_out, mixed_out, hn_out,
    q_s, kv_all, w_all, xat, unit_s, recip_s, wo_all, blocks, gains_g, xa, xa_plain, proj, bias, accum, sums,
    own_sem, keep_sem, zs, cs, ps, a2a, pass_sem, glsem, gsem, wlsem, wsem, olsem, osem,
):
    me = Place(planes, depth)
    half = turns // 2
    count = tok_ref.shape[0]
    width = D // planes
    rows = wqkv_ref.shape[0]
    full = blocks.shape[3]
    gains = Spread(me, gains_g, glsem, gsem)
    weights = Spread(me, w_all, wlsem, wsem)
    outputs = Spread(me, wo_all, olsem, osem)
    passing = Pass(me, w_any, pass_sem)
    kept = []

    def keep(source, into):
        copy = pltpu.make_async_copy(source, into, keep_sem.at[len(kept)])
        copy.start()
        kept.append(copy)

    gains_g[me.dp, me.z, me.core] = gain_ref[...]
    w_all[me.dp, me.z, me.core] = wqkv_ref[...].astype(BF)
    wo_all[me.dp, me.z, me.core] = wout_ref[...].astype(BF)
    for d in range(planes):
        for m in range(2):
            blocks[d, m] = wpair_ref[:, (m * planes + d) * full : (m * planes + d + 1) * full].astype(BF)
        blocks[d, 2] = wdown_ref[:, d * full : (d + 1) * full].astype(BF)
    own_block = pltpu.make_async_copy(blocks.at[me.dp], w_any.at[me.ctx, me.dp], own_sem.at[0])
    own_block.start()
    own_og = pltpu.make_async_copy(og_ref, og_all.at[0], own_sem.at[1])
    own_og.start()
    greet(me.plane() + me.line() + [me.sibling()])
    gains.line()
    weights.line()

    def a2a_copy(o):
        return remote(
            blocks.at[me.dp ^ o], w_any.at[me.ctx, me.dp], a2a.at[0, o], a2a.at[1, o], me.across(o)
        )

    for o in range(1, planes):
        a2a_copy(o).start()
    outputs.line()
    unit, _ = unit_of(tok_ref[...].astype(F32), 1)
    xa_plain[...] = unit
    gains.first()
    weights.first()
    own_block.wait()
    for o in range(1, planes):
        block = w_any.at[me.ctx, me.dp ^ o]
        remote(block, block, a2a.at[0, o], a2a.at[1, o], me.across(o)).wait_recv()
    passing.step(1)
    for o in range(1, planes):
        gains.relay(o)
    for o in range(planes):
        gains.arrive(o)
    devices = planes * depth * 2
    table = gains_g[...].reshape(devices, 8, 128)[:, 0, :].astype(BF)
    entries = devices * n_gains
    index = lax.broadcasted_iota(jnp.int32, (128, entries), 1)
    pick = jnp.where(
        index % n_gains == lax.broadcasted_iota(jnp.int32, (128, entries), 0), 1.0, 0.0
    ).astype(BF)
    spread = dot(table, pick, NN)
    owner = lax.broadcasted_iota(jnp.int32, (devices, entries), 1) // n_gains
    device = lax.broadcasted_iota(jnp.int32, (devices, entries), 0)
    gains_row = 1.0 + jnp.sum(jnp.where(owner == device, spread, 0.0), axis=0, keepdims=True)
    gains_out[...] = gains_row
    normed = (xa_plain[...] * gains_row[:, :D]).astype(BF)
    xat[...] = normed.T
    keep(xat, xat_any)
    for d in range(planes):
        xa[d] = normed[:, d * width : (d + 1) * width]
    proj[...] = jnp.zeros_like(proj)
    for o in range(planes):
        if o > 0:
            weights.relay(o)
        weights.arrive(o)
        proj[...] += dot(xa[me.dp ^ o], w_all[me.dp ^ o].reshape(width, 2 * HQ), NN)
    tail_row = gains_row[:, 2 * D : 2 * D + 128]
    gain_q, gain_k = column_of(tail_row, 0), column_of(tail_row, HEAD_DIM)
    cosine, sine = cos_ref[...], sin_ref[...]

    def four_raw(h):
        four = proj[:, h * HEAD_DIM : (h + 4) * HEAD_DIM].T
        results, recips = [], []
        for i in range(4):
            value, recip = unit_of(four[i * HEAD_DIM : (i + 1) * HEAD_DIM], 0)
            unit_s[pl.ds((h + i) * HEAD_DIM, HEAD_DIM), :] = value
            recips.append(recip)
            results.append(turned(value * (gain_q if h < HEADS else gain_k), cosine, sine))
        recip_s[h // 4] = jnp.concatenate(recips, axis=0)
        return jnp.concatenate(results, axis=0)

    for h in range(HEADS, HEADS + KV_HEADS, 4):
        kv_all[0, :, pl.ds((h - HEADS) * HEAD_DIM, 4 * HEAD_DIM)] = four_raw(h).T.astype(BF)
    kv_all[0, :, pl.ds(HK, HK)] = proj[:, HQ + HK :].astype(BF)

    def z_copy(k):
        return remote(kv_all.at[0], kv_all.at[2 * k], zs.at[0, k], zs.at[1, k], me.along(me.ahead(k)))

    def c_copy(i):
        return remote(
            kv_all.at[2 * i + 2 * me.core], kv_all.at[2 * i + 1], cs.at[0, i], cs.at[1, i], me.sibling()
        )

    for k in range(1, half + 1):
        @pl.when(me.z + k < depth)
        def _():
            z_copy(k).start()

    @pl.when(me.core == 0)
    def _():
        c_copy(0).start()

    outputs.first()
    passing.step(2)
    for h in range(0, HEADS, 4):
        q_s[pl.ds(h * HEAD_DIM, 4 * HEAD_DIM), :] = (four_raw(h) * HEAD_DIM ** (-0.5)).astype(BF)
    keep(q_s, q_any)
    keep(unit_s, unit_any)
    keep(recip_s, recip_any)
    keep(w_all, wqkv_any)
    shares = []
    for o in range(1, planes):
        share = remote(og_ref, og_all.at[o], ps.at[0, o], ps.at[1, o], me.across(o))
        share.start()
        shares.append(share)
    accum[...] = jnp.zeros_like(accum)
    sums[...] = jnp.zeros_like(sums)

    def visit(slot):
        fill_bias(bias, lower_ref[...], slot)

        def four_heads(t, carry):
            keys = kv_all[slot, :, pl.ds(pl.multiple_of(t * 128, 128), 128)]
            values = kv_all[slot, :, pl.ds(pl.multiple_of(HK + t * 128, 128), 128)]
            totals = []
            for u in range(2):
                key = keys[:, u * 64 : u * 64 + 64]
                value = values[:, u * 64 : u * 64 + 64]
                for g in range(2):
                    at = pl.ds(pl.multiple_of(t * 256 + u * 128 + g * 64, 64), 64)
                    weight = jnp.exp(dot(key, q_s[at, :], NN) + bias[...])
                    totals.append(jnp.sum(weight, axis=0, keepdims=True))
                    accum[at, :] += dot(value, weight.astype(BF), TN)
            sums[t] += jnp.concatenate(totals, axis=0)
            return carry

        lax.fori_loop(0, GROUPS, four_heads, 0)

    visit(0)
    for k in range(1, half + 1):
        there = me.z - k >= 0

        @pl.when(there)
        def _():
            z_copy(k).wait_recv()

        @pl.when(there & (me.core == 1))
        def _():
            c_copy(k - 1).start()

        if k < half:
            @pl.when(there & (me.core == 0))
            def _():
                c_copy(k).start()

        @pl.when(there)
        def _():
            visit(2 * k)

    if depth > 2:
        passing.step(3)
    for i in range(half):
        @pl.when(me.z - i - 1 + me.core >= 0)
        def _():
            c_copy(i).wait_recv()
            visit(2 * i + 1)

    keep(kv_all, kv_any)
    for o in range(1, planes):
        outputs.relay(o)
    for t in range(GROUPS):
        total = sums[t]
        lse_out[t] = jnp.log(total)
        for h in range(4):
            at = pl.ds(t * 256 + h * 64, 64)
            o_out[at, :] = (accum[at, :] / total[h : h + 1, :]).astype(BF)
    for o in range(planes):
        outputs.arrive(o)
    keep(wo_all, wo_any)
    mixed = tok_ref[...].astype(F32) + dot(o_out[...].T, wo_all[...].reshape(HQ, D), NN)
    mixed_out[...] = mixed
    unit, _ = unit_of(mixed, 1)
    hn_out[...] = (unit * gains_out[:, D : 2 * D]).astype(BF)
    for s in range(4, depth + 1):
        passing.step(s)
    passing.finish()

    for i in range(half):
        @pl.when(me.z - i - me.core >= 0)
        def _():
            c_copy(i).wait_send()

    for k in range(1, half + 1):
        @pl.when(me.z + k < depth)
        def _():
            z_copy(k).wait_send()

    for o in range(1, planes):
        a2a_copy(o).wait_send()
    for share in shares:
        share.wait()
    gains.finish()
    weights.finish()
    outputs.finish()
    own_og.wait()
    for copy in kept:
        copy.wait()


def ahead(tokens, cosine, sine, lower, gains_block, w_qkv, w_output, w_gate_up, w_down, cotangent, n_gains, planes, depth, turns, collective_id):
    half = turns // 2
    count = tokens.shape[0]
    rows = w_qkv.shape[0]
    full = w_down.shape[1] // planes
    shapes = [
        ((HQ, count), BF),
        ((turns + 1, count, 2 * HK), BF),
        ((planes, depth, 2, rows, 2 * HQ), BF),
        ((D, count), BF),
        ((HQ + HK, count), F32),
        (((HEADS + KV_HEADS) // 4, 4, count), F32),
        ((planes, count, D), BF),
        ((planes, depth, 2, rows, D), BF),
        ((depth * 2, planes, 3, rows, full), BF),
        ((1, planes * depth * 2 * n_gains), F32),
        ((HQ, count), BF),
        ((GROUPS, 4, count), F32),
        ((count, D), F32),
        ((count, D), BF),
    ]
    return pl.pallas_call(
        functools.partial(ahead_kernel, planes, depth, turns, n_gains),
        out_shape=tuple(jax.ShapeDtypeStruct(s, k) for s, k in shapes),
        in_specs=[VMEM] * 9 + [ANY],
        out_specs=(ANY,) * 9 + (VMEM,) * 5,
        scratch_shapes=[pltpu.VMEM(*shapes[i]) for i in (0, 1, 2, 3, 4, 5, 7)]
        + [
            pltpu.VMEM((planes, 3, rows, full), BF),
            pltpu.VMEM((planes, depth, 2, 8, 128), F32),
            pltpu.VMEM((planes, count, D // planes), BF),
            pltpu.VMEM((count, D), F32),
            pltpu.VMEM((count, 2 * HQ), F32),
            pltpu.VMEM((count, count), F32),
            pltpu.VMEM((HQ, count), F32),
            pltpu.VMEM((GROUPS, 4, count), F32),
            DMA((2,)),
            DMA((8,)),
            DMA((2, half + 1)),
            DMA((2, half)),
            DMA((2, planes)),
            DMA((2, planes)),
            DMA((8, depth + 1)),
        ]
        + spread_sems(planes, depth) * 3,
        compiler_params=params(collective_id),
        cost_estimate=pl.CostEstimate(flops=40 << 30, bytes_accessed=8 << 20, transcendentals=0),
    )(tokens, cosine, sine, lower, gains_block, w_qkv, w_output, w_gate_up, w_down, cotangent)


def ffn_kernel(
    planes, depth, hn_ref, og_ref, w_any, gn_out, parts_out, grads_out,
    w, hns, hnt, ogt, mid, pair, send_gn, recv_gn, own_gn, stage, wsem, hsem, gsem, osem,
):
    me = Place(planes, depth)
    count, width = hn_ref.shape
    full = w.shape[2]
    ctxs, dps, rows = w_any.shape[0], w_any.shape[1], w_any.shape[3]
    chunk = 384 if full % 384 == 0 else full

    def w_copy(i, m):
        c, d = i // dps, i % dps
        return pltpu.make_async_copy(
            w_any.at[c, d, m], w.at[m, pl.ds((d * ctxs + c) * rows, rows), :], wsem.at[m, i]
        )

    def load(i, carry):
        for m in range(3):
            w_copy(i, m).start()
        return carry

    lax.fori_loop(0, ctxs * dps, load, 0)
    greet(me.plane())

    def hn_copy(o):
        return remote(hn_ref, hns.at[o], hsem.at[0, o], hsem.at[1, o], me.across(o))

    def gn_copy(o):
        return remote(send_gn.at[o], recv_gn.at[o], gsem.at[0, o], gsem.at[1, o], me.across(o))

    near = [o for o in range(1, planes) if o & (o - 1) == 0]
    far = [o for o in range(1, planes) if o & (o - 1) != 0]
    for o in near:
        hn_copy(o).start()
    hns[0] = hn_ref[...]

    def loaded(i, carry):
        for m in range(3):
            w_copy(i, m).wait()
        return carry

    lax.fori_loop(0, ctxs * dps, loaded, 0)

    def block(o, carry):
        @pl.when(o > 0)
        def _():
            hn_copy(o).wait_recv()

        hn = hns[o]
        og = og_ref[o]
        at = pl.ds(pl.multiple_of(o * count, 128), count)
        hnt[:, at] = hn.T
        ogt[:, at] = og.T
        own_gn[0] = jnp.zeros((count, width), F32)
        own_gn[1] = jnp.zeros((count, width), F32)

        def part(j, inner):
            cols = pl.ds(pl.multiple_of(j * chunk, 128), chunk)
            w_gate, w_up, w_down = w[0, :, cols], w[1, :, cols], w[2, :, cols]
            gate = dot(hn, w_gate, NN)
            upper = dot(hn, w_up, NN)
            sigma = 1.0 / (1.0 + jnp.exp(-gate))
            active = gate * sigma
            middle = (active * upper).astype(BF)
            gmid = dot(og, w_down, NN)
            ggate = (gmid * upper * sigma * (1.0 + gate * (1.0 - sigma))).astype(BF)
            gupper = (gmid * active).astype(BF)
            mid[at, cols] = middle
            pair[0, at, cols] = ggate
            pair[1, at, cols] = gupper
            own_gn[0] += dot(ggate, w_gate, NT) + dot(gupper, w_up, NT)
            own_gn[1] += dot(middle, w_down, NT)
            return inner

        lax.fori_loop(0, full // chunk, part, 0)
        parts_out[o] = own_gn[1].astype(BF)

        @pl.when(o > 0)
        def _():
            send_gn[o] = own_gn[0].astype(BF)
            gn_copy(o).start()

        @pl.when(o == 0)
        def _():
            gn_out[...] = own_gn[0]
            for other in far:
                hn_copy(other).start()

        return carry

    lax.fori_loop(0, planes, block, 0)

    strip = ctxs * rows

    def out_copy(m, d):
        return pltpu.make_async_copy(stage.at[m], grads_out.at[:, d, m], osem.at[m])

    def weight_grads(d, carry):
        left = pl.ds(pl.multiple_of(d * strip, 128), strip)
        for m in (2, 0, 1):
            @pl.when(d > 0)
            def _():
                out_copy(m, d - 1).wait()

            if m == 2:
                total = dot(ogt[left, :], mid[...], NN)
            else:
                total = dot(hnt[left, :], pair[m], NN)
            stage[m] = total.astype(BF).reshape(ctxs, rows, full)
            out_copy(m, d).start()
        return carry

    lax.fori_loop(0, dps, weight_grads, 0)
    for m in range(3):
        out_copy(m, dps - 1).wait()
    total = gn_out[...]
    for o in range(1, planes):
        gn_copy(o).wait_recv()
        total = total + recv_gn[o].astype(F32)
    gn_out[...] = total
    for o in range(1, planes):
        gn_copy(o).wait_send()
        hn_copy(o).wait_send()


def ffn(hn, og_all, w_all, planes, depth, collective_id):
    count, width = hn.shape
    ctxs, dps, _, rows, full = w_all.shape
    tokens = planes * count
    flops = 18 * tokens * width * full
    return pl.pallas_call(
        functools.partial(ffn_kernel, planes, depth),
        out_shape=(
            jax.ShapeDtypeStruct((count, width), F32),
            jax.ShapeDtypeStruct((planes, count, width), BF),
            jax.ShapeDtypeStruct((ctxs, dps, 3, rows, full), BF),
        ),
        in_specs=[VMEM, VMEM, ANY],
        out_specs=(VMEM, VMEM, ANY),
        scratch_shapes=[
            pltpu.VMEM((3, width, full), BF),
            pltpu.VMEM((planes, count, width), BF),
            pltpu.VMEM((width, tokens), BF),
            pltpu.VMEM((width, tokens), BF),
            pltpu.VMEM((tokens, full), BF),
            pltpu.VMEM((2, tokens, full), BF),
            pltpu.VMEM((planes, count, width), BF),
            pltpu.VMEM((planes, count, width), BF),
            pltpu.VMEM((2, count, width), F32),
            pltpu.VMEM((3, ctxs, rows, full), BF),
            DMA((3, ctxs * dps)),
            DMA((2, planes)),
            DMA((2, planes)),
            DMA((3,)),
        ],
        compiler_params=params(collective_id),
        cost_estimate=pl.CostEstimate(flops=flops, bytes_accessed=20 << 20, transcendentals=0),
    )(hn, og_all, w_all)


class Fold:
    def __init__(self, me, g_any, scratch):
        self.me, self.g = me, g_any
        self.mine, self.other, self.from_line, self.ready, self.landed, self.sems, self.psems = scratch

    def own_copy(self, z):
        return pltpu.make_async_copy(
            self.g.at[z * 2 + self.me.core], self.mine.at[z], self.sems.at[0, z]
        )

    def core_copy(self, z):
        me = self.me
        return remote(
            self.g.at[z * 2 + 1 - me.core], self.other.at[z], self.sems.at[1, z], self.sems.at[2, z], me.sibling()
        )

    def start(self):
        for z in range(self.me.depth):
            self.own_copy(z).start()

    def first(self):
        for z in range(self.me.depth):
            self.core_copy(z).start()

    def add(self, total, term):
        def plane(d, carry):
            total[d] = (total[d].astype(F32) + term[d].astype(F32)).astype(BF)
            return carry

        lax.fori_loop(0, self.me.planes, plane, 0)

    def second(self):
        for z in range(self.me.depth):
            self.own_copy(z).wait()
            self.core_copy(z).wait_recv()
            self.add(self.mine.at[z], self.other.at[z])

    def target(self, k, down):
        me = self.me
        return k - (me.depth - 1) + me.z if down else me.depth - 1 - k + me.z

    def sends(self, k, down):
        me = self.me
        return self.target(k, down) >= 0 if down else me.z <= k

    def copy(self, k, down):
        me = self.me
        t = self.target(k, down)
        slot = me.depth if k == me.depth - 2 and not down else t
        kind = 5 if down else 3
        return remote(
            self.mine.at[t], self.from_line.at[slot], self.sems.at[kind, k], self.sems.at[kind + 1, k],
            me.along(me.z - 1 if down else me.z + 1),
        )

    def arrived(self, k, slot, down):
        block = self.from_line.at[slot]
        kind = 5 if down else 3
        remote(block, block, self.sems.at[kind, k], self.sems.at[kind + 1, k], self.me.sibling()).wait_recv()

    def step(self, k):
        me = self.me
        for down in (False, True):
            edge = me.z == me.depth - 1 if down else me.z == 0

            @pl.when(self.sends(k, down))
            def _():
                t = self.target(k, down)
                if k > 0:
                    @pl.when(jnp.logical_not(edge))
                    def _():
                        self.arrived(k - 1, t, down)
                        self.add(self.mine.at[t], self.from_line.at[t])

                self.copy(k, down).start()

    def total(self):
        me = self.me
        k = me.depth - 2

        @pl.when(me.z < me.depth - 1)
        def _():
            self.arrived(k, me.z, True)
            self.add(self.mine.at[me.z], self.from_line.at[me.z])

        @pl.when(me.z > 0)
        def _():
            self.arrived(k, me.depth, False)
            self.add(self.mine.at[me.z], self.from_line.at[me.depth])

        self.ready[...] = self.mine[me.z]
        for o in range(1, me.planes):
            self.plane_copy(o).start()

    def plane_copy(self, o):
        me = self.me
        return remote(
            self.ready.at[me.dp ^ o], self.landed.at[me.dp], self.psems.at[0, o], self.psems.at[1, o], me.across(o)
        )

    def last(self):
        me = self.me
        self.landed[me.dp] = self.ready[me.dp]
        for o in range(1, me.planes):
            block = self.landed.at[me.dp ^ o]
            remote(block, block, self.psems.at[0, o], self.psems.at[1, o], me.across(o)).wait_recv()

    def finish(self):
        me = self.me
        for z in range(me.depth):
            self.core_copy(z).wait_send()
        for k in range(me.depth - 1):
            for down in (False, True):
                @pl.when(self.sends(k, down))
                def _():
                    self.copy(k, down).wait_send()
        for o in range(1, me.planes):
            self.plane_copy(o).wait_send()


FOLD = 7


def fold_scratch(planes, depth, rows, full):
    block = (planes, 3, rows, full)
    return [
        pltpu.VMEM((depth,) + block, BF),
        pltpu.VMEM((depth,) + block, BF),
        pltpu.VMEM((depth + 1,) + block, BF),
        pltpu.VMEM(block, BF),
        pltpu.VMEM(block, BF),
        DMA((7, depth)),
        DMA((2, planes)),
    ]


def home_kernel(
    planes, depth, turns, n_gains,
    gn_ref, mixed_ref, og_ref, gains_ref, o_ref, lse_ref, q_ref, lower_ref, cos_ref, sin_ref, tok_ref,
    wo_any, kv_any, parts_any, grads_any, unit_any, recip_any, w_any, xat_any,
    block_out, grad_out, shard_out, shard_qkv, gains_out, pair_out, down_out,
    wo, kv, unit_s, recip_s, w_all, xat, own_part, gq, grad_kv, gmixed_s,
    bias, gob, delta, gkv, from_core, from_z, from_plane, partial, gproj, partial_q, gains_p, *rest,
):
    me = Place(planes, depth)
    collect = Collect(me, partial, rest[:COLLECT])
    collect_q = Collect(me, partial_q, rest[COLLECT : 2 * COLLECT])
    small = Collect(me, gains_p, rest[2 * COLLECT : 3 * COLLECT])
    fold = Fold(me, grads_any, rest[3 * COLLECT : 3 * COLLECT + FOLD])
    cs, zs, ps, load = rest[3 * COLLECT + FOLD :]
    half = turns // 2
    count = gn_ref.shape[0]
    sources = [wo_any, kv_any, unit_any, recip_any, w_any, xat_any, parts_any.at[0]]
    places = [wo, kv, unit_s, recip_s, w_all, xat, own_part]
    loads = [pltpu.make_async_copy(a, b, load.at[i]) for i, (a, b) in enumerate(zip(sources, places))]
    for copy in loads[:2]:
        copy.start()
    fold.start()
    for copy in loads[2:]:
        copy.start()
    greet(me.plane() + me.line() + [me.sibling()])
    fold.first()

    def c_copy(i):
        return remote(gkv.at[2 * i + 1], from_core.at[i], cs.at[0, i], cs.at[1, i], me.sibling())

    def z_copy(k):
        return remote(gkv.at[2 * k], from_z.at[k - 1], zs.at[0, k], zs.at[1, k], me.along(me.behind(k)))

    def p_copy(o):
        return remote(parts_any.at[o], from_plane.at[o - 1], ps.at[0, o], ps.at[1, o], me.across(o))

    for o in range(1, planes):
        p_copy(o).start()
    unit, recip = unit_of(mixed_ref[...], 1)
    grad = gn_ref[...]
    scaled = grad * gains_ref[:, D : 2 * D]
    inner = jnp.mean(scaled * unit, axis=1, keepdims=True)
    gmixed = og_ref[...].astype(F32) + recip * (scaled - unit * inner)
    gmixed_s[...] = gmixed
    dgf = jnp.sum(grad * unit, axis=0, keepdims=True)
    gmixed_b = gmixed.astype(BF)
    loads[0].wait()
    gob[...] = dot(wo[...].reshape(HQ, D), gmixed_b, NT).astype(BF)
    for t in range(GROUPS):
        rows = []
        for h in range(4):
            at = pl.ds(t * 256 + h * 64, 64)
            rows.append(
                jnp.sum(gob[at, :].astype(F32) * o_ref[at, :].astype(F32), axis=0, keepdims=True)
            )
        delta[t] = jnp.concatenate(rows, axis=0)
    half_rows = D // planes
    order = list(range(1, planes)) + [0]
    for o in order:
        d = me.dp ^ o
        rows = o_ref[pl.ds(pl.multiple_of(d * half_rows, 128), half_rows), :]
        partial[d] = dot(rows, gmixed_b, NN).astype(BF).reshape(partial.shape[1:])
        collect.first(o)
    fold.second()
    fold.step(0)
    gq[...] = jnp.zeros_like(gq)
    loads[1].wait()

    def visit(slot):
        fill_bias(bias, lower_ref[...], slot)

        def four_heads(t, carry):
            key_at = pl.ds(pl.multiple_of(t * 128, 128), 128)
            value_at = pl.ds(pl.multiple_of(HK + t * 128, 128), 128)
            keys, values = kv[slot, :, key_at], kv[slot, :, value_at]
            lse_t, delta_t = lse_ref[t], delta[t]
            grad_keys, grad_values = [], []
            for u in range(2):
                key = keys[:, u * 64 : u * 64 + 64]
                value = values[:, u * 64 : u * 64 + 64]
                grad_key, grad_value = 0.0, 0.0
                for g in range(2):
                    h = 2 * u + g
                    at = pl.ds(pl.multiple_of(t * 256 + h * 64, 64), 64)
                    query, gob_h = q_ref[at, :], gob[at, :]
                    probs = jnp.exp(dot(key, query, NN) + bias[...] - lse_t[h : h + 1, :])
                    grad_value = grad_value + dot(probs.astype(BF), gob_h, NT)
                    grad_scores = (probs * (dot(value, gob_h, NN) - delta_t[h : h + 1, :])).astype(BF)
                    grad_key = grad_key + dot(grad_scores, query, NT)
                    gq[at, :] += dot(key, grad_scores, TN)
                grad_keys.append(grad_key)
                grad_values.append(grad_value)
            gkv[slot, :, key_at] = jnp.concatenate(grad_keys, axis=1).astype(BF)
            gkv[slot, :, value_at] = jnp.concatenate(grad_values, axis=1).astype(BF)
            return carry

        lax.fori_loop(0, GROUPS, four_heads, 0)

    for i in range(half - 1, -1, -1):
        @pl.when(me.z - i - 1 + me.core >= 0)
        def _():
            visit(2 * i + 1)
            c_copy(i).start()

    for k in range(half, 0, -1):
        @pl.when(me.z - k >= 0)
        def _():
            visit(2 * k)

            @pl.when(me.core == 0)
            def _():
                if k < half:
                    c_copy(k).wait_recv()
                    gkv[2 * k] = (gkv[2 * k].astype(F32) + from_core[k].astype(F32)).astype(BF)

            @pl.when(me.core == 1)
            def _():
                c_copy(k - 1).wait_recv()
                gkv[2 * k] = (gkv[2 * k].astype(F32) + from_core[k - 1].astype(F32)).astype(BF)

            z_copy(k).start()

    for o in order:
        collect.second(o)
    if depth > 2:
        fold.step(1)
    visit(0)
    value_o = collect.third()
    total = mixed_ref[...]
    loads[6].wait()
    total = total + own_part[...].astype(F32)
    for o in range(1, planes):
        p_copy(o).wait_recv()
        total = total + from_plane[o - 1].astype(F32)
    block_out[...] = total.astype(BF)
    shard_out[...] = collect.last(value_o)
    grad_kv[...] = gkv[0].astype(F32)

    for i in (2, 3, 5, 4):
        loads[i].wait()
    tail_row = gains_ref[:, 2 * D : 2 * D + 128]
    gain_q, gain_k = column_of(tail_row, 0), column_of(tail_row, HEAD_DIM)
    cosine, sine = cos_ref[...], -sin_ref[...]
    gained = [0.0, 0.0]

    def four_grads(h):
        kind = 0 if h < HEADS else 1
        if kind == 0:
            four = gq[pl.ds(h * HEAD_DIM, 4 * HEAD_DIM), :] * HEAD_DIM ** (-0.5)
        else:
            four = grad_kv[:, pl.ds((h - HEADS) * HEAD_DIM, 4 * HEAD_DIM)].T
        recips = recip_s[h // 4]
        results = []
        for i in range(4):
            unit = unit_s[pl.ds((h + i) * HEAD_DIM, HEAD_DIM), :]
            grad = turned(four[i * HEAD_DIM : (i + 1) * HEAD_DIM], cosine, sine)
            scaled = grad * (gain_k if kind else gain_q)
            inner = jnp.mean(scaled * unit, axis=0, keepdims=True)
            results.append(recips[i : i + 1, :] * (scaled - unit * inner))
            gained[kind] = gained[kind] + grad * unit
        gproj[:, pl.ds(h * HEAD_DIM, 4 * HEAD_DIM)] = jnp.concatenate(results, axis=0).T.astype(BF)

    for h in range(0, HEADS, 4):
        four_grads(h)

    @pl.when(me.core == 0)
    def _():
        c_copy(0).wait_recv()
        grad_kv[...] += from_core[0].astype(F32)

    for k in range(1, half + 1):
        @pl.when(me.z + k < depth)
        def _():
            z_copy(k).wait_recv()
            grad_kv[...] += from_z[k - 1].astype(F32)

    for h in range(HEADS, HEADS + KV_HEADS, 4):
        four_grads(h)
    gproj[:, pl.ds(HQ + HK, HK)] = grad_kv[:, pl.ds(HK, HK)].astype(BF)
    for o in order:
        d = me.dp ^ o
        rows = xat[pl.ds(pl.multiple_of(d * half_rows, 128), half_rows), :]
        partial_q[d] = dot(rows, gproj[...], NN).astype(BF).reshape(partial_q.shape[1:])
        collect_q.first(o)
        if o != order[0]:
            collect_q.second(order[order.index(o) - 1])
    collect_q.second(0)
    for k in range(2, depth - 1):
        fold.step(k)
    grad = dot(gproj[...], w_all[...].reshape(D, 2 * HQ), NT)
    unit, recip = unit_of(tok_ref[...].astype(F32), 1)
    scaled = grad * gains_ref[:, :D]
    inner = jnp.mean(scaled * unit, axis=1, keepdims=True)
    grad_out[...] = gmixed_s[...] + recip * (scaled - unit * inner)
    dga = jnp.sum(grad * unit, axis=0, keepdims=True)
    lane = lax.broadcasted_iota(jnp.int32, (HEAD_DIM, 128), 1)
    entry = lax.broadcasted_iota(jnp.int32, (HEAD_DIM, 128), 0)
    sums = [jnp.sum(g, axis=1, keepdims=True) for g in gained]
    last = jnp.sum(
        jnp.where(lane == entry, sums[0], 0.0) + jnp.where(lane == entry + HEAD_DIM, sums[1], 0.0),
        axis=0,
        keepdims=True,
    )
    whole = jnp.concatenate([dga, dgf, last], axis=1)
    devices = planes * depth * 2
    entries = devices * n_gains
    index = lax.broadcasted_iota(jnp.int32, (devices, entries), 1)
    device = lax.broadcasted_iota(jnp.int32, (devices, entries), 0)
    apart = jnp.where(index // n_gains == device, whole, 0.0)
    pick = jnp.where(
        lax.broadcasted_iota(jnp.int32, (128, entries), 1) % n_gains
        == lax.broadcasted_iota(jnp.int32, (128, entries), 0),
        1.0,
        0.0,
    )
    table = lax.dot_general(
        apart, pick, NT, preferred_element_type=F32, precision=lax.Precision.HIGHEST
    )
    gains_p[...] = jnp.broadcast_to(table[:, None, :], (devices, 8, 128)).reshape(gains_p.shape)
    for o in order:
        small.first(o)
    for o in order:
        small.second(o)
    value = collect_q.third()
    little = small.third()
    fold.total()
    shard_qkv[...] = collect_q.last(value)
    gains_out[...] = small.last(little)
    fold.last()
    full = fold.landed.shape[3]
    for d in range(planes):
        for m in range(2):
            pair_out[:, (m * planes + d) * full : (m * planes + d + 1) * full] = fold.landed[d, m]
        down_out[:, d * full : (d + 1) * full] = fold.landed[d, 2]

    for o in range(1, planes):
        p_copy(o).wait_send()
    for i in range(half):
        @pl.when(me.z - i - 1 + me.core >= 0)
        def _():
            c_copy(i).wait_send()
    for k in range(1, half + 1):
        @pl.when(me.z - k >= 0)
        def _():
            z_copy(k).wait_send()
    collect.finish()
    collect_q.finish()
    small.finish()
    fold.finish()


def home(near, far, n_gains, planes, depth, turns, collective_id):
    half = turns // 2
    count = near[0].shape[0]
    wo_all, kv_all, _, grads, unit, recip, w_all, xat = far
    rows = wo_all.shape[3]
    full = grads.shape[4]
    return pl.pallas_call(
        functools.partial(home_kernel, planes, depth, turns, n_gains),
        out_shape=(
            jax.ShapeDtypeStruct((count, D), BF),
            jax.ShapeDtypeStruct((count, D), F32),
            jax.ShapeDtypeStruct((rows, D), F32),
            jax.ShapeDtypeStruct((rows, 2 * HQ), F32),
            jax.ShapeDtypeStruct((8, 128), F32),
            jax.ShapeDtypeStruct((rows, 2 * planes * full), BF),
            jax.ShapeDtypeStruct((rows, planes * full), BF),
        ),
        in_specs=[VMEM] * len(near) + [ANY] * len(far),
        out_specs=(VMEM,) * 7,
        scratch_shapes=[pltpu.VMEM(a.shape, a.dtype) for a in (wo_all, kv_all, unit, recip, w_all, xat)]
        + [
            pltpu.VMEM((count, D), BF),
            pltpu.VMEM((HQ, count), F32),
            pltpu.VMEM((count, 2 * HK), F32),
            pltpu.VMEM((count, D), F32),
            pltpu.VMEM((count, count), F32),
            pltpu.VMEM((HQ, count), BF),
            pltpu.VMEM((GROUPS, 4, count), F32),
            pltpu.VMEM((turns + 1, count, 2 * HK), BF),
            pltpu.VMEM((half, count, 2 * HK), BF),
            pltpu.VMEM((half, count, 2 * HK), BF),
            pltpu.VMEM((planes - 1, count, D), BF),
            pltpu.VMEM((planes, depth, 2, rows, D), BF),
            pltpu.VMEM((count, 2 * HQ), BF),
            pltpu.VMEM((planes, depth, 2, rows, 2 * HQ), BF),
            pltpu.VMEM((planes, depth, 2, 8, 128), F32),
        ]
        + collect_scratch(planes, depth, rows, D, BF)
        + collect_scratch(planes, depth, rows, 2 * HQ, BF)
        + collect_scratch(planes, depth, 8, 128, F32)
        + fold_scratch(planes, depth, rows, full)
        + [DMA((2, half)), DMA((2, half + 1)), DMA((2, planes)), DMA((7,))],
        compiler_params=params(collective_id),
        cost_estimate=pl.CostEstimate(flops=60 << 30, bytes_accessed=8 << 20, transcendentals=0),
    )(*near, *far)


def per_device(
    tokens_in,
    positions,
    out_grad,
    w_qkv,
    w_output,
    w_gate_up,
    w_down,
    norm_gains,
    first_qkv,
    first_output,
    first_gate_up,
    first_down,
    first_gains,
    second_qkv,
    second_output,
    second_gate_up,
    second_down,
    second_gains,
):
    planes, ctxs = lax.axis_size("dp"), lax.axis_size("ctx")
    depth = ctxs // 2
    turns = ctxs // 2
    rows = w_qkv.shape[0]
    full = w_down.shape[1] // planes
    n_gains = norm_gains.shape[0]
    count = tokens_in.shape[0] * tokens_in.shape[1]
    tokens = tokens_in.reshape(count, D)
    places = positions.reshape(count)
    cotangent = out_grad.reshape(count, D)

    gains_block = jnp.pad(norm_gains.astype(BF).astype(F32)[None, :], ((0, 7), (0, 128 - n_gains)))
    cosine, sine = rope_tables(places)
    lower = (jnp.arange(count, dtype=jnp.int32) - places)[None, :]
    (
        query, kv_all, qkv_all, xat, unit_heads, recip_heads, og_all, output_all, w_all,
        gains_row, attn_t, lse, mixed, hn,
    ) = ahead(
        tokens, cosine, sine, lower, gains_block, w_qkv, w_output, w_gate_up, w_down, cotangent,
        n_gains, planes, depth, turns, 0,
    )
    w_used = w_all if rows % 16 == 0 else w_all.transpose(2, 1, 0, 3, 4).reshape(1, 1, 3, D, full)
    grad_normed, parts, grads = ffn(hn, og_all, w_used, planes, depth, 1)
    if rows % 16 != 0:
        grads = grads.reshape(3, planes, ctxs, rows, full).transpose(2, 1, 0, 3, 4)
    block_out, input_grad, shard_output, shard_qkv, gains_tile, pair_b, down_b = home(
        (grad_normed, mixed, cotangent, gains_row, attn_t, lse, query, lower, cosine, sine, tokens),
        (output_all, kv_all, parts, grads, unit_heads, recip_heads, qkv_all, xat),
        n_gains, planes, depth, turns, 2,
    )
    shard_gains = gains_tile[0, :n_gains]
    shard_gate_up = pair_b.astype(F32)
    shard_down = down_b.astype(F32)

    new_qkv, new_first_qkv, new_second_qkv = adam_step(
        w_qkv, shard_qkv, first_qkv, second_qkv, 0.02, 0.1
    )
    new_output, new_first_output, new_second_output = adam_step(
        w_output, shard_output, first_output, second_output, 0.2, 0.1
    )
    new_gate_up, new_first_gate_up, new_second_gate_up = adam_step(
        w_gate_up, shard_gate_up, first_gate_up, second_gate_up, 0.02, 0.1
    )
    new_down, new_first_down, new_second_down = adam_step(
        w_down, shard_down, first_down, second_down, 0.02, 0.1
    )
    new_gains, new_first_gains, new_second_gains = adam_step(
        norm_gains, shard_gains, first_gains, second_gains, 0.1, 0.0
    )
    return (
        block_out.reshape(tokens_in.shape),
        input_grad.reshape(tokens_in.shape),
        shard_qkv,
        shard_output,
        shard_gate_up,
        shard_down,
        shard_gains,
        new_qkv,
        new_output,
        new_gate_up,
        new_down,
        new_gains,
        new_first_qkv,
        new_first_output,
        new_first_gate_up,
        new_first_down,
        new_first_gains,
        new_second_qkv,
        new_second_output,
        new_second_gate_up,
        new_second_down,
        new_second_gains,
    )


def solution(mesh):
    in_specs = (
        P("dp", "ctx", None),
        P("dp", "ctx"),
        P("dp", "ctx", None),
        P(("dp", "ctx"), None),
        P(("dp", "ctx"), None),
        P(("dp", "ctx"), None),
        P(("dp", "ctx"), None),
        P(("dp", "ctx")),
        P(("dp", "ctx"), None),
        P(("dp", "ctx"), None),
        P(("dp", "ctx"), None),
        P(("dp", "ctx"), None),
        P(("dp", "ctx")),
        P(("dp", "ctx"), None),
        P(("dp", "ctx"), None),
        P(("dp", "ctx"), None),
        P(("dp", "ctx"), None),
        P(("dp", "ctx")),
    )
    out_specs = (
        P("dp", "ctx", None),
        P("dp", "ctx", None),
        P(("dp", "ctx"), None),
        P(("dp", "ctx"), None),
        P(("dp", "ctx"), None),
        P(("dp", "ctx"), None),
        P(("dp", "ctx")),
        P(("dp", "ctx"), None),
        P(("dp", "ctx"), None),
        P(("dp", "ctx"), None),
        P(("dp", "ctx"), None),
        P(("dp", "ctx")),
        P(("dp", "ctx"), None),
        P(("dp", "ctx"), None),
        P(("dp", "ctx"), None),
        P(("dp", "ctx"), None),
        P(("dp", "ctx")),
        P(("dp", "ctx"), None),
        P(("dp", "ctx"), None),
        P(("dp", "ctx"), None),
        P(("dp", "ctx"), None),
        P(("dp", "ctx")),
    )
    return jax.shard_map(
        per_device, mesh=mesh, in_specs=in_specs, out_specs=out_specs, check_vma=False
    )
```

time: 387 us -> 338 us (0.87)
  Pallas kernels: 346 us -> 319 us
  between operations: 14.1 us -> 0.87 us
  other arithmetic: 17.1 us -> 12.4 us
    pallas_call x6 -> x2, Pallas kernels: 290 us -> 261 us  [the longest x1 167 us: home(): pl.pallas_call(functools.partial(home_kernel, planes, depth, turns, n_gai...]
    convert_element_type x5 -> x0, other arithmetic: 5.56 us -> none  [the longest x1 1.72 us: per_device(): w_qkv.astype(BF)]
  transfers between devices with their start and end apart: 3 -> 0, of which waited for: 0 -> 0; matrix products, arithmetic and copies ran while one was open for 1% -> 0% of each run, Pallas kernels for 65% -> 0%
where the time goes in v3:
time: 338 us
  Pallas kernels  319 us (94%)
  other arithmetic  12.4 us (4%)
  local copies, waits for them, and re-layouts  5.37 us (2%)
    pallas_call x1, Pallas kernels, home(): pl.pallas_call(functools.partial(home_kernel, planes, depth, turns, n_gai...  167 us
    pallas_call x1, Pallas kernels, ahead(): pl.pallas_call(functools.partial(ahead_kernel, planes, depth, turns, n_ga...  93.6 us
    pallas_call x1, Pallas kernels, ffn(): pl.pallas_call(functools.partial(ffn_kernel, planes, depth), out_shape=(j...  58.2 us
    sub x5, other arithmetic, adam_step(): weight - rate * (first_hat / (jnp.sqrt(second_hat) + ADAM_EPS) + decay *...  8.95 us

profile of v3, /device:TPU:0, one launch (start us, length us, event | category | flops | bytes accessed | tf_op | source)
XLA Modules:
  0.0 337.8 jit_solution(3157328592417600760)
XLA Ops:
  0.7 0.7 convert_bitcast_fusion
  1.3 1.3 iota_subtract_fusion
  2.7 0.6 pad_convert_fusion.gain_ref
  3.2 0.8 multiply_sine_fusion
  4.1 93.6 %shard_map.345 = (bf16[1024,256]{1,0:T(8,128)(2,1)}, bf16[5,256,1024]{2,1,0:T(8,128)(2,1)}, bf16[4,4,2,32,2048]{4,3,2,1,0:T(8,128)(2,1)}, bf16[1024,256]{1,0:T(8...) custom-call(bf16[256,1024]{1,0:T(8,128)(2,1)} %bitcast.13, ...), custom_call_target="tpu_custom_call" | custom-call | flops 42949672960 | bytes 8388608 | tf_op jit(solution)/shard_map/pallas_call | solution.py:570
  97.7 58.2 %shard_map.346 = (f32[256,1024]{1,0:T(8,128)}, bf16[4,256,1024]{2,1,0:T(8,128)(2,1)}, bf16[8,4,3,32,1152]{4,3,2,1,0:T(8,128)(2,1)}) custom-call(bf16[256,1024]{1,0:T(8,128)(2,1)} %get-tuple-element.46.hn_ref, bf16[4,256,1024]{2,1,0:T(8,128)(2,1)} %get-tuple-element.47.og_ref, bf16[8,4,3,32,1152]{4,3,2,1,0:T(8,128)(2,1)} %get-tuple-element.48.w_any), custom_call_target="tpu_custom_call" | custom-call | flops 21743271936 | bytes 20971520 | tf_op jit(solution)/shard_map/pallas_call | solution.py:729
  155.9 0.0 copy-start.18
  155.9 0.0 copy-start.19
  155.9 0.0 copy-start.20
  155.9 0.0 copy-start.15
  155.9 0.0 copy-start.16
  155.9 0.0 copy-start.17
  155.9 0.0 copy-start.12
  156.0 0.0 copy-start.13
  156.0 0.0 copy-start.14
  156.0 167.4 %shard_map.347 = (bf16[256,1024]{1,0:T(8,128)(2,1)}, f32[256,1024]{1,0:T(8,128)}, f32[32,1024]{1,0:T(8,128)}, f32[32,2048]{1,0:T(8,128)}, f32[8,128]{1,0:T(8,128...) custom-call(f32[256,1024]{1,0:T(8,128)} %get-tuple-element.49.gn_ref, f32[256,1024]{1,0:T(8,128)} %get-tuple-element.50.mixed_ref, ...), custom_call_target="tpu_custom_call" | custom-call | flops 64424509440 | bytes 8388608 | tf_op jit(solution)/shard_map/pallas_call | solution.py:1152
  323.4 0.0 copy-done.18
  323.4 0.0 copy-done.19
  323.4 0.0 copy-done.20
  323.4 1.2 multiply_subtract_fusion.4
  324.6 0.0 copy-done.15
  324.6 0.0 copy-done.16
  324.6 0.0 copy-done.17
  324.6 0.0 copy-start.5
  324.6 0.0 copy-start.6
  324.6 0.0 copy-start.7
  324.7 0.0 copy-start.11
  324.7 1.8 multiply_subtract_fusion.3
  326.5 0.0 copy-done.12
  326.5 0.0 copy-done.13
  326.5 0.0 copy-done.14
  326.5 1.9 multiply_subtract_fusion.2
  328.5 0.0 copy-done.6
  328.5 0.0 copy-start
  328.5 0.0 copy-start.1
  328.5 0.0 copy-start.2
  328.5 1.5 multiply_subtract_fusion.1
  330.1 0.1 copy-done
  330.2 0.8 copy-done.1
  331.0 0.4 copy-done.2
  331.3 0.1 copy-done.8
  331.5 2.4 multiply_subtract_fusion
  333.9 0.8 copy.44
  334.7 0.6 copy-done.4
  335.3 1.0 copy.45
  336.3 0.1 copy-done.3
  336.4 0.7 copy.46
  337.1 0.7 copy.47
  (11 shorter events, 0.0 us)
Async XLA Ops:
  155.9 167.5 %copy-start.18 = (f32[68]{0:T(128)S(1)}, f32[68]{0:T(128)}, u32[]{:S(2)}) copy-start(f32[68]{0:T(128)} %param.25) | copy-start | bytes 820
  155.9 167.5 %copy-start.19 = (f32[68]{0:T(128)S(1)}, f32[68]{0:T(128)}, u32[]{:S(2)}) copy-start(f32[68]{0:T(128)} %param.30) | copy-start | bytes 820
  155.9 167.5 %copy-start.20 = (f32[68]{0:T(128)S(1)}, f32[68]{0:T(128)}, u32[]{:S(2)}) copy-start(f32[68]{0:T(128)} %param.35) | copy-start | bytes 820
  155.9 168.7 %copy-start.15 = (f32[32,1024]{1,0:T(8,128)S(1)}, f32[32,1024]{1,0:T(8,128)}, u32[]{:S(2)}) copy-start(f32[32,1024]{1,0:T(8,128)} %wout_ref.1) | copy-start | bytes 393220
  155.9 168.7 %copy-start.16 = (f32[32,1024]{1,0:T(8,128)S(1)}, f32[32,1024]{1,0:T(8,128)}, u32[]{:S(2)}) copy-start(f32[32,1024]{1,0:T(8,128)} %param.27) | copy-start | bytes 393220
  155.9 168.7 %copy-start.17 = (f32[32,1024]{1,0:T(8,128)S(1)}, f32[32,1024]{1,0:T(8,128)}, u32[]{:S(2)}) copy-start(f32[32,1024]{1,0:T(8,128)} %param.32) | copy-start | bytes 393220
  155.9 170.6 %copy-start.12 = (f32[32,2048]{1,0:T(8,128)S(1)}, f32[32,2048]{1,0:T(8,128)}, u32[]{:S(2)}) copy-start(f32[32,2048]{1,0:T(8,128)} %wqkv_ref.1) | copy-start | bytes 786436
  156.0 170.6 %copy-start.13 = (f32[32,2048]{1,0:T(8,128)S(1)}, f32[32,2048]{1,0:T(8,128)}, u32[]{:S(2)}) copy-start(f32[32,2048]{1,0:T(8,128)} %param.26) | copy-start | bytes 786436
  156.0 170.5 %copy-start.14 = (f32[32,2048]{1,0:T(8,128)S(1)}, f32[32,2048]{1,0:T(8,128)}, u32[]{:S(2)}) copy-start(f32[32,2048]{1,0:T(8,128)} %param.31) | copy-start | bytes 786436
  324.6 3.8 %copy-start.5 = (f32[32,4608]{1,0:T(8,128)S(1)}, f32[32,4608]{1,0:T(8,128)}, u32[]{:S(2)}) copy-start(f32[32,4608]{1,0:T(8,128)} %wdown_ref.1) | copy-start | bytes 1769476
  324.6 3.8 %copy-start.6 = (f32[32,4608]{1,0:T(8,128)S(1)}, f32[32,4608]{1,0:T(8,128)}, u32[]{:S(2)}) copy-start(f32[32,4608]{1,0:T(8,128)} %param.29) | copy-start | bytes 1769476
  324.6 3.8 %copy-start.7 = (f32[32,4608]{1,0:T(8,128)S(1)}, f32[32,4608]{1,0:T(8,128)}, u32[]{:S(2)}) copy-start(f32[32,4608]{1,0:T(8,128)} %param.34) | copy-start | bytes 1769476
  324.7 3.8 %copy-start.11 = (bf16[32,4608]{1,0:T(8,128)(2,1)S(1)}, bf16[32,4608]{1,0:T(8,128)(2,1)}, u32[]{:S(2)}) copy-start(bf16[32,4608]{1,0:T(8,128)(2,1)} %get-tuple-element.68) | copy-start | bytes 884740
  328.5 1.7 copy-start
  328.5 2.5 copy-start.1
  328.5 2.8 copy-start.2
  328.5 2.9 copy-start.8
  331.5 2.4 copy-start.10
  333.9 1.4 copy-start.4
  335.3 1.1 copy-start.3
  335.3 1.8 copy-start.9

commit v4 on v3

--- a/solution.py
+++ b/solution.py
@@ -88,6 +88,14 @@
         return [self.along(self.ahead(k)) for k in range(1, self.depth)]
 
 
+def near(planes):
+    return [o for o in range(1, planes) if o & (o - 1) == 0]
+
+
+def far(planes):
+    return [o for o in range(1, planes) if o & (o - 1) != 0]
+
+
 def greet(devices):
     barrier = pltpu.get_barrier_semaphore()
     for device in devices:
@@ -137,9 +145,13 @@
             remote(
                 block, block, self.line_sems.at[0, k], self.line_sems.at[1, k], me.along(me.ahead(k))
             ).wait_recv()
-        for o in range(1, me.planes):
+        self.push(self.mine(0, me.core), self.mine(0, me.core), 2, 0, me.sibling())
+        self.plane(near(me.planes))
+
+    def plane(self, places):
+        me = self.me
+        for o in places:
             self.push(self.mine(0, me.core), self.mine(0, me.core), 0, o, me.across(o))
-        self.push(self.mine(0, me.core), self.mine(0, me.core), 2, 0, me.sibling())
 
     def relay(self, o):
         block = self.mine(o, self.me.core)
@@ -267,7 +279,7 @@
     def copy(self, kind, s, down, core=None, device=None):
         me = self.me
         z = me.z + s - 1 if down else me.z - s + 1
-        block = self.w.at[z * 2 + (me.core if core is None else core)]
+        block = self.w.at[:, :, z * 2 + (me.core if core is None else core)]
         device = me.sibling() if device is None else device
         return remote(block, block, self.sems.at[kind, s], self.sems.at[kind + 1, s], device)
 
@@ -290,7 +302,7 @@
                 def _():
                     me = self.me
                     z = me.z + s - 1 if down else me.z - s + 1
-                    block = self.w.at[z * 2 + me.core]
+                    block = self.w.at[:, :, z * 2 + me.core]
                     kind = 2 if down else 0
                     remote(
                         block, block, self.sems.at[kind, s - 1], self.sems.at[kind + 1, s - 1], me.sibling()
@@ -304,6 +316,14 @@
                 @pl.when(self.held(s, down))
                 def _():
                     self.copy(6 if down else 4, s, down).start()
+
+    def arrive(self):
+        for s in range(1, self.me.depth + 1):
+            for down in (False, True):
+                if s > 1 or not down:
+                    @pl.when(self.held(s, down))
+                    def _():
+                        self.copy(6 if down else 4, s, down, 1 - self.me.core).wait_recv()
 
     def finish(self):
         for s in range(1, self.me.depth + 1):
@@ -316,27 +336,31 @@
                     @pl.when(self.held(s, down))
                     def _():
                         self.copy(6 if down else 4, s, down).wait_send()
-                        self.copy(6 if down else 4, s, down, 1 - self.me.core).wait_recv()
-
-
-def ahead_kernel(
+
+
+def fore_kernel(
     planes, depth, turns, n_gains,
     tok_ref, cos_ref, sin_ref, lower_ref, gain_ref, wqkv_ref, wout_ref, wpair_ref, wdown_ref, og_ref,
-    q_any, kv_any, wqkv_any, xat_any, unit_any, recip_any, og_all, wo_any, w_any,
-    gains_out, o_out, lse_out, mixed_out, hn_out,
-    q_s, kv_all, w_all, xat, unit_s, recip_s, wo_all, blocks, gains_g, xa, xa_plain, proj, bias, accum, sums,
-    own_sem, keep_sem, zs, cs, ps, a2a, pass_sem, glsem, gsem, wlsem, wsem, olsem, osem,
+    q_any, kv_any, wq_any, wkv_any, xat_any, unit_any, recip_any, wo_any, parts_any, spill_any, grads_a, grads_b, mine_any,
+    gains_out, o_out, lse_out, mixed_out, gn_out,
+    q_s, kv_all, wq_all, wkv_all, xat, unit_s, recip_s, wo_all, blocks_a, blocks_b, gains_g, xa, proj, bias, accum, sums,
+    wa, wb, hns, ogs, hnt, ogt, mid, pair, send_gn, recv_gn, part_s, stage, mine,
+    own_sem, keep_sem, zs, cs, ps, a2a_a, a2a_b, pass_a, pass_b, hsem, nsem, psem, ssem, stsem,
+    glsem, gsem, qlsem, qsem, wlsem, wsem, olsem, osem, *fold_rest,
 ):
     me = Place(planes, depth)
     half = turns // 2
     count = tok_ref.shape[0]
     width = D // planes
     rows = wqkv_ref.shape[0]
-    full = blocks.shape[3]
+    halves = (blocks_a.shape[3], blocks_b.shape[3])
+    full = sum(halves)
     gains = Spread(me, gains_g, glsem, gsem)
-    weights = Spread(me, w_all, wlsem, wsem)
+    queries = Spread(me, wq_all, qlsem, qsem)
+    weights = Spread(me, wkv_all, wlsem, wsem)
     outputs = Spread(me, wo_all, olsem, osem)
-    passing = Pass(me, w_any, pass_sem)
+    pass_first, pass_second = Pass(me, wa, pass_a), Pass(me, wb, pass_b)
+    fold = Fold(me, grads_a, mine, fold_rest)
     kept = []
 
     def keep(source, into):
@@ -345,37 +369,48 @@
         kept.append(copy)
 
     gains_g[me.dp, me.z, me.core] = gain_ref[...]
-    w_all[me.dp, me.z, me.core] = wqkv_ref[...].astype(BF)
+    wq_all[me.dp, me.z, me.core] = wqkv_ref[:, :HQ].astype(BF)
+    wkv_all[me.dp, me.z, me.core] = wqkv_ref[:, HQ:].astype(BF)
     wo_all[me.dp, me.z, me.core] = wout_ref[...].astype(BF)
     for d in range(planes):
-        for m in range(2):
-            blocks[d, m] = wpair_ref[:, (m * planes + d) * full : (m * planes + d + 1) * full].astype(BF)
-        blocks[d, 2] = wdown_ref[:, d * full : (d + 1) * full].astype(BF)
-    own_block = pltpu.make_async_copy(blocks.at[me.dp], w_any.at[me.ctx, me.dp], own_sem.at[0])
-    own_block.start()
-    own_og = pltpu.make_async_copy(og_ref, og_all.at[0], own_sem.at[1])
+        for m in range(3):
+            source = wdown_ref if m == 2 else wpair_ref
+            at = d * full if m == 2 else (m * planes + d) * full
+            blocks_a[d, m] = source[:, at : at + halves[0]].astype(BF)
+            blocks_b[d, m] = source[:, at + halves[0] : at + full].astype(BF)
+    wa[:, me.dp, me.ctx] = blocks_a[me.dp]
+    wb[:, me.dp, me.ctx] = blocks_b[me.dp]
+    own_og = pltpu.make_async_copy(og_ref, ogs.at[0], own_sem.at[1])
     own_og.start()
     greet(me.plane() + me.line() + [me.sibling()])
     gains.line()
     weights.line()
 
-    def a2a_copy(o):
+    def a2a_copy(part, o):
+        source, into, sems = ((blocks_a, wa, a2a_a), (blocks_b, wb, a2a_b))[part]
         return remote(
-            blocks.at[me.dp ^ o], w_any.at[me.ctx, me.dp], a2a.at[0, o], a2a.at[1, o], me.across(o)
+            source.at[me.dp ^ o], into.at[:, me.dp, me.ctx], sems.at[0, o], sems.at[1, o], me.across(o)
         )
 
-    for o in range(1, planes):
-        a2a_copy(o).start()
+    def a2a_wait(part):
+        into, sems = ((wa, a2a_a), (wb, a2a_b))[part]
+        for o in range(1, planes):
+            block = into.at[:, me.dp ^ o, me.ctx]
+            remote(block, block, sems.at[0, o], sems.at[1, o], me.across(o)).wait_recv()
+
+    for part in range(2):
+        for o in range(1, planes):
+            a2a_copy(part, o).start()
+    queries.line()
     outputs.line()
     unit, _ = unit_of(tok_ref[...].astype(F32), 1)
-    xa_plain[...] = unit
+    proj[:, :D] = unit
     gains.first()
+    gains.plane(far(planes))
     weights.first()
-    own_block.wait()
-    for o in range(1, planes):
-        block = w_any.at[me.ctx, me.dp ^ o]
-        remote(block, block, a2a.at[0, o], a2a.at[1, o], me.across(o)).wait_recv()
-    passing.step(1)
+    a2a_wait(0)
+    pass_first.step(1)
+    queries.first()
     for o in range(1, planes):
         gains.relay(o)
     for o in range(planes):
@@ -392,17 +427,24 @@
     device = lax.broadcasted_iota(jnp.int32, (devices, entries), 0)
     gains_row = 1.0 + jnp.sum(jnp.where(owner == device, spread, 0.0), axis=0, keepdims=True)
     gains_out[...] = gains_row
-    normed = (xa_plain[...] * gains_row[:, :D]).astype(BF)
+    normed = (proj[:, :D] * gains_row[:, :D]).astype(BF)
     xat[...] = normed.T
     keep(xat, xat_any)
     for d in range(planes):
         xa[d] = normed[:, d * width : (d + 1) * width]
-    proj[...] = jnp.zeros_like(proj)
-    for o in range(planes):
-        if o > 0:
-            weights.relay(o)
-        weights.arrive(o)
-        proj[...] += dot(xa[me.dp ^ o], w_all[me.dp ^ o].reshape(width, 2 * HQ), NN)
+
+    def project(source, table, at):
+        proj[:, at] = jnp.zeros((count, D), F32)
+        places = [0] + near(planes) + far(planes)
+        for o in places:
+            if o > 0:
+                source.relay(o)
+            source.arrive(o)
+            if o == near(planes)[-1]:
+                source.plane(far(planes))
+            proj[:, at] += dot(xa[me.dp ^ o], table[me.dp ^ o].reshape(width, D), NN)
+
+    project(weights, wkv_all, pl.ds(HQ, 2 * HK))
     tail_row = gains_row[:, 2 * D : 2 * D + 128]
     gain_q, gain_k = column_of(tail_row, 0), column_of(tail_row, HEAD_DIM)
     cosine, sine = cos_ref[...], sin_ref[...]
@@ -439,19 +481,23 @@
     def _():
         c_copy(0).start()
 
+    pass_first.step(2)
+    project(queries, wq_all, pl.ds(0, HQ))
     outputs.first()
-    passing.step(2)
     for h in range(0, HEADS, 4):
         q_s[pl.ds(h * HEAD_DIM, 4 * HEAD_DIM), :] = (four_raw(h) * HEAD_DIM ** (-0.5)).astype(BF)
     keep(q_s, q_any)
     keep(unit_s, unit_any)
     keep(recip_s, recip_any)
-    keep(w_all, wqkv_any)
+    keep(wq_all, wq_any)
+    keep(wkv_all, wkv_any)
+    outputs.plane(far(planes))
     shares = []
     for o in range(1, planes):
-        share = remote(og_ref, og_all.at[o], ps.at[0, o], ps.at[1, o], me.across(o))
+        share = remote(og_ref, ogs.at[o], ps.at[0, o], ps.at[1, o], me.across(o))
         share.start()
         shares.append(share)
+    pass_first.step(3)
     accum[...] = jnp.zeros_like(accum)
     sums[...] = jnp.zeros_like(sums)
 
@@ -496,8 +542,8 @@
         def _():
             visit(2 * k)
 
-    if depth > 2:
-        passing.step(3)
+    a2a_wait(1)
+    pass_second.step(1)
     for i in range(half):
         @pl.when(me.z - i - 1 + me.core >= 0)
         def _():
@@ -519,142 +565,46 @@
     mixed = tok_ref[...].astype(F32) + dot(o_out[...].T, wo_all[...].reshape(HQ, D), NN)
     mixed_out[...] = mixed
     unit, _ = unit_of(mixed, 1)
-    hn_out[...] = (unit * gains_out[:, D : 2 * D]).astype(BF)
+    hns[0] = (unit * gains_out[:, D : 2 * D]).astype(BF)
+
+    def hn_copy(o):
+        return remote(hns.at[0], hns.at[o], hsem.at[0, o], hsem.at[1, o], me.across(o))
+
+    def gn_copy(o):
+        return remote(send_gn.at[o - 1], recv_gn.at[o - 1], nsem.at[0, o], nsem.at[1, o], me.across(o))
+
+    def spill_copy(o, back):
+        ends = (spill_any.at[o], proj) if back else (proj, spill_any.at[o])
+        return pltpu.make_async_copy(*ends, ssem.at[0])
+
+    def parts_copy(o):
+        return pltpu.make_async_copy(part_s, parts_any.at[o], psem.at[0])
+
+    for o in near(planes):
+        hn_copy(o).start()
     for s in range(4, depth + 1):
-        passing.step(s)
-    passing.finish()
-
-    for i in range(half):
-        @pl.when(me.z - i - me.core >= 0)
-        def _():
-            c_copy(i).wait_send()
-
-    for k in range(1, half + 1):
-        @pl.when(me.z + k < depth)
-        def _():
-            z_copy(k).wait_send()
-
-    for o in range(1, planes):
-        a2a_copy(o).wait_send()
-    for share in shares:
-        share.wait()
-    gains.finish()
-    weights.finish()
-    outputs.finish()
+        pass_first.step(s)
+    pass_first.arrive()
     own_og.wait()
-    for copy in kept:
-        copy.wait()
-
-
-def ahead(tokens, cosine, sine, lower, gains_block, w_qkv, w_output, w_gate_up, w_down, cotangent, n_gains, planes, depth, turns, collective_id):
-    half = turns // 2
-    count = tokens.shape[0]
-    rows = w_qkv.shape[0]
-    full = w_down.shape[1] // planes
-    shapes = [
-        ((HQ, count), BF),
-        ((turns + 1, count, 2 * HK), BF),
-        ((planes, depth, 2, rows, 2 * HQ), BF),
-        ((D, count), BF),
-        ((HQ + HK, count), F32),
-        (((HEADS + KV_HEADS) // 4, 4, count), F32),
-        ((planes, count, D), BF),
-        ((planes, depth, 2, rows, D), BF),
-        ((depth * 2, planes, 3, rows, full), BF),
-        ((1, planes * depth * 2 * n_gains), F32),
-        ((HQ, count), BF),
-        ((GROUPS, 4, count), F32),
-        ((count, D), F32),
-        ((count, D), BF),
-    ]
-    return pl.pallas_call(
-        functools.partial(ahead_kernel, planes, depth, turns, n_gains),
-        out_shape=tuple(jax.ShapeDtypeStruct(s, k) for s, k in shapes),
-        in_specs=[VMEM] * 9 + [ANY],
-        out_specs=(ANY,) * 9 + (VMEM,) * 5,
-        scratch_shapes=[pltpu.VMEM(*shapes[i]) for i in (0, 1, 2, 3, 4, 5, 7)]
-        + [
-            pltpu.VMEM((planes, 3, rows, full), BF),
-            pltpu.VMEM((planes, depth, 2, 8, 128), F32),
-            pltpu.VMEM((planes, count, D // planes), BF),
-            pltpu.VMEM((count, D), F32),
-            pltpu.VMEM((count, 2 * HQ), F32),
-            pltpu.VMEM((count, count), F32),
-            pltpu.VMEM((HQ, count), F32),
-            pltpu.VMEM((GROUPS, 4, count), F32),
-            DMA((2,)),
-            DMA((8,)),
-            DMA((2, half + 1)),
-            DMA((2, half)),
-            DMA((2, planes)),
-            DMA((2, planes)),
-            DMA((8, depth + 1)),
-        ]
-        + spread_sems(planes, depth) * 3,
-        compiler_params=params(collective_id),
-        cost_estimate=pl.CostEstimate(flops=40 << 30, bytes_accessed=8 << 20, transcendentals=0),
-    )(tokens, cosine, sine, lower, gains_block, w_qkv, w_output, w_gate_up, w_down, cotangent)
-
-
-def ffn_kernel(
-    planes, depth, hn_ref, og_ref, w_any, gn_out, parts_out, grads_out,
-    w, hns, hnt, ogt, mid, pair, send_gn, recv_gn, own_gn, stage, wsem, hsem, gsem, osem,
-):
-    me = Place(planes, depth)
-    count, width = hn_ref.shape
-    full = w.shape[2]
-    ctxs, dps, rows = w_any.shape[0], w_any.shape[1], w_any.shape[3]
-    chunk = 384 if full % 384 == 0 else full
-
-    def w_copy(i, m):
-        c, d = i // dps, i % dps
-        return pltpu.make_async_copy(
-            w_any.at[c, d, m], w.at[m, pl.ds((d * ctxs + c) * rows, rows), :], wsem.at[m, i]
-        )
-
-    def load(i, carry):
-        for m in range(3):
-            w_copy(i, m).start()
-        return carry
-
-    lax.fori_loop(0, ctxs * dps, load, 0)
-    greet(me.plane())
-
-    def hn_copy(o):
-        return remote(hn_ref, hns.at[o], hsem.at[0, o], hsem.at[1, o], me.across(o))
-
-    def gn_copy(o):
-        return remote(send_gn.at[o], recv_gn.at[o], gsem.at[0, o], gsem.at[1, o], me.across(o))
-
-    near = [o for o in range(1, planes) if o & (o - 1) == 0]
-    far = [o for o in range(1, planes) if o & (o - 1) != 0]
-    for o in near:
-        hn_copy(o).start()
-    hns[0] = hn_ref[...]
-
-    def loaded(i, carry):
-        for m in range(3):
-            w_copy(i, m).wait()
-        return carry
-
-    lax.fori_loop(0, ctxs * dps, loaded, 0)
-
-    def block(o, carry):
-        @pl.when(o > 0)
-        def _():
-            hn_copy(o).wait_recv()
-
-        hn = hns[o]
-        og = og_ref[o]
-        at = pl.ds(pl.multiple_of(o * count, 128), count)
-        hnt[:, at] = hn.T
-        ogt[:, at] = og.T
-        own_gn[0] = jnp.zeros((count, width), F32)
-        own_gn[1] = jnp.zeros((count, width), F32)
-
-        def part(j, inner):
-            cols = pl.ds(pl.multiple_of(j * chunk, 128), chunk)
-            w_gate, w_up, w_down = w[0, :, cols], w[1, :, cols], w[2, :, cols]
+
+    def ffn_part(part):
+        w, f = (wa, wb)[part], halves[part]
+
+        def block(o, carry):
+            if part == 0:
+                @pl.when(o > 0)
+                def _():
+                    hn_copy(o).wait_recv()
+                    remote(og_ref, ogs.at[o], ps.at[0, o], ps.at[1, o], me.across(o)).wait_recv()
+            else:
+                spill_copy(o, True).start()
+
+            hn, og = hns[o], ogs[o]
+            at = pl.ds(pl.multiple_of(o * count, 128), count)
+            if part == 0:
+                hnt[:, at] = hn.T
+                ogt[:, at] = og.T
+            w_gate, w_up, w_down = (w[m].reshape(D, f) for m in range(3))
             gate = dot(hn, w_gate, NN)
             upper = dot(hn, w_up, NN)
             sigma = 1.0 / (1.0 + jnp.exp(-gate))
@@ -663,103 +613,209 @@
             gmid = dot(og, w_down, NN)
             ggate = (gmid * upper * sigma * (1.0 + gate * (1.0 - sigma))).astype(BF)
             gupper = (gmid * active).astype(BF)
-            mid[at, cols] = middle
-            pair[0, at, cols] = ggate
-            pair[1, at, cols] = gupper
-            own_gn[0] += dot(ggate, w_gate, NT) + dot(gupper, w_up, NT)
-            own_gn[1] += dot(middle, w_down, NT)
-            return inner
-
-        lax.fori_loop(0, full // chunk, part, 0)
-        parts_out[o] = own_gn[1].astype(BF)
-
-        @pl.when(o > 0)
-        def _():
-            send_gn[o] = own_gn[0].astype(BF)
-            gn_copy(o).start()
-
-        @pl.when(o == 0)
-        def _():
-            gn_out[...] = own_gn[0]
-            for other in far:
-                hn_copy(other).start()
-
-        return carry
-
-    lax.fori_loop(0, planes, block, 0)
-
-    strip = ctxs * rows
-
-    def out_copy(m, d):
-        return pltpu.make_async_copy(stage.at[m], grads_out.at[:, d, m], osem.at[m])
-
-    def weight_grads(d, carry):
-        left = pl.ds(pl.multiple_of(d * strip, 128), strip)
-        for m in (2, 0, 1):
-            @pl.when(d > 0)
-            def _():
-                out_copy(m, d - 1).wait()
-
-            if m == 2:
-                total = dot(ogt[left, :], mid[...], NN)
+            mid[at, :f] = middle
+            pair[0, at, :f] = ggate
+            pair[1, at, :f] = gupper
+            gn = dot(ggate, w_gate, NT) + dot(gupper, w_up, NT)
+            out = dot(middle, w_down, NT)
+            if part == 0:
+                @pl.when(o > 0)
+                def _():
+                    spill_copy(o - 1, False).wait()
+
+                proj[:, :D] = gn
+                proj[:, D:] = out
+                spill_copy(o, False).start()
+
+                @pl.when(o == 0)
+                def _():
+                    for other in far(planes):
+                        hn_copy(other).start()
+                    pass_second.step(2)
+
+                @pl.when(o == planes // 2)
+                def _():
+                    pass_second.step(3)
             else:
-                total = dot(hnt[left, :], pair[m], NN)
-            stage[m] = total.astype(BF).reshape(ctxs, rows, full)
-            out_copy(m, d).start()
-        return carry
-
-    lax.fori_loop(0, dps, weight_grads, 0)
-    for m in range(3):
-        out_copy(m, dps - 1).wait()
+                spill_copy(o, True).wait()
+                gn = gn + proj[:, :D]
+                out = out + proj[:, D:]
+
+                @pl.when(o > 0)
+                def _():
+                    parts_copy(o - 1).wait()
+                    send_gn[o - 1] = gn.astype(BF)
+                    gn_copy(o).start()
+
+                @pl.when(o == 0)
+                def _():
+                    gn_out[...] = gn
+                    fold.second()
+                    fold.step(0)
+
+                @pl.when(o == planes // 2)
+                def _():
+                    fold.step(1)
+
+                part_s[...] = out.astype(BF)
+                parts_copy(o).start()
+            return carry
+
+        lax.fori_loop(0, planes, block, 0)
+        if part == 0:
+            spill_copy(planes - 1, False).wait()
+        else:
+            parts_copy(planes - 1).wait()
+        strip = D // planes
+        grads = (grads_a, grads_b)[part]
+
+        def out_copy(m, d):
+            return pltpu.make_async_copy(stage.at[m, :, :, :f], grads.at[:, d, m], stsem.at[m])
+
+        def weight_grads(d, carry):
+            left = pl.ds(pl.multiple_of(d * strip, 128), strip)
+            for m in (2, 0, 1):
+                @pl.when(d > 0)
+                def _():
+                    out_copy(m, d - 1).wait()
+
+                if m == 2:
+                    total = dot(ogt[left, :], mid[:, :f], NN)
+                else:
+                    total = dot(hnt[left, :], pair[m, :, :f], NN)
+                stage[m, :, :, :f] = total.astype(BF).reshape(depth * 2, rows, f)
+                out_copy(m, d).start()
+            return carry
+
+        lax.fori_loop(0, planes, weight_grads, 0)
+        for m in range(3):
+            out_copy(m, planes - 1).wait()
+
+    ffn_part(0)
+    fold.first()
+    for s in range(4, depth + 1):
+        pass_second.step(s)
+    pass_second.arrive()
+    ffn_part(1)
     total = gn_out[...]
     for o in range(1, planes):
         gn_copy(o).wait_recv()
-        total = total + recv_gn[o].astype(F32)
+        total = total + recv_gn[o - 1].astype(F32)
     gn_out[...] = total
+    fold.settle(EARLY - 1)
+    keep(mine, mine_any)
+    pass_first.finish()
+    pass_second.finish()
+    fold.finish(True, range(EARLY))
     for o in range(1, planes):
         gn_copy(o).wait_send()
         hn_copy(o).wait_send()
 
-
-def ffn(hn, og_all, w_all, planes, depth, collective_id):
-    count, width = hn.shape
-    ctxs, dps, _, rows, full = w_all.shape
-    tokens = planes * count
-    flops = 18 * tokens * width * full
+    for i in range(half):
+        @pl.when(me.z - i - me.core >= 0)
+        def _():
+            c_copy(i).wait_send()
+
+    for k in range(1, half + 1):
+        @pl.when(me.z + k < depth)
+        def _():
+            z_copy(k).wait_send()
+
+    for o in range(1, planes):
+        a2a_copy(0, o).wait_send()
+        a2a_copy(1, o).wait_send()
+    for share in shares:
+        share.wait_send()
+    gains.finish()
+    queries.finish()
+    weights.finish()
+    outputs.finish()
+    for copy in kept:
+        copy.wait()
+
+
+def fore(tokens, cosine, sine, lower, gains_block, w_qkv, w_output, w_gate_up, w_down, cotangent, n_gains, planes, depth, turns, collective_id):
+    half = turns // 2
+    count = tokens.shape[0]
+    rows = w_qkv.shape[0]
+    first, second = split(w_down.shape[1] // planes)
+    devices = planes * depth * 2
+    everyone = (planes, depth, 2, rows)
+    shapes = [
+        ((HQ, count), BF),
+        ((turns + 1, count, 2 * HK), BF),
+        (everyone + (HQ,), BF),
+        (everyone + (2 * HK,), BF),
+        ((D, count), BF),
+        ((HQ + HK, count), F32),
+        (((HEADS + KV_HEADS) // 4, 4, count), F32),
+        (everyone + (D,), BF),
+        ((planes, count, D), BF),
+        ((planes, count, 2 * D), F32),
+        ((depth * 2, planes, 3, rows, first), BF),
+        ((depth * 2, planes, 3, rows, second), BF),
+        ((depth, planes, 3, rows, first), BF),
+        ((1, devices * n_gains), F32),
+        ((HQ, count), BF),
+        ((GROUPS, 4, count), F32),
+        ((count, D), F32),
+        ((count, D), F32),
+    ]
+    flops = 18 * planes * count * D * (first + second)
     return pl.pallas_call(
-        functools.partial(ffn_kernel, planes, depth),
-        out_shape=(
-            jax.ShapeDtypeStruct((count, width), F32),
-            jax.ShapeDtypeStruct((planes, count, width), BF),
-            jax.ShapeDtypeStruct((ctxs, dps, 3, rows, full), BF),
-        ),
-        in_specs=[VMEM, VMEM, ANY],
-        out_specs=(VMEM, VMEM, ANY),
-        scratch_shapes=[
-            pltpu.VMEM((3, width, full), BF),
-            pltpu.VMEM((planes, count, width), BF),
-            pltpu.VMEM((width, tokens), BF),
-            pltpu.VMEM((width, tokens), BF),
-            pltpu.VMEM((tokens, full), BF),
-            pltpu.VMEM((2, tokens, full), BF),
-            pltpu.VMEM((planes, count, width), BF),
-            pltpu.VMEM((planes, count, width), BF),
-            pltpu.VMEM((2, count, width), F32),
-            pltpu.VMEM((3, ctxs, rows, full), BF),
-            DMA((3, ctxs * dps)),
+        functools.partial(fore_kernel, planes, depth, turns, n_gains),
+        out_shape=tuple(jax.ShapeDtypeStruct(s, k) for s, k in shapes),
+        in_specs=[VMEM] * 9 + [ANY],
+        out_specs=(ANY,) * 13 + (VMEM,) * 5,
+        scratch_shapes=[pltpu.VMEM(*shape) for shape in shapes[:8]]
+        + [
+            pltpu.VMEM((planes, 3, rows, first), BF),
+            pltpu.VMEM((planes, 3, rows, second), BF),
+            pltpu.VMEM((planes, depth, 2, 8, 128), F32),
+            pltpu.VMEM((planes, count, D // planes), BF),
+            pltpu.VMEM((count, 2 * HQ), F32),
+            pltpu.VMEM((count, count), F32),
+            pltpu.VMEM((HQ, count), F32),
+            pltpu.VMEM((GROUPS, 4, count), F32),
+            pltpu.VMEM((3, planes, depth * 2, rows, first), BF),
+            pltpu.VMEM((3, planes, depth * 2, rows, second), BF),
+            pltpu.VMEM((planes, count, D), BF),
+            pltpu.VMEM((planes, count, D), BF),
+            pltpu.VMEM((D, planes * count), BF),
+            pltpu.VMEM((D, planes * count), BF),
+            pltpu.VMEM((planes * count, max(first, second)), BF),
+            pltpu.VMEM((2, planes * count, max(first, second)), BF),
+            pltpu.VMEM((planes - 1, count, D), BF),
+            pltpu.VMEM((planes - 1, count, D), BF),
+            pltpu.VMEM((count, D), BF),
+            pltpu.VMEM((3, depth * 2, rows, max(first, second)), BF),
+            pltpu.VMEM((depth, planes, 3, rows, first), BF),
+            DMA((2,)),
+            DMA((9,)),
+            DMA((2, half + 1)),
+            DMA((2, half)),
             DMA((2, planes)),
             DMA((2, planes)),
+            DMA((2, planes)),
+            DMA((8, depth + 1)),
+            DMA((8, depth + 1)),
+            DMA((2, planes)),
+            DMA((2, planes)),
+            DMA((1,)),
+            DMA((1,)),
             DMA((3,)),
-        ],
+        ]
+        + spread_sems(planes, depth) * 4
+        + fold_scratch(planes, depth, rows, first),
         compiler_params=params(collective_id),
-        cost_estimate=pl.CostEstimate(flops=flops, bytes_accessed=20 << 20, transcendentals=0),
-    )(hn, og_all, w_all)
+        cost_estimate=pl.CostEstimate(flops=flops, bytes_accessed=30 << 20, transcendentals=0),
+    )(tokens, cosine, sine, lower, gains_block, w_qkv, w_output, w_gate_up, w_down, cotangent)
 
 
 class Fold:
-    def __init__(self, me, g_any, scratch):
-        self.me, self.g = me, g_any
-        self.mine, self.other, self.from_line, self.ready, self.landed, self.sems, self.psems = scratch
+    def __init__(self, me, g_any, mine, scratch):
+        self.me, self.g, self.mine = me, g_any, mine
+        self.other, self.from_line, self.sems = scratch
 
     def own_copy(self, z):
         return pltpu.make_async_copy(
@@ -772,13 +828,10 @@
             self.g.at[z * 2 + 1 - me.core], self.other.at[z], self.sems.at[1, z], self.sems.at[2, z], me.sibling()
         )
 
-    def start(self):
-        for z in range(self.me.depth):
-            self.own_copy(z).start()
-
     def first(self):
         for z in range(self.me.depth):
             self.core_copy(z).start()
+            self.own_copy(z).start()
 
     def add(self, total, term):
         def plane(d, carry):
@@ -793,131 +846,144 @@
             self.core_copy(z).wait_recv()
             self.add(self.mine.at[z], self.other.at[z])
 
-    def target(self, k, down):
-        me = self.me
-        return k - (me.depth - 1) + me.z if down else me.depth - 1 - k + me.z
+    def target(self, z, k, down):
+        return k - (self.me.depth - 1) + z if down else self.me.depth - 1 - k + z
 
     def sends(self, k, down):
         me = self.me
-        return self.target(k, down) >= 0 if down else me.z <= k
+        return self.target(me.z, k, down) >= 0 if down else me.z <= k
+
+    def slot(self, t, k, down):
+        return self.me.depth if k == self.me.depth - 2 and not down else t
 
     def copy(self, k, down):
         me = self.me
-        t = self.target(k, down)
-        slot = me.depth if k == me.depth - 2 and not down else t
+        t = self.target(me.z, k, down)
         kind = 5 if down else 3
         return remote(
-            self.mine.at[t], self.from_line.at[slot], self.sems.at[kind, k], self.sems.at[kind + 1, k],
+            self.mine.at[t], self.from_line.at[self.slot(t, k, down)], self.sems.at[kind, k], self.sems.at[kind + 1, k],
             me.along(me.z - 1 if down else me.z + 1),
         )
 
-    def arrived(self, k, slot, down):
-        block = self.from_line.at[slot]
-        kind = 5 if down else 3
-        remote(block, block, self.sems.at[kind, k], self.sems.at[kind + 1, k], self.me.sibling()).wait_recv()
-
-    def step(self, k):
-        me = self.me
+    def send(self, k):
         for down in (False, True):
-            edge = me.z == me.depth - 1 if down else me.z == 0
-
             @pl.when(self.sends(k, down))
             def _():
-                t = self.target(k, down)
-                if k > 0:
-                    @pl.when(jnp.logical_not(edge))
-                    def _():
-                        self.arrived(k - 1, t, down)
-                        self.add(self.mine.at[t], self.from_line.at[t])
-
                 self.copy(k, down).start()
 
-    def total(self):
-        me = self.me
-        k = me.depth - 2
-
-        @pl.when(me.z < me.depth - 1)
-        def _():
-            self.arrived(k, me.z, True)
-            self.add(self.mine.at[me.z], self.from_line.at[me.z])
-
-        @pl.when(me.z > 0)
-        def _():
-            self.arrived(k, me.depth, False)
-            self.add(self.mine.at[me.z], self.from_line.at[me.depth])
-
-        self.ready[...] = self.mine[me.z]
-        for o in range(1, me.planes):
-            self.plane_copy(o).start()
-
-    def plane_copy(self, o):
-        me = self.me
-        return remote(
-            self.ready.at[me.dp ^ o], self.landed.at[me.dp], self.psems.at[0, o], self.psems.at[1, o], me.across(o)
-        )
-
-    def last(self):
-        me = self.me
-        self.landed[me.dp] = self.ready[me.dp]
-        for o in range(1, me.planes):
-            block = self.landed.at[me.dp ^ o]
-            remote(block, block, self.psems.at[0, o], self.psems.at[1, o], me.across(o)).wait_recv()
-
-    def finish(self):
-        me = self.me
-        for z in range(me.depth):
-            self.core_copy(z).wait_send()
-        for k in range(me.depth - 1):
+    def settle(self, k):
+        me = self.me
+        for down in (False, True):
+            t = self.target(me.z + 1 if down else me.z - 1, k, down)
+            comes = (me.z < me.depth - 1) & (t >= 0) if down else (me.z > 0) & (me.z - 1 <= k)
+
+            @pl.when(comes)
+            def _():
+                block = self.from_line.at[self.slot(t, k, down)]
+                kind = 5 if down else 3
+                remote(
+                    block, block, self.sems.at[kind, k], self.sems.at[kind + 1, k], me.sibling()
+                ).wait_recv()
+                self.add(self.mine.at[t], block)
+
+    def step(self, k):
+        if k > 0:
+            self.settle(k - 1)
+        self.send(k)
+
+    def finish(self, first, steps):
+        if first:
+            for z in range(self.me.depth):
+                self.core_copy(z).wait_send()
+        for k in steps:
             for down in (False, True):
                 @pl.when(self.sends(k, down))
                 def _():
                     self.copy(k, down).wait_send()
+
+
+class Swap:
+    def __init__(self, me, ready, landed, sems):
+        self.me, self.ready, self.landed, self.sems = me, ready, landed, sems
+
+    def copy(self, o):
+        me = self.me
+        return remote(
+            self.ready.at[me.dp ^ o], self.landed.at[me.dp], self.sems.at[0, o], self.sems.at[1, o], me.across(o)
+        )
+
+    def start(self, value):
+        self.ready[...] = value
+        for o in range(1, self.me.planes):
+            self.copy(o).start()
+
+    def last(self):
+        me = self.me
+        self.landed[me.dp] = self.ready[me.dp]
         for o in range(1, me.planes):
-            self.plane_copy(o).wait_send()
-
-
-FOLD = 7
+            block = self.landed.at[me.dp ^ o]
+            remote(block, block, self.sems.at[0, o], self.sems.at[1, o], me.across(o)).wait_recv()
+
+    def finish(self):
+        for o in range(1, self.me.planes):
+            self.copy(o).wait_send()
+
+
+FOLD = 3
 
 
 def fold_scratch(planes, depth, rows, full):
     block = (planes, 3, rows, full)
     return [
         pltpu.VMEM((depth,) + block, BF),
-        pltpu.VMEM((depth,) + block, BF),
         pltpu.VMEM((depth + 1,) + block, BF),
-        pltpu.VMEM(block, BF),
-        pltpu.VMEM(block, BF),
         DMA((7, depth)),
-        DMA((2, planes)),
     ]
+
+
+def split(full):
+    first = (full // 128 + 1) // 2 * 128
+    return (first, full - first)
+
+
+EARLY = 2
 
 
 def home_kernel(
     planes, depth, turns, n_gains,
     gn_ref, mixed_ref, og_ref, gains_ref, o_ref, lse_ref, q_ref, lower_ref, cos_ref, sin_ref, tok_ref,
-    wo_any, kv_any, parts_any, grads_any, unit_any, recip_any, w_any, xat_any,
+    wo_any, kv_any, parts_any, grads_b, mine_a, unit_any, recip_any, wq_any, wkv_any, xat_any,
     block_out, grad_out, shard_out, shard_qkv, gains_out, pair_out, down_out,
-    wo, kv, unit_s, recip_s, w_all, xat, own_part, gq, grad_kv, gmixed_s,
-    bias, gob, delta, gkv, from_core, from_z, from_plane, partial, gproj, partial_q, gains_p, *rest,
+    wo, kv, unit_s, recip_s, wq_all, wkv_all, xat, own_part, gq, grad_kv, gmixed_s,
+    bias, gob, delta, gkv, from_core, from_z, from_plane, partial, gproj, partial_q, partial_kv, gains_p, *rest,
 ):
     me = Place(planes, depth)
     collect = Collect(me, partial, rest[:COLLECT])
     collect_q = Collect(me, partial_q, rest[COLLECT : 2 * COLLECT])
-    small = Collect(me, gains_p, rest[2 * COLLECT : 3 * COLLECT])
-    fold = Fold(me, grads_any, rest[3 * COLLECT : 3 * COLLECT + FOLD])
-    cs, zs, ps, load = rest[3 * COLLECT + FOLD :]
+    collect_kv = Collect(me, partial_kv, rest[2 * COLLECT : 3 * COLLECT])
+    small = Collect(me, gains_p, rest[3 * COLLECT : 4 * COLLECT])
+    rest = rest[4 * COLLECT :]
+    mine_first, ready_first, landed_first, swap_first, mine_second, ready_second, landed_second, swap_second = rest[:8]
+    folds = (
+        Fold(me, None, mine_first, (None,) + rest[8:10]),
+        Fold(me, grads_b, mine_second, rest[10 : 10 + FOLD]),
+    )
+    swaps = (
+        Swap(me, ready_first, landed_first, swap_first),
+        Swap(me, ready_second, landed_second, swap_second),
+    )
+    cs, zs, ps, load = rest[10 + FOLD :]
     half = turns // 2
     count = gn_ref.shape[0]
-    sources = [wo_any, kv_any, unit_any, recip_any, w_any, xat_any, parts_any.at[0]]
-    places = [wo, kv, unit_s, recip_s, w_all, xat, own_part]
+    sources = [wo_any, kv_any, unit_any, recip_any, xat_any, parts_any.at[0], wq_any, wkv_any, mine_a]
+    places = [wo, kv, unit_s, recip_s, xat, own_part, wq_all, wkv_all, mine_first]
     loads = [pltpu.make_async_copy(a, b, load.at[i]) for i, (a, b) in enumerate(zip(sources, places))]
-    for copy in loads[:2]:
-        copy.start()
-    fold.start()
-    for copy in loads[2:]:
+    for copy in loads[8:] + loads[:8]:
         copy.start()
     greet(me.plane() + me.line() + [me.sibling()])
-    fold.first()
+    loads[8].wait()
+    folds[0].send(EARLY)
+    folds[1].first()
 
     def c_copy(i):
         return remote(gkv.at[2 * i + 1], from_core.at[i], cs.at[0, i], cs.at[1, i], me.sibling())
@@ -955,8 +1021,8 @@
         rows = o_ref[pl.ds(pl.multiple_of(d * half_rows, 128), half_rows), :]
         partial[d] = dot(rows, gmixed_b, NN).astype(BF).reshape(partial.shape[1:])
         collect.first(o)
-    fold.second()
-    fold.step(0)
+    folds[1].second()
+    folds[1].step(0)
     gq[...] = jnp.zeros_like(gq)
     loads[1].wait()
 
@@ -1014,23 +1080,8 @@
 
             z_copy(k).start()
 
-    for o in order:
-        collect.second(o)
-    if depth > 2:
-        fold.step(1)
     visit(0)
-    value_o = collect.third()
-    total = mixed_ref[...]
-    loads[6].wait()
-    total = total + own_part[...].astype(F32)
-    for o in range(1, planes):
-        p_copy(o).wait_recv()
-        total = total + from_plane[o - 1].astype(F32)
-    block_out[...] = total.astype(BF)
-    shard_out[...] = collect.last(value_o)
-    grad_kv[...] = gkv[0].astype(F32)
-
-    for i in (2, 3, 5, 4):
+    for i in (2, 3, 4):
         loads[i].wait()
     tail_row = gains_ref[:, 2 * D : 2 * D + 128]
     gain_q, gain_k = column_of(tail_row, 0), column_of(tail_row, HEAD_DIM)
@@ -1054,8 +1105,25 @@
             gained[kind] = gained[kind] + grad * unit
         gproj[:, pl.ds(h * HEAD_DIM, 4 * HEAD_DIM)] = jnp.concatenate(results, axis=0).T.astype(BF)
 
+    def gather_grads(columns, table, collected):
+        for o in order:
+            d = me.dp ^ o
+            rows = xat[pl.ds(pl.multiple_of(d * half_rows, 128), half_rows), :]
+            table[d] = dot(rows, gproj[:, columns], NN).astype(BF).reshape(table.shape[1:])
+            collected.first(o)
+            if o != order[0]:
+                collected.second(order[order.index(o) - 1])
+        collected.second(0)
+
+    for o in order:
+        collect.second(o)
     for h in range(0, HEADS, 4):
         four_grads(h)
+    gather_grads(pl.ds(0, HQ), partial_q, collect_q)
+    folds[1].step(1)
+    for k in range(EARLY + 1, depth - 1):
+        folds[0].step(k)
+    grad_kv[...] = gkv[0].astype(F32)
 
     @pl.when(me.core == 0)
     def _():
@@ -1071,22 +1139,22 @@
     for h in range(HEADS, HEADS + KV_HEADS, 4):
         four_grads(h)
     gproj[:, pl.ds(HQ + HK, HK)] = grad_kv[:, pl.ds(HK, HK)].astype(BF)
-    for o in order:
-        d = me.dp ^ o
-        rows = xat[pl.ds(pl.multiple_of(d * half_rows, 128), half_rows), :]
-        partial_q[d] = dot(rows, gproj[...], NN).astype(BF).reshape(partial_q.shape[1:])
-        collect_q.first(o)
-        if o != order[0]:
-            collect_q.second(order[order.index(o) - 1])
-    collect_q.second(0)
-    for k in range(2, depth - 1):
-        fold.step(k)
-    grad = dot(gproj[...], w_all[...].reshape(D, 2 * HQ), NT)
+    gather_grads(pl.ds(HQ, 2 * HK), partial_kv, collect_kv)
+    value_o = collect.third()
+    value_q = collect_q.third()
+    for i in (6, 7):
+        loads[i].wait()
+    grad = dot(gproj[:, :HQ], wq_all[...].reshape(D, HQ), NT)
+    grad = grad + dot(gproj[:, HQ:], wkv_all[...].reshape(D, 2 * HK), NT)
     unit, recip = unit_of(tok_ref[...].astype(F32), 1)
     scaled = grad * gains_ref[:, :D]
     inner = jnp.mean(scaled * unit, axis=1, keepdims=True)
     grad_out[...] = gmixed_s[...] + recip * (scaled - unit * inner)
     dga = jnp.sum(grad * unit, axis=0, keepdims=True)
+    for k in range(2, depth - 1):
+        folds[1].step(k)
+    folds[0].settle(depth - 2)
+    swaps[0].start(mine_first[me.z])
     lane = lax.broadcasted_iota(jnp.int32, (HEAD_DIM, 128), 1)
     entry = lax.broadcasted_iota(jnp.int32, (HEAD_DIM, 128), 0)
     sums = [jnp.sum(g, axis=1, keepdims=True) for g in gained]
@@ -1115,17 +1183,33 @@
         small.first(o)
     for o in order:
         small.second(o)
-    value = collect_q.third()
+    value_kv = collect_kv.third()
     little = small.third()
-    fold.total()
-    shard_qkv[...] = collect_q.last(value)
+    total = mixed_ref[...]
+    loads[5].wait()
+    total = total + own_part[...].astype(F32)
+    for o in range(1, planes):
+        p_copy(o).wait_recv()
+        total = total + from_plane[o - 1].astype(F32)
+    block_out[...] = total.astype(BF)
+    folds[1].settle(depth - 2)
+    swaps[1].start(mine_second[me.z])
+    shard_out[...] = collect.last(value_o)
+    shard_qkv[:, :HQ] = collect_q.last(value_q)
+    shard_qkv[:, HQ:] = collect_kv.last(value_kv)
     gains_out[...] = small.last(little)
-    fold.last()
-    full = fold.landed.shape[3]
-    for d in range(planes):
-        for m in range(2):
-            pair_out[:, (m * planes + d) * full : (m * planes + d + 1) * full] = fold.landed[d, m]
-        down_out[:, d * full : (d + 1) * full] = fold.landed[d, 2]
+    start = 0
+    full = landed_first.shape[3] + landed_second.shape[3]
+    for swap in swaps:
+        swap.last()
+        f = swap.landed.shape[3]
+        for d in range(planes):
+            for m in range(2):
+                at = (m * planes + d) * full + start
+                pair_out[:, at : at + f] = swap.landed[d, m]
+            at = d * full + start
+            down_out[:, at : at + f] = swap.landed[d, 2]
+        start = f
 
     for o in range(1, planes):
         p_copy(o).wait_send()
@@ -1139,16 +1223,21 @@
             z_copy(k).wait_send()
     collect.finish()
     collect_q.finish()
+    collect_kv.finish()
     small.finish()
-    fold.finish()
-
-
-def home(near, far, n_gains, planes, depth, turns, collective_id):
+    folds[0].finish(False, range(EARLY, depth - 1))
+    folds[1].finish(True, range(depth - 1))
+    for swap in swaps:
+        swap.finish()
+
+
+def home(first, second, n_gains, planes, depth, turns, collective_id):
     half = turns // 2
-    count = near[0].shape[0]
-    wo_all, kv_all, _, grads, unit, recip, w_all, xat = far
+    count = first[0].shape[0]
+    wo_all, kv_all, _, grads, mine, unit, recip, wq_all, wkv_all, xat = second
     rows = wo_all.shape[3]
-    full = grads.shape[4]
+    parts = (mine.shape[4], grads.shape[4])
+    full = sum(parts)
     return pl.pallas_call(
         functools.partial(home_kernel, planes, depth, turns, n_gains),
         out_shape=(
@@ -1160,9 +1249,9 @@
             jax.ShapeDtypeStruct((rows, 2 * planes * full), BF),
             jax.ShapeDtypeStruct((rows, planes * full), BF),
         ),
-        in_specs=[VMEM] * len(near) + [ANY] * len(far),
+        in_specs=[VMEM] * len(first) + [ANY] * len(second),
         out_specs=(VMEM,) * 7,
-        scratch_shapes=[pltpu.VMEM(a.shape, a.dtype) for a in (wo_all, kv_all, unit, recip, w_all, xat)]
+        scratch_shapes=[pltpu.VMEM(a.shape, a.dtype) for a in (wo_all, kv_all, unit, recip, wq_all, wkv_all, xat)]
         + [
             pltpu.VMEM((count, D), BF),
             pltpu.VMEM((HQ, count), F32),
@@ -1177,17 +1266,30 @@
             pltpu.VMEM((planes - 1, count, D), BF),
             pltpu.VMEM((planes, depth, 2, rows, D), BF),
             pltpu.VMEM((count, 2 * HQ), BF),
-            pltpu.VMEM((planes, depth, 2, rows, 2 * HQ), BF),
+            pltpu.VMEM((planes, depth, 2, rows, HQ), BF),
+            pltpu.VMEM((planes, depth, 2, rows, 2 * HK), BF),
             pltpu.VMEM((planes, depth, 2, 8, 128), F32),
         ]
         + collect_scratch(planes, depth, rows, D, BF)
-        + collect_scratch(planes, depth, rows, 2 * HQ, BF)
+        + collect_scratch(planes, depth, rows, HQ, BF)
+        + collect_scratch(planes, depth, rows, 2 * HK, BF)
         + collect_scratch(planes, depth, 8, 128, F32)
-        + fold_scratch(planes, depth, rows, full)
-        + [DMA((2, half)), DMA((2, half + 1)), DMA((2, planes)), DMA((7,))],
+        + [
+            scratch
+            for part in parts
+            for scratch in (
+                pltpu.VMEM((depth, planes, 3, rows, part), BF),
+                pltpu.VMEM((planes, 3, rows, part), BF),
+                pltpu.VMEM((planes, 3, rows, part), BF),
+                DMA((2, planes)),
+            )
+        ]
+        + fold_scratch(planes, depth, rows, parts[0])[1:]
+        + fold_scratch(planes, depth, rows, parts[1])
+        + [DMA((2, half)), DMA((2, half + 1)), DMA((2, planes)), DMA((9,))],
         compiler_params=params(collective_id),
         cost_estimate=pl.CostEstimate(flops=60 << 30, bytes_accessed=8 << 20, transcendentals=0),
-    )(*near, *far)
+    )(*first, *second)
 
 
 def per_device(
@@ -1214,7 +1316,6 @@
     depth = ctxs // 2
     turns = ctxs // 2
     rows = w_qkv.shape[0]
-    full = w_down.shape[1] // planes
     n_gains = norm_gains.shape[0]
     count = tokens_in.shape[0] * tokens_in.shape[1]
     tokens = tokens_in.reshape(count, D)
@@ -1225,20 +1326,16 @@
     cosine, sine = rope_tables(places)
     lower = (jnp.arange(count, dtype=jnp.int32) - places)[None, :]
     (
-        query, kv_all, qkv_all, xat, unit_heads, recip_heads, og_all, output_all, w_all,
-        gains_row, attn_t, lse, mixed, hn,
-    ) = ahead(
+        query, kv_all, wq_all, wkv_all, xat, unit_heads, recip_heads, output_all, parts, _, _, grads, mine,
+        gains_row, attn_t, lse, mixed, grad_normed,
+    ) = fore(
         tokens, cosine, sine, lower, gains_block, w_qkv, w_output, w_gate_up, w_down, cotangent,
         n_gains, planes, depth, turns, 0,
     )
-    w_used = w_all if rows % 16 == 0 else w_all.transpose(2, 1, 0, 3, 4).reshape(1, 1, 3, D, full)
-    grad_normed, parts, grads = ffn(hn, og_all, w_used, planes, depth, 1)
-    if rows % 16 != 0:
-        grads = grads.reshape(3, planes, ctxs, rows, full).transpose(2, 1, 0, 3, 4)
     block_out, input_grad, shard_output, shard_qkv, gains_tile, pair_b, down_b = home(
         (grad_normed, mixed, cotangent, gains_row, attn_t, lse, query, lower, cosine, sine, tokens),
-        (output_all, kv_all, parts, grads, unit_heads, recip_heads, qkv_all, xat),
-        n_gains, planes, depth, turns, 2,
+        (output_all, kv_all, parts, grads, mine, unit_heads, recip_heads, wq_all, wkv_all, xat),
+        n_gains, planes, depth, turns, 1,
     )
     shard_gains = gains_tile[0, :n_gains]
     shard_gate_up = pair_b.astype(F32)

time: 338 us -> 302 us (0.89)
  Pallas kernels: 319 us -> 280 us
    pallas_call x1, Pallas kernels: 167 us -> 112 us  [home(): pl.pallas_call(functools.partial(home_kernel, planes, depth, turns, n_gai...]
    pallas_call x2 -> x1, Pallas kernels: 152 us -> 168 us  [fore(): pl.pallas_call(functools.partial(fore_kernel, planes, depth, turns, n_gai...]
where the time goes in v4:
time: 302 us; the launch traced here: 299 us
  Pallas kernels  280 us (93%)
  other arithmetic  12.4 us (4%)
  local copies, waits for them, and re-layouts  5.37 us (2%)
    pallas_call x1, Pallas kernels, fore(): pl.pallas_call(functools.partial(fore_kernel, planes, depth, turns, n_gai...  168 us
    pallas_call x1, Pallas kernels, home(): pl.pallas_call(functools.partial(home_kernel, planes, depth, turns, n_gai...  112 us
    sub x5, other arithmetic, adam_step(): weight - rate * (first_hat / (jnp.sqrt(second_hat) + ADAM_EPS) + decay *...  8.95 us

profile of v4, /device:TPU:0, one launch (start us, length us, event | category | flops | bytes accessed | tf_op | source)
XLA Modules:
  0.0 299.1 jit_solution(13048880488438601668)
XLA Ops:
  0.7 0.7 convert_bitcast_fusion
  1.3 1.3 iota_subtract_fusion
  2.7 0.6 pad_convert_fusion.gain_ref
  3.2 0.8 multiply_sine_fusion
  4.1 168.5 %shard_map.345 = (bf16[1024,256]{1,0:T(8,128)(2,1)}, bf16[5,256,1024]{2,1,0:T(8,128)(2,1)}, bf16[4,4,2,32,1024]{4,3,2,1,0:T(8,128)(2,1)}, bf16[4,4,2,32,1024]{4,...) custom-call(bf16[256,1024]{1,0:T(8,128)(2,1)} %bitcast.13, ...), custom_call_target="tpu_custom_call" | custom-call | flops 21743271936 | bytes 31457280 | tf_op jit(solution)/shard_map/pallas_call | solution.py:765
  172.6 0.0 copy-start.18
  172.6 0.0 copy-start.19
  172.6 0.0 copy-start.20
  172.6 0.0 copy-start.15
  172.6 0.0 copy-start.16
  172.6 0.0 copy-start.17
  172.6 0.0 copy-start.12
  172.6 0.0 copy-start.13
  172.7 0.0 copy-start.14
  172.7 112.0 %shard_map.346 = (bf16[256,1024]{1,0:T(8,128)(2,1)}, f32[256,1024]{1,0:T(8,128)}, f32[32,1024]{1,0:T(8,128)}, f32[32,2048]{1,0:T(8,128)}, f32[8,128]{1,0:T(8,128...) custom-call(f32[256,1024]{1,0:T(8,128)} %get-tuple-element.45.gn_ref, f32[256,1024]{1,0:T(8,128)} %get-tuple-element.46.mixed_ref, ...), custom_call_target="tpu_custom_call" | custom-call | flops 64424509440 | bytes 8388608 | tf_op jit(solution)/shard_map/pallas_call | solution.py:1241
  284.7 0.0 copy-done.18
  284.7 0.0 copy-done.19
  284.7 0.0 copy-done.20
  284.7 1.2 multiply_subtract_fusion.4
  285.9 0.0 copy-done.15
  285.9 0.0 copy-done.16
  285.9 0.0 copy-done.17
  286.0 0.0 copy-start.5
  286.0 0.0 copy-start.6
  286.0 0.0 copy-start.7
  286.0 0.0 copy-start.11
  286.0 1.8 multiply_subtract_fusion.3
  287.8 0.0 copy-done.12
  287.8 0.0 copy-done.13
  287.8 0.0 copy-done.14
  287.9 1.9 multiply_subtract_fusion.2
  289.8 0.0 copy-done.6
  289.8 0.0 copy-start
  289.8 0.0 copy-start.1
  289.8 0.0 copy-start.2
  289.9 1.5 multiply_subtract_fusion.1
  291.4 0.1 copy-done
  291.5 0.8 copy-done.1
  292.3 0.4 copy-done.2
  292.7 0.1 copy-done.8
  292.8 2.4 multiply_subtract_fusion
  295.2 0.8 copy.44
  296.0 0.6 copy-done.4
  296.6 1.0 copy.45
  297.6 0.1 copy-done.3
  297.7 0.7 copy.46
  298.4 0.0 copy-done.9
  298.4 0.7 copy.47
  (10 shorter events, 0.0 us)
Async XLA Ops:
  172.6 112.1 %copy-start.18 = (f32[68]{0:T(128)S(1)}, f32[68]{0:T(128)}, u32[]{:S(2)}) copy-start(f32[68]{0:T(128)} %param.25) | copy-start | bytes 820
  172.6 112.1 %copy-start.19 = (f32[68]{0:T(128)S(1)}, f32[68]{0:T(128)}, u32[]{:S(2)}) copy-start(f32[68]{0:T(128)} %param.30) | copy-start | bytes 820
  172.6 112.1 %copy-start.20 = (f32[68]{0:T(128)S(1)}, f32[68]{0:T(128)}, u32[]{:S(2)}) copy-start(f32[68]{0:T(128)} %param.35) | copy-start | bytes 820
  172.6 113.4 %copy-start.15 = (f32[32,1024]{1,0:T(8,128)S(1)}, f32[32,1024]{1,0:T(8,128)}, u32[]{:S(2)}) copy-start(f32[32,1024]{1,0:T(8,128)} %wout_ref.1) | copy-start | bytes 393220
  172.6 113.3 %copy-start.16 = (f32[32,1024]{1,0:T(8,128)S(1)}, f32[32,1024]{1,0:T(8,128)}, u32[]{:S(2)}) copy-start(f32[32,1024]{1,0:T(8,128)} %param.27) | copy-start | bytes 393220
  172.6 113.3 %copy-start.17 = (f32[32,1024]{1,0:T(8,128)S(1)}, f32[32,1024]{1,0:T(8,128)}, u32[]{:S(2)}) copy-start(f32[32,1024]{1,0:T(8,128)} %param.32) | copy-start | bytes 393220
  172.6 115.2 %copy-start.12 = (f32[32,2048]{1,0:T(8,128)S(1)}, f32[32,2048]{1,0:T(8,128)}, u32[]{:S(2)}) copy-start(f32[32,2048]{1,0:T(8,128)} %wqkv_ref.1) | copy-start | bytes 786436
  172.6 115.2 %copy-start.13 = (f32[32,2048]{1,0:T(8,128)S(1)}, f32[32,2048]{1,0:T(8,128)}, u32[]{:S(2)}) copy-start(f32[32,2048]{1,0:T(8,128)} %param.26) | copy-start | bytes 786436
  172.7 115.2 %copy-start.14 = (f32[32,2048]{1,0:T(8,128)S(1)}, f32[32,2048]{1,0:T(8,128)}, u32[]{:S(2)}) copy-start(f32[32,2048]{1,0:T(8,128)} %param.31) | copy-start | bytes 786436
  286.0 3.8 %copy-start.5 = (f32[32,4608]{1,0:T(8,128)S(1)}, f32[32,4608]{1,0:T(8,128)}, u32[]{:S(2)}) copy-start(f32[32,4608]{1,0:T(8,128)} %wdown_ref.1) | copy-start | bytes 1769476
  286.0 3.8 %copy-start.6 = (f32[32,4608]{1,0:T(8,128)S(1)}, f32[32,4608]{1,0:T(8,128)}, u32[]{:S(2)}) copy-start(f32[32,4608]{1,0:T(8,128)} %param.29) | copy-start | bytes 1769476
  286.0 3.8 %copy-start.7 = (f32[32,4608]{1,0:T(8,128)S(1)}, f32[32,4608]{1,0:T(8,128)}, u32[]{:S(2)}) copy-start(f32[32,4608]{1,0:T(8,128)} %param.34) | copy-start | bytes 1769476
  286.0 3.8 %copy-start.11 = (bf16[32,4608]{1,0:T(8,128)(2,1)S(1)}, bf16[32,4608]{1,0:T(8,128)(2,1)}, u32[]{:S(2)}) copy-start(bf16[32,4608]{1,0:T(8,128)(2,1)} %get-tuple-element.66) | copy-start | bytes 884740
  289.8 1.7 copy-start
  289.8 2.5 copy-start.1
  289.8 2.8 copy-start.2
  289.9 2.9 copy-start.8
  292.8 2.4 copy-start.10
  295.2 1.4 copy-start.4
  296.6 1.1 copy-start.3
  296.6 1.8 copy-start.9

commit v5 on v4

--- a/solution.py
+++ b/solution.py
@@ -116,8 +116,9 @@
 
 
 class Spread:
-    def __init__(self, me, g_ref, line_sems, sems):
+    def __init__(self, me, g_ref, line_sems, sems, halves=True):
         self.me, self.g, self.line_sems, self.sems = me, g_ref, line_sems, sems
+        self.by_halves = halves and me.planes == 4
         self.sent = []
 
     def push(self, src, dst, kind, o, device):
@@ -153,9 +154,24 @@
         for o in places:
             self.push(self.mine(0, me.core), self.mine(0, me.core), 0, o, me.across(o))
 
+    def part(self, o, number):
+        half = self.me.depth // 2
+        return self.g.at[self.me.dp ^ o, pl.ds(number * half, half), self.me.core]
+
     def relay(self, o):
         block = self.mine(o, self.me.core)
-        remote(block, block, self.sems.at[0, o], self.sems.at[1, o], self.me.sibling()).wait_recv()
+        if self.by_halves and o == 3:
+            for number in range(2):
+                piece = self.part(o, number)
+                kind = 4 + 2 * number
+                remote(
+                    piece, piece, self.sems.at[kind, o], self.sems.at[kind + 1, o], self.me.sibling()
+                ).wait_recv()
+        else:
+            remote(block, block, self.sems.at[0, o], self.sems.at[1, o], self.me.sibling()).wait_recv()
+        if self.by_halves and o < 3:
+            piece = self.part(o, o - 1)
+            self.push(piece, piece, 2 + 2 * o, 3, self.me.across(3 - o))
         self.push(block, block, 2, o, self.me.sibling())
 
     def arrive(self, o):
@@ -168,7 +184,7 @@
 
 
 def spread_sems(planes, depth):
-    return [DMA((2, depth)), DMA((4, planes))]
+    return [DMA((2, depth)), DMA((8, planes))]
 
 
 class Collect:
@@ -345,7 +361,7 @@
     gains_out, o_out, lse_out, mixed_out, gn_out,
     q_s, kv_all, wq_all, wkv_all, xat, unit_s, recip_s, wo_all, blocks_a, blocks_b, gains_g, xa, proj, bias, accum, sums,
     wa, wb, hns, ogs, hnt, ogt, mid, pair, send_gn, recv_gn, part_s, stage, mine,
-    own_sem, keep_sem, zs, cs, ps, a2a_a, a2a_b, pass_a, pass_b, hsem, nsem, psem, ssem, stsem,
+    own_sem, keep_sem, zs, cs, ps, a2a_a, a2a_b, pass_a, pass_b, hsem, nsem, psem, ssem, stsem, og_halves, hn_halves, dsem,
     glsem, gsem, qlsem, qsem, wlsem, wsem, olsem, osem, *fold_rest,
 ):
     me = Place(planes, depth)
@@ -355,7 +371,7 @@
     rows = wqkv_ref.shape[0]
     halves = (blocks_a.shape[3], blocks_b.shape[3])
     full = sum(halves)
-    gains = Spread(me, gains_g, glsem, gsem)
+    gains = Spread(me, gains_g, glsem, gsem, False)
     queries = Spread(me, wq_all, qlsem, qsem)
     weights = Spread(me, wkv_all, wlsem, wsem)
     outputs = Spread(me, wo_all, olsem, osem)
@@ -440,7 +456,7 @@
             if o > 0:
                 source.relay(o)
             source.arrive(o)
-            if o == near(planes)[-1]:
+            if o == near(planes)[-1] and planes != 4:
                 source.plane(far(planes))
             proj[:, at] += dot(xa[me.dp ^ o], table[me.dp ^ o].reshape(width, D), NN)
 
@@ -464,6 +480,12 @@
         kv_all[0, :, pl.ds((h - HEADS) * HEAD_DIM, 4 * HEAD_DIM)] = four_raw(h).T.astype(BF)
     kv_all[0, :, pl.ds(HK, HK)] = proj[:, HQ + HK :].astype(BF)
 
+    def half_copy(slots, sems, o):
+        rows = pl.ds((o - 1) * (count // 2), count // 2)
+        return remote(
+            slots.at[o, rows], slots.at[3, rows], sems.at[0, o], sems.at[1, o], me.across(3 - o)
+        )
+
     def z_copy(k):
         return remote(kv_all.at[0], kv_all.at[2 * k], zs.at[0, k], zs.at[1, k], me.along(me.ahead(k)))
 
@@ -481,7 +503,6 @@
     def _():
         c_copy(0).start()
 
-    pass_first.step(2)
     project(queries, wq_all, pl.ds(0, HQ))
     outputs.first()
     for h in range(0, HEADS, 4):
@@ -491,13 +512,14 @@
     keep(recip_s, recip_any)
     keep(wq_all, wq_any)
     keep(wkv_all, wkv_any)
-    outputs.plane(far(planes))
+    square = planes == 4
+    if not square:
+        outputs.plane(far(planes))
     shares = []
-    for o in range(1, planes):
+    for o in near(planes) if square else range(1, planes):
         share = remote(og_ref, ogs.at[o], ps.at[0, o], ps.at[1, o], me.across(o))
         share.start()
         shares.append(share)
-    pass_first.step(3)
     accum[...] = jnp.zeros_like(accum)
     sums[...] = jnp.zeros_like(sums)
 
@@ -542,17 +564,23 @@
         def _():
             visit(2 * k)
 
-    a2a_wait(1)
-    pass_second.step(1)
+    pass_first.step(2)
     for i in range(half):
         @pl.when(me.z - i - 1 + me.core >= 0)
         def _():
             c_copy(i).wait_recv()
             visit(2 * i + 1)
 
+    pass_first.step(3)
+    a2a_wait(1)
+    pass_second.step(1)
     keep(kv_all, kv_any)
     for o in range(1, planes):
         outputs.relay(o)
+    if square:
+        for o in (1, 2):
+            remote(og_ref, ogs.at[o], ps.at[0, o], ps.at[1, o], me.across(o)).wait_recv()
+            half_copy(ogs, og_halves, o).start()
     for t in range(GROUPS):
         total = sums[t]
         lse_out[t] = jnp.log(total)
@@ -573,6 +601,15 @@
     def gn_copy(o):
         return remote(send_gn.at[o - 1], recv_gn.at[o - 1], nsem.at[0, o], nsem.at[1, o], me.across(o))
 
+    def diagonal_rows(other):
+        return pl.ds((other - 1) * (count // 2), count // 2)
+
+    def diagonal_copy(other):
+        rows = diagonal_rows(other)
+        return remote(
+            send_gn.at[2, rows], recv_gn.at[2, rows], dsem.at[0, other], dsem.at[1, other], me.across(other)
+        )
+
     def spill_copy(o, back):
         ends = (spill_any.at[o], proj) if back else (proj, spill_any.at[o])
         return pltpu.make_async_copy(*ends, ssem.at[0])
@@ -590,12 +627,26 @@
     def ffn_part(part):
         w, f = (wa, wb)[part], halves[part]
 
-        def block(o, carry):
+        def block(i, carry):
+            o = i if part == 0 else planes - 1 - i
             if part == 0:
-                @pl.when(o > 0)
-                def _():
-                    hn_copy(o).wait_recv()
-                    remote(og_ref, ogs.at[o], ps.at[0, o], ps.at[1, o], me.across(o)).wait_recv()
+                if square:
+                    @pl.when(o == 1)
+                    def _():
+                        for other in (1, 2):
+                            hn_copy(other).wait_recv()
+                            half_copy(hns, hn_halves, other).start()
+
+                    @pl.when(o == 3)
+                    def _():
+                        for other in (1, 2):
+                            half_copy(ogs, og_halves, other).wait_recv()
+                            half_copy(hns, hn_halves, other).wait_recv()
+                else:
+                    @pl.when(o > 0)
+                    def _():
+                        hn_copy(o).wait_recv()
+                        remote(og_ref, ogs.at[o], ps.at[0, o], ps.at[1, o], me.across(o)).wait_recv()
             else:
                 spill_copy(o, True).start()
 
@@ -629,8 +680,9 @@
 
                 @pl.when(o == 0)
                 def _():
-                    for other in far(planes):
-                        hn_copy(other).start()
+                    if not square:
+                        for other in far(planes):
+                            hn_copy(other).start()
                     pass_second.step(2)
 
                 @pl.when(o == planes // 2)
@@ -641,19 +693,43 @@
                 gn = gn + proj[:, :D]
                 out = out + proj[:, D:]
 
-                @pl.when(o > 0)
+                @pl.when(i > 0)
                 def _():
-                    parts_copy(o - 1).wait()
-                    send_gn[o - 1] = gn.astype(BF)
-                    gn_copy(o).start()
+                    parts_copy(o + 1).wait()
+
+                if square:
+                    proj[:, :D] = gn
+
+                    @pl.when(o == 3)
+                    def _():
+                        send_gn[2] = gn.astype(BF)
+                        for other in (1, 2):
+                            diagonal_copy(other).start()
+
+                    for other in (1, 2):
+                        @pl.when(o == other)
+                        def _():
+                            rows = diagonal_rows(3 - other)
+                            diagonal_copy(3 - other).wait_recv()
+                            proj[rows, :D] += recv_gn[2, rows].astype(F32)
+                            send_gn[other - 1] = proj[:, :D].astype(BF)
+                            gn_copy(other).start()
+                else:
+                    @pl.when(o > 0)
+                    def _():
+                        send_gn[o - 1] = gn.astype(BF)
+                        gn_copy(o).start()
 
                 @pl.when(o == 0)
                 def _():
                     gn_out[...] = gn
+
+                @pl.when(i == 0)
+                def _():
                     fold.second()
                     fold.step(0)
 
-                @pl.when(o == planes // 2)
+                @pl.when(i == planes // 2)
                 def _():
                     fold.step(1)
 
@@ -665,7 +741,7 @@
         if part == 0:
             spill_copy(planes - 1, False).wait()
         else:
-            parts_copy(planes - 1).wait()
+            parts_copy(0).wait()
         strip = D // planes
         grads = (grads_a, grads_b)[part]
 
@@ -698,7 +774,7 @@
     pass_second.arrive()
     ffn_part(1)
     total = gn_out[...]
-    for o in range(1, planes):
+    for o in (1, 2) if square else range(1, planes):
         gn_copy(o).wait_recv()
         total = total + recv_gn[o - 1].astype(F32)
     gn_out[...] = total
@@ -707,9 +783,13 @@
     pass_first.finish()
     pass_second.finish()
     fold.finish(True, range(EARLY))
-    for o in range(1, planes):
+    for o in (1, 2) if square else range(1, planes):
         gn_copy(o).wait_send()
         hn_copy(o).wait_send()
+        if square:
+            diagonal_copy(o).wait_send()
+            half_copy(hns, hn_halves, o).wait_send()
+            half_copy(ogs, og_halves, o).wait_send()
 
     for i in range(half):
         @pl.when(me.z - i - me.core >= 0)
@@ -804,6 +884,9 @@
             DMA((1,)),
             DMA((1,)),
             DMA((3,)),
+            DMA((2, 3)),
+            DMA((2, 3)),
+            DMA((2, 3)),
         ]
         + spread_sems(planes, depth) * 4
         + fold_scratch(planes, depth, rows, first),

time: 302 us -> 277 us (0.917)
  Pallas kernels: 280 us -> 257 us
    pallas_call x1, Pallas kernels: 168 us -> 152 us  [fore(): pl.pallas_call(functools.partial(fore_kernel, planes, depth, turns, n_gai...]
    pallas_call x1, Pallas kernels: 112 us -> 104 us  [home(): pl.pallas_call(functools.partial(home_kernel, planes, depth, turns, n_gai...]
where the time goes in v5:
time: 277 us; the launch traced here: 275 us
  Pallas kernels  257 us (93%)
  other arithmetic  12.4 us (4%)
  local copies, waits for them, and re-layouts  5.37 us (2%)
    pallas_call x1, Pallas kernels, fore(): pl.pallas_call(functools.partial(fore_kernel, planes, depth, turns, n_gai...  152 us
    pallas_call x1, Pallas kernels, home(): pl.pallas_call(functools.partial(home_kernel, planes, depth, turns, n_gai...  104 us
    sub x5, other arithmetic, adam_step(): weight - rate * (first_hat / (jnp.sqrt(second_hat) + ADAM_EPS) + decay *...  8.95 us

profile of v5, /device:TPU:0, one launch (start us, length us, event | category | flops | bytes accessed | tf_op | source)
XLA Modules:
  0.0 275.2 jit_solution(9903349343939638733)
XLA Ops:
  0.7 0.7 convert_bitcast_fusion
  1.3 1.3 iota_subtract_fusion
  2.7 0.6 pad_convert_fusion.gain_ref
  3.2 0.8 multiply_sine_fusion
  4.1 152.3 %shard_map.345 = (bf16[1024,256]{1,0:T(8,128)(2,1)}, bf16[5,256,1024]{2,1,0:T(8,128)(2,1)}, bf16[4,4,2,32,1024]{4,3,2,1,0:T(8,128)(2,1)}, bf16[4,4,2,32,1024]{4,...) custom-call(bf16[256,1024]{1,0:T(8,128)(2,1)} %bitcast.13, ...), custom_call_target="tpu_custom_call" | custom-call | flops 21743271936 | bytes 31457280 | tf_op jit(solution)/shard_map/pallas_call | solution.py:845
  156.3 0.0 copy-start.18
  156.4 0.0 copy-start.19
  156.4 0.0 copy-start.20
  156.4 0.0 copy-start.15
  156.4 0.0 copy-start.16
  156.4 0.0 copy-start.17
  156.4 0.0 copy-start.12
  156.4 0.0 copy-start.13
  156.4 0.0 copy-start.14
  156.5 104.3 %shard_map.346 = (bf16[256,1024]{1,0:T(8,128)(2,1)}, f32[256,1024]{1,0:T(8,128)}, f32[32,1024]{1,0:T(8,128)}, f32[32,2048]{1,0:T(8,128)}, f32[8,128]{1,0:T(8,128...) custom-call(f32[256,1024]{1,0:T(8,128)} %get-tuple-element.45.gn_ref, f32[256,1024]{1,0:T(8,128)} %get-tuple-element.46.mixed_ref, ...), custom_call_target="tpu_custom_call" | custom-call | flops 64424509440 | bytes 8388608 | tf_op jit(solution)/shard_map/pallas_call | solution.py:1324
  260.8 0.0 copy-done.18
  260.8 0.0 copy-done.19
  260.8 0.0 copy-done.20
  260.8 1.2 multiply_subtract_fusion.4
  262.0 0.0 copy-done.15
  262.0 0.0 copy-done.16
  262.0 0.0 copy-done.17
  262.0 0.0 copy-start.5
  262.1 0.0 copy-start.6
  262.1 0.0 copy-start.7
  262.1 0.0 copy-start.11
  262.1 1.8 multiply_subtract_fusion.3
  263.9 0.0 copy-done.13
  263.9 1.9 multiply_subtract_fusion.2
  265.9 0.0 copy-done.5
  265.9 0.0 copy-done.7
  265.9 0.0 copy-start
  265.9 0.0 copy-start.1
  265.9 0.0 copy-start.2
  265.9 0.0 copy-start.8
  265.9 1.5 multiply_subtract_fusion.1
  267.5 0.1 copy-done
  267.6 0.8 copy-done.1
  268.4 0.4 copy-done.2
  268.7 0.1 copy-done.8
  268.9 2.4 multiply_subtract_fusion
  271.3 0.0 copy-done.10
  271.3 0.8 copy.44
  272.1 0.6 copy-done.4
  272.7 1.0 copy.45
  273.7 0.1 copy-done.3
  273.8 0.7 copy.46
  274.5 0.7 copy.47
  (10 shorter events, 0.0 us)
Async XLA Ops:
  156.3 104.4 %copy-start.18 = (f32[68]{0:T(128)S(1)}, f32[68]{0:T(128)}, u32[]{:S(2)}) copy-start(f32[68]{0:T(128)} %param.25) | copy-start | bytes 820
  156.4 104.4 %copy-start.19 = (f32[68]{0:T(128)S(1)}, f32[68]{0:T(128)}, u32[]{:S(2)}) copy-start(f32[68]{0:T(128)} %param.30) | copy-start | bytes 820
  156.4 104.4 %copy-start.20 = (f32[68]{0:T(128)S(1)}, f32[68]{0:T(128)}, u32[]{:S(2)}) copy-start(f32[68]{0:T(128)} %param.35) | copy-start | bytes 820
  156.4 105.6 %copy-start.15 = (f32[32,1024]{1,0:T(8,128)S(1)}, f32[32,1024]{1,0:T(8,128)}, u32[]{:S(2)}) copy-start(f32[32,1024]{1,0:T(8,128)} %wout_ref.1) | copy-start | bytes 393220
  156.4 105.6 %copy-start.16 = (f32[32,1024]{1,0:T(8,128)S(1)}, f32[32,1024]{1,0:T(8,128)}, u32[]{:S(2)}) copy-start(f32[32,1024]{1,0:T(8,128)} %param.27) | copy-start | bytes 393220
  156.4 105.6 %copy-start.17 = (f32[32,1024]{1,0:T(8,128)S(1)}, f32[32,1024]{1,0:T(8,128)}, u32[]{:S(2)}) copy-start(f32[32,1024]{1,0:T(8,128)} %param.32) | copy-start | bytes 393220
  156.4 107.5 %copy-start.12 = (f32[32,2048]{1,0:T(8,128)S(1)}, f32[32,2048]{1,0:T(8,128)}, u32[]{:S(2)}) copy-start(f32[32,2048]{1,0:T(8,128)} %wqkv_ref.1) | copy-start | bytes 786436
  156.4 107.5 %copy-start.13 = (f32[32,2048]{1,0:T(8,128)S(1)}, f32[32,2048]{1,0:T(8,128)}, u32[]{:S(2)}) copy-start(f32[32,2048]{1,0:T(8,128)} %param.26) | copy-start | bytes 786436
  156.4 107.5 %copy-start.14 = (f32[32,2048]{1,0:T(8,128)S(1)}, f32[32,2048]{1,0:T(8,128)}, u32[]{:S(2)}) copy-start(f32[32,2048]{1,0:T(8,128)} %param.31) | copy-start | bytes 786436
  262.0 3.8 %copy-start.5 = (f32[32,4608]{1,0:T(8,128)S(1)}, f32[32,4608]{1,0:T(8,128)}, u32[]{:S(2)}) copy-start(f32[32,4608]{1,0:T(8,128)} %wdown_ref.1) | copy-start | bytes 1769476
  262.1 3.8 %copy-start.6 = (f32[32,4608]{1,0:T(8,128)S(1)}, f32[32,4608]{1,0:T(8,128)}, u32[]{:S(2)}) copy-start(f32[32,4608]{1,0:T(8,128)} %param.29) | copy-start | bytes 1769476
  262.1 3.8 %copy-start.7 = (f32[32,4608]{1,0:T(8,128)S(1)}, f32[32,4608]{1,0:T(8,128)}, u32[]{:S(2)}) copy-start(f32[32,4608]{1,0:T(8,128)} %param.34) | copy-start | bytes 1769476
  262.1 3.8 %copy-start.11 = (bf16[32,4608]{1,0:T(8,128)(2,1)S(1)}, bf16[32,4608]{1,0:T(8,128)(2,1)}, u32[]{:S(2)}) copy-start(bf16[32,4608]{1,0:T(8,128)(2,1)} %get-tuple-element.66) | copy-start | bytes 884740
  265.9 1.7 copy-start
  265.9 2.5 copy-start.1
  265.9 2.8 %copy-start.2 = (f32[32,9216]{1,0:T(8,128)S(1)}, f32[32,9216]{1,0:T(8,128)}, u32[]{:S(2)}) copy-start(f32[32,9216]{1,0:T(8,128)} %param.33) | copy-start | bytes 3538948
  265.9 2.9 %copy-start.8 = (bf16[32,9216]{1,0:T(8,128)(2,1)S(1)}, bf16[32,9216]{1,0:T(8,128)(2,1)}, u32[]{:S(2)}) copy-start(bf16[32,9216]{1,0:T(8,128)(2,1)} %get-tuple-element.65) | copy-start | bytes 1769476
  268.9 2.4 copy-start.10
  271.3 1.4 copy-start.4
  272.7 1.1 copy-start.3
  272.7 1.8 copy-start.9

commit v6 on v5

--- a/solution.py
+++ b/solution.py
@@ -23,13 +23,6 @@
 BETA_ONE = 0.9
 BETA_TWO = 0.95
 ADAM_EPS = 1e-08
-
-
-def rope_tables(places):
-    half = HEAD_DIM // 2
-    freqs = jnp.exp(-math.log(THETA) * (2.0 * jnp.arange(half, dtype=jnp.float32) / HEAD_DIM))
-    angles = freqs[:, None] * places.astype(jnp.float32)[None, :]
-    return (jnp.cos(angles), jnp.sin(angles))
 
 
 def adam_step(weight, grad, first, second, rate, decay):
@@ -356,9 +349,9 @@
 
 def fore_kernel(
     planes, depth, turns, n_gains,
-    tok_ref, cos_ref, sin_ref, lower_ref, gain_ref, wqkv_ref, wout_ref, wpair_ref, wdown_ref, og_ref,
+    tok_ref, place_ref, gain_ref, wqkv_ref, wout_ref, wpair_ref, wdown_ref, og_ref,
     q_any, kv_any, wq_any, wkv_any, xat_any, unit_any, recip_any, wo_any, parts_any, spill_any, grads_a, grads_b, mine_any,
-    gains_out, o_out, lse_out, mixed_out, gn_out,
+    gains_out, o_out, lse_out, mixed_out, gn_out, cos_ref, sin_ref, lower_ref,
     q_s, kv_all, wq_all, wkv_all, xat, unit_s, recip_s, wo_all, blocks_a, blocks_b, gains_g, xa, proj, bias, accum, sums,
     wa, wb, hns, ogs, hnt, ogt, mid, pair, send_gn, recv_gn, part_s, stage, mine,
     own_sem, keep_sem, zs, cs, ps, a2a_a, a2a_b, pass_a, pass_b, hsem, nsem, psem, ssem, stsem, og_halves, hn_halves, dsem,
@@ -384,7 +377,9 @@
         copy.start()
         kept.append(copy)
 
-    gains_g[me.dp, me.z, me.core] = gain_ref[...]
+    here = gains_g.at[me.dp, me.z, me.core]
+    here[...] = jnp.zeros((8, 128), F32)
+    here[0:1, 0:n_gains] = gain_ref[...].astype(BF).astype(F32)
     wq_all[me.dp, me.z, me.core] = wqkv_ref[:, :HQ].astype(BF)
     wkv_all[me.dp, me.z, me.core] = wqkv_ref[:, HQ:].astype(BF)
     wo_all[me.dp, me.z, me.core] = wout_ref[...].astype(BF)
@@ -417,16 +412,20 @@
     for part in range(2):
         for o in range(1, planes):
             a2a_copy(part, o).start()
-    queries.line()
-    outputs.line()
     unit, _ = unit_of(tok_ref[...].astype(F32), 1)
     proj[:, :D] = unit
+    places = place_ref[...]
+    lower_ref[...] = lax.broadcasted_iota(jnp.int32, (1, count), 1) - places
+    steps = lax.broadcasted_iota(jnp.int32, (HEAD_DIM // 2, 1), 0).astype(F32)
+    angles = jnp.exp(-math.log(THETA) * (2.0 * steps / HEAD_DIM)) * places.astype(F32)
+    cos_ref[...] = jnp.cos(angles)
+    sin_ref[...] = jnp.sin(angles)
     gains.first()
     gains.plane(far(planes))
     weights.first()
+    queries.line()
     a2a_wait(0)
     pass_first.step(1)
-    queries.first()
     for o in range(1, planes):
         gains.relay(o)
     for o in range(planes):
@@ -461,6 +460,8 @@
             proj[:, at] += dot(xa[me.dp ^ o], table[me.dp ^ o].reshape(width, D), NN)
 
     project(weights, wkv_all, pl.ds(HQ, 2 * HK))
+    queries.first()
+    outputs.line()
     tail_row = gains_row[:, 2 * D : 2 * D + 128]
     gain_q, gain_k = column_of(tail_row, 0), column_of(tail_row, HEAD_DIM)
     cosine, sine = cos_ref[...], sin_ref[...]
@@ -487,17 +488,19 @@
         )
 
     def z_copy(k):
-        return remote(kv_all.at[0], kv_all.at[2 * k], zs.at[0, k], zs.at[1, k], me.along(me.ahead(k)))
+        return remote(kv_all.at[2 * k - 2], kv_all.at[2 * k], zs.at[0, k], zs.at[1, k], me.along(me.ahead(1)))
+
+    def z_sends(k):
+        return (me.z + 1 < depth) & (me.z - k + 1 >= 0)
 
     def c_copy(i):
         return remote(
             kv_all.at[2 * i + 2 * me.core], kv_all.at[2 * i + 1], cs.at[0, i], cs.at[1, i], me.sibling()
         )
 
-    for k in range(1, half + 1):
-        @pl.when(me.z + k < depth)
-        def _():
-            z_copy(k).start()
+    @pl.when(z_sends(1))
+    def _():
+        z_copy(1).start()
 
     @pl.when(me.core == 0)
     def _():
@@ -550,6 +553,11 @@
         @pl.when(there)
         def _():
             z_copy(k).wait_recv()
+
+        if k < half:
+            @pl.when(z_sends(k + 1))
+            def _():
+                z_copy(k + 1).start()
 
         @pl.when(there & (me.core == 1))
         def _():
@@ -797,7 +805,7 @@
             c_copy(i).wait_send()
 
     for k in range(1, half + 1):
-        @pl.when(me.z + k < depth)
+        @pl.when(z_sends(k))
         def _():
             z_copy(k).wait_send()
 
@@ -814,7 +822,7 @@
         copy.wait()
 
 
-def fore(tokens, cosine, sine, lower, gains_block, w_qkv, w_output, w_gate_up, w_down, cotangent, n_gains, planes, depth, turns, collective_id):
+def fore(tokens, places, gains, w_qkv, w_output, w_gate_up, w_down, cotangent, n_gains, planes, depth, turns, collective_id):
     half = turns // 2
     count = tokens.shape[0]
     rows = w_qkv.shape[0]
@@ -840,13 +848,16 @@
         ((GROUPS, 4, count), F32),
         ((count, D), F32),
         ((count, D), F32),
+        ((HEAD_DIM // 2, count), F32),
+        ((HEAD_DIM // 2, count), F32),
+        ((1, count), jnp.int32),
     ]
     flops = 18 * planes * count * D * (first + second)
     return pl.pallas_call(
         functools.partial(fore_kernel, planes, depth, turns, n_gains),
         out_shape=tuple(jax.ShapeDtypeStruct(s, k) for s, k in shapes),
-        in_specs=[VMEM] * 9 + [ANY],
-        out_specs=(ANY,) * 13 + (VMEM,) * 5,
+        in_specs=[VMEM] * 7 + [ANY],
+        out_specs=(ANY,) * 13 + (VMEM,) * 8,
         scratch_shapes=[pltpu.VMEM(*shape) for shape in shapes[:8]]
         + [
             pltpu.VMEM((planes, 3, rows, first), BF),
@@ -892,7 +903,7 @@
         + fold_scratch(planes, depth, rows, first),
         compiler_params=params(collective_id),
         cost_estimate=pl.CostEstimate(flops=flops, bytes_accessed=30 << 20, transcendentals=0),
-    )(tokens, cosine, sine, lower, gains_block, w_qkv, w_output, w_gate_up, w_down, cotangent)
+    )(tokens, places, gains, w_qkv, w_output, w_gate_up, w_down, cotangent)
 
 
 class Fold:
@@ -1072,7 +1083,18 @@
         return remote(gkv.at[2 * i + 1], from_core.at[i], cs.at[0, i], cs.at[1, i], me.sibling())
 
     def z_copy(k):
-        return remote(gkv.at[2 * k], from_z.at[k - 1], zs.at[0, k], zs.at[1, k], me.along(me.behind(k)))
+        return remote(gkv.at[2 * k], from_z.at[k - 1], zs.at[0, k], zs.at[1, k], me.along(me.behind(1)))
+
+    def join(k):
+        if k < half:
+            @pl.when((me.z - k >= 0) & (me.z + 1 < depth))
+            def _():
+                z_copy(k + 1).wait_recv()
+                gkv[2 * k] = (gkv[2 * k].astype(F32) + from_z[k].astype(F32)).astype(BF)
+
+        @pl.when(me.z - k >= 0)
+        def _():
+            z_copy(k).start()
 
     def p_copy(o):
         return remote(parts_any.at[o], from_plane.at[o - 1], ps.at[0, o], ps.at[1, o], me.across(o))
@@ -1099,13 +1121,6 @@
         delta[t] = jnp.concatenate(rows, axis=0)
     half_rows = D // planes
     order = list(range(1, planes)) + [0]
-    for o in order:
-        d = me.dp ^ o
-        rows = o_ref[pl.ds(pl.multiple_of(d * half_rows, 128), half_rows), :]
-        partial[d] = dot(rows, gmixed_b, NN).astype(BF).reshape(partial.shape[1:])
-        collect.first(o)
-    folds[1].second()
-    folds[1].step(0)
     gq[...] = jnp.zeros_like(gq)
     loads[1].wait()
 
@@ -1161,9 +1176,19 @@
                 c_copy(k - 1).wait_recv()
                 gkv[2 * k] = (gkv[2 * k].astype(F32) + from_core[k - 1].astype(F32)).astype(BF)
 
-            z_copy(k).start()
-
+        if k == half:
+            join(k)
+
+    folds[1].second()
+    folds[1].step(0)
     visit(0)
+    for k in range(half - 1, 0, -1):
+        join(k)
+    for o in order:
+        d = me.dp ^ o
+        rows = o_ref[pl.ds(pl.multiple_of(d * half_rows, 128), half_rows), :]
+        partial[d] = dot(rows, gmixed_b, NN).astype(BF).reshape(partial.shape[1:])
+        collect.first(o)
     for i in (2, 3, 4):
         loads[i].wait()
     tail_row = gains_ref[:, 2 * D : 2 * D + 128]
@@ -1213,11 +1238,10 @@
         c_copy(0).wait_recv()
         grad_kv[...] += from_core[0].astype(F32)
 
-    for k in range(1, half + 1):
-        @pl.when(me.z + k < depth)
-        def _():
-            z_copy(k).wait_recv()
-            grad_kv[...] += from_z[k - 1].astype(F32)
+    @pl.when(me.z + 1 < depth)
+    def _():
+        z_copy(1).wait_recv()
+        grad_kv[...] += from_z[0].astype(F32)
 
     for h in range(HEADS, HEADS + KV_HEADS, 4):
         four_grads(h)
@@ -1375,6 +1399,35 @@
     )(*first, *second)
 
 
+def adam_kernel(rates, *refs):
+    n = len(rates)
+    for i, rate in enumerate(rates):
+        weight, grad, first, second = (r[...] for r in refs[4 * i : 4 * i + 4])
+        grad = grad.astype(F32)
+        outs = refs[4 * (n + i) : 4 * (n + i) + 4]
+        for out, value in zip(outs, (grad,) + adam_step(weight, grad, first, second, rate, 0.1)):
+            out[...] = value
+
+
+def adam(groups, rates):
+    rows = groups[0][0].shape[0]
+    block = 16 if rows % 16 == 0 else rows
+    specs, shapes = [], []
+    for group in groups:
+        columns = group[0].shape[1]
+        specs += [pl.BlockSpec((block, columns), lambda i: (i, 0))] * 4
+        shapes += [jax.ShapeDtypeStruct((rows, columns), F32)] * 4
+    outs = pl.pallas_call(
+        functools.partial(adam_kernel, rates),
+        out_shape=tuple(shapes),
+        grid=(rows // block,),
+        in_specs=specs,
+        out_specs=tuple(specs),
+        compiler_params=pltpu.CompilerParams(vmem_limit_bytes=VMEM_BYTES),
+    )(*[array for group in groups for array in group])
+    return [outs[4 * i : 4 * i + 4] for i in range(len(groups))]
+
+
 def per_device(
     tokens_in,
     positions,
@@ -1402,17 +1455,14 @@
     n_gains = norm_gains.shape[0]
     count = tokens_in.shape[0] * tokens_in.shape[1]
     tokens = tokens_in.reshape(count, D)
-    places = positions.reshape(count)
+    places = positions.reshape(1, count)
     cotangent = out_grad.reshape(count, D)
 
-    gains_block = jnp.pad(norm_gains.astype(BF).astype(F32)[None, :], ((0, 7), (0, 128 - n_gains)))
-    cosine, sine = rope_tables(places)
-    lower = (jnp.arange(count, dtype=jnp.int32) - places)[None, :]
     (
         query, kv_all, wq_all, wkv_all, xat, unit_heads, recip_heads, output_all, parts, _, _, grads, mine,
-        gains_row, attn_t, lse, mixed, grad_normed,
+        gains_row, attn_t, lse, mixed, grad_normed, cosine, sine, lower,
     ) = fore(
-        tokens, cosine, sine, lower, gains_block, w_qkv, w_output, w_gate_up, w_down, cotangent,
+        tokens, places, norm_gains[None, :], w_qkv, w_output, w_gate_up, w_down, cotangent,
         n_gains, planes, depth, turns, 0,
     )
     block_out, input_grad, shard_output, shard_qkv, gains_tile, pair_b, down_b = home(
@@ -1421,20 +1471,19 @@
         n_gains, planes, depth, turns, 1,
     )
     shard_gains = gains_tile[0, :n_gains]
-    shard_gate_up = pair_b.astype(F32)
-    shard_down = down_b.astype(F32)
-
-    new_qkv, new_first_qkv, new_second_qkv = adam_step(
-        w_qkv, shard_qkv, first_qkv, second_qkv, 0.02, 0.1
-    )
-    new_output, new_first_output, new_second_output = adam_step(
-        w_output, shard_output, first_output, second_output, 0.2, 0.1
-    )
-    new_gate_up, new_first_gate_up, new_second_gate_up = adam_step(
-        w_gate_up, shard_gate_up, first_gate_up, second_gate_up, 0.02, 0.1
-    )
-    new_down, new_first_down, new_second_down = adam_step(
-        w_down, shard_down, first_down, second_down, 0.02, 0.1
+    (
+        (shard_qkv, new_qkv, new_first_qkv, new_second_qkv),
+        (shard_output, new_output, new_first_output, new_second_output),
+        (shard_gate_up, new_gate_up, new_first_gate_up, new_second_gate_up),
+        (shard_down, new_down, new_first_down, new_second_down),
+    ) = adam(
+        (
+            (w_qkv, shard_qkv, first_qkv, second_qkv),
+            (w_output, shard_output, first_output, second_output),
+            (w_gate_up, pair_b, first_gate_up, second_gate_up),
+            (w_down, down_b, first_down, second_down),
+        ),
+        (0.02, 0.2, 0.02, 0.02),
     )
     new_gains, new_first_gains, new_second_gains = adam_step(
         norm_gains, shard_gains, first_gains, second_gains, 0.1, 0.0

time: 277 us -> 257 us (0.928)
  other arithmetic: 12.4 us -> 1.21 us
  Pallas kernels: 257 us -> 252 us
  local copies, waits for them, and re-layouts: 5.37 us -> 1.79 us
    pallas_call x1, Pallas kernels: 104 us -> 91.3 us  [home(): pl.pallas_call(functools.partial(home_kernel, planes, depth, turns, n_gai...]
    sub x5 -> x1, other arithmetic: 8.95 us -> 1.21 us  [adam_step(): weight - rate * (first_hat / (jnp.sqrt(second_hat) + ADAM_EPS) + decay *...]
    pallas_call x0 -> x1, Pallas kernels: none -> 6.76 us  [adam(): pl.pallas_call(functools.partial(adam_kernel, rates), out_shape=tuple(sha...]
    unnamed x46 -> x12, local copies, waits for them, and re-layouts: 5.37 us -> 1.79 us
where the time goes in v6:
time: 257 us; the launch traced here: 256 us
  Pallas kernels  252 us (98%)
    pallas_call x1, Pallas kernels, fore(): pl.pallas_call(functools.partial(fore_kernel, planes, depth, turns, n_gai...  154 us
    pallas_call x1, Pallas kernels, home(): pl.pallas_call(functools.partial(home_kernel, planes, depth, turns, n_gai...  91.3 us
    pallas_call x1, Pallas kernels, adam(): pl.pallas_call(functools.partial(adam_kernel, rates), out_shape=tuple(sha...  6.76 us

profile of v6, /device:TPU:0, one launch (start us, length us, event | category | flops | bytes accessed | tf_op | source)
XLA Modules:
  0.0 256.1 jit_solution(1106920675514714648)
XLA Ops:
  0.7 154.2 %shard_map.345 = (bf16[1024,256]{1,0:T(8,128)(2,1)}, bf16[5,256,1024]{2,1,0:T(8,128)(2,1)}, bf16[4,4,2,32,1024]{4,3,2,1,0:T(8,128)(2,1)}, bf16[4,4,2,32,1024]{4,...) custom-call(bf16[256,1024]{1,0:T(8,128)(2,1)} %bitcast.11, ...), custom_call_target="tpu_custom_call" | custom-call | flops 21743271936 | bytes 31457280 | tf_op jit(solution)/shard_map/pallas_call | solution.py:856
  154.9 0.0 copy-start.2
  154.9 0.0 copy-start.3
  154.9 0.0 copy-start.4
  154.9 91.3 %shard_map.346 = (bf16[256,1024]{1,0:T(8,128)(2,1)}, f32[256,1024]{1,0:T(8,128)}, f32[32,1024]{1,0:T(8,128)}, f32[32,2048]{1,0:T(8,128)}, f32[8,128]{1,0:T(8,128...) custom-call(f32[256,1024]{1,0:T(8,128)} %get-tuple-element.64.gn_ref, f32[256,1024]{1,0:T(8,128)} %get-tuple-element.65.mixed_ref, ...), custom_call_target="tpu_custom_call" | custom-call | flops 64424509440 | bytes 8388608 | tf_op jit(solution)/shard_map/pallas_call | solution.py:1348
  246.3 0.0 copy-done.2
  246.3 0.0 copy-done.3
  246.3 0.0 copy-done.4
  246.3 1.2 multiply_subtract_fusion
  247.5 0.0 copy-start.1
  247.5 0.0 copy-start
  247.5 6.8 %shard_map.347 = (f32[32,2048]{1,0:T(8,128)}, f32[32,2048]{1,0:T(8,128)}, f32[32,2048]{1,0:T(8,128)}, f32[32,2048]{1,0:T(8,128)}, f32[32,1024]{1,0:T(8,128)}, /*...) custom-call(f32[32,2048]{1,0:T(8,128)} %refs_0_.1, ...), custom_call_target="tpu_custom_call" | custom-call | tf_op jit(solution)/shard_map/pallas_call | solution.py:1420
  254.3 0.0 copy-done.1
  254.3 0.8 copy.42
  255.1 0.0 copy-done
  255.1 1.0 copy.43
Async XLA Ops:
  154.9 91.4 %copy-start.2 = (f32[68]{0:T(128)S(1)}, f32[68]{0:T(128)}, u32[]{:S(2)}) copy-start(f32[68]{0:T(128)} %param.25) | copy-start | bytes 820
  154.9 91.4 %copy-start.3 = (f32[68]{0:T(128)S(1)}, f32[68]{0:T(128)}, u32[]{:S(2)}) copy-start(f32[68]{0:T(128)} %param.30) | copy-start | bytes 820
  154.9 91.4 %copy-start.4 = (f32[68]{0:T(128)S(1)}, f32[68]{0:T(128)}, u32[]{:S(2)}) copy-start(f32[68]{0:T(128)} %param.35) | copy-start | bytes 820
  247.5 6.8 %copy-start.1 = (bf16[256,1024]{1,0:T(8,128)(2,1)S(1)}, bf16[256,1024]{1,0:T(8,128)(2,1)}, u32[]{:S(2)}) copy-start(bf16[256,1024]{1,0:T(8,128)(2,1)} %get-tuple-element.83) | copy-start | bytes 1572868
  247.5 7.6 %copy-start = (f32[256,1024]{1,0:T(8,128)S(1)}, f32[256,1024]{1,0:T(8,128)}, u32[]{:S(2)}) copy-start(f32[256,1024]{1,0:T(8,128)} %get-tuple-element.84) | copy-start | bytes 3145732

commit v7 on v6

--- a/solution.py
+++ b/solution.py
@@ -43,7 +43,7 @@
 NN = (((1,), (0,)), ((), ()))
 NT = (((1,), (1,)), ((), ()))
 TN = (((0,), (0,)), ((), ()))
-VMEM_BYTES = 60 << 20
+VMEM_BYTES = 121 << 19
 GROUPS = HEADS // 4
 
 
@@ -274,11 +274,18 @@
     return jnp.concatenate([a * cosine - b * sine, b * cosine + a * sine], axis=0)
 
 
+def paired(h, count):
+    rows = slice(h // 2 * HEAD_DIM, (h // 2 + 1) * HEAD_DIM)
+    return rows, slice(h % 2 * count, (h % 2 + 1) * count)
+
+
 def fill_bias(bias, lower, slot):
     count = bias.shape[0]
     query = lax.broadcasted_iota(jnp.int32, (count, count), 1)
     key = lax.broadcasted_iota(jnp.int32, (count, count), 0) - slot * count
-    bias[...] = jnp.where((key <= query) & (key >= lower), 0.0, NEG_BIG)
+    allowed = jnp.where((key <= query) & (key >= lower), 0.0, NEG_BIG)
+    bias[:, :count] = allowed
+    bias[:, count:] = allowed
 
 
 class Pass:
@@ -509,7 +516,9 @@
     project(queries, wq_all, pl.ds(0, HQ))
     outputs.first()
     for h in range(0, HEADS, 4):
-        q_s[pl.ds(h * HEAD_DIM, 4 * HEAD_DIM), :] = (four_raw(h) * HEAD_DIM ** (-0.5)).astype(BF)
+        four = (four_raw(h) * HEAD_DIM ** (-0.5)).astype(BF)
+        for i in range(4):
+            q_s[paired(h + i, count)] = four[i * HEAD_DIM : (i + 1) * HEAD_DIM]
     keep(q_s, q_any)
     keep(unit_s, unit_any)
     keep(recip_s, recip_any)
@@ -536,11 +545,10 @@
             for u in range(2):
                 key = keys[:, u * 64 : u * 64 + 64]
                 value = values[:, u * 64 : u * 64 + 64]
-                for g in range(2):
-                    at = pl.ds(pl.multiple_of(t * 256 + u * 128 + g * 64, 64), 64)
-                    weight = jnp.exp(dot(key, q_s[at, :], NN) + bias[...])
-                    totals.append(jnp.sum(weight, axis=0, keepdims=True))
-                    accum[at, :] += dot(value, weight.astype(BF), TN)
+                at = pl.ds(pl.multiple_of(t * 128 + u * 64, 64), 64)
+                weight = jnp.exp(dot(key, q_s[at, :], NN) + bias[...])
+                totals.append(jnp.sum(weight, axis=0, keepdims=True))
+                accum[at, :] += dot(value, weight.astype(BF), TN)
             sums[t] += jnp.concatenate(totals, axis=0)
             return carry
 
@@ -590,11 +598,11 @@
             remote(og_ref, ogs.at[o], ps.at[0, o], ps.at[1, o], me.across(o)).wait_recv()
             half_copy(ogs, og_halves, o).start()
     for t in range(GROUPS):
-        total = sums[t]
-        lse_out[t] = jnp.log(total)
-        for h in range(4):
-            at = pl.ds(t * 256 + h * 64, 64)
-            o_out[at, :] = (accum[at, :] / total[h : h + 1, :]).astype(BF)
+        lse_out[t] = jnp.log(sums[t])
+    for h in range(HEADS):
+        at = paired(h, count)
+        total = sums[h // 4, h // 2 % 2 : h // 2 % 2 + 1, at[1]]
+        o_out[pl.ds(h * HEAD_DIM, HEAD_DIM), :] = (accum[at] / total).astype(BF)
     for o in range(planes):
         outputs.arrive(o)
     keep(wo_all, wo_any)
@@ -830,7 +838,7 @@
     devices = planes * depth * 2
     everyone = (planes, depth, 2, rows)
     shapes = [
-        ((HQ, count), BF),
+        ((HK, 2 * count), BF),
         ((turns + 1, count, 2 * HK), BF),
         (everyone + (HQ,), BF),
         (everyone + (2 * HK,), BF),
@@ -845,7 +853,7 @@
         ((depth, planes, 3, rows, first), BF),
         ((1, devices * n_gains), F32),
         ((HQ, count), BF),
-        ((GROUPS, 4, count), F32),
+        ((GROUPS, 2, 2 * count), F32),
         ((count, D), F32),
         ((count, D), F32),
         ((HEAD_DIM // 2, count), F32),
@@ -865,9 +873,9 @@
             pltpu.VMEM((planes, depth, 2, 8, 128), F32),
             pltpu.VMEM((planes, count, D // planes), BF),
             pltpu.VMEM((count, 2 * HQ), F32),
-            pltpu.VMEM((count, count), F32),
-            pltpu.VMEM((HQ, count), F32),
-            pltpu.VMEM((GROUPS, 4, count), F32),
+            pltpu.VMEM((count, 2 * count), F32),
+            pltpu.VMEM((HK, 2 * count), F32),
+            pltpu.VMEM((GROUPS, 2, 2 * count), F32),
             pltpu.VMEM((3, planes, depth * 2, rows, first), BF),
             pltpu.VMEM((3, planes, depth * 2, rows, second), BF),
             pltpu.VMEM((planes, count, D), BF),
@@ -1110,15 +1118,14 @@
     dgf = jnp.sum(grad * unit, axis=0, keepdims=True)
     gmixed_b = gmixed.astype(BF)
     loads[0].wait()
-    gob[...] = dot(wo[...].reshape(HQ, D), gmixed_b, NT).astype(BF)
-    for t in range(GROUPS):
-        rows = []
-        for h in range(4):
-            at = pl.ds(t * 256 + h * 64, 64)
-            rows.append(
-                jnp.sum(gob[at, :].astype(F32) * o_ref[at, :].astype(F32), axis=0, keepdims=True)
-            )
-        delta[t] = jnp.concatenate(rows, axis=0)
+    gob_all = dot(wo[...].reshape(HQ, D), gmixed_b, NT).astype(BF)
+    for h in range(HEADS):
+        gob_h = gob_all[h * HEAD_DIM : (h + 1) * HEAD_DIM]
+        gob[paired(h, count)] = gob_h
+        out = o_ref[pl.ds(h * HEAD_DIM, HEAD_DIM), :].astype(F32)
+        delta[h // 4, h // 2 % 2 : h // 2 % 2 + 1, paired(h, count)[1]] = jnp.sum(
+            gob_h.astype(F32) * out, axis=0, keepdims=True
+        )
     half_rows = D // planes
     order = list(range(1, planes)) + [0]
     gq[...] = jnp.zeros_like(gq)
@@ -1136,16 +1143,13 @@
             for u in range(2):
                 key = keys[:, u * 64 : u * 64 + 64]
                 value = values[:, u * 64 : u * 64 + 64]
-                grad_key, grad_value = 0.0, 0.0
-                for g in range(2):
-                    h = 2 * u + g
-                    at = pl.ds(pl.multiple_of(t * 256 + h * 64, 64), 64)
-                    query, gob_h = q_ref[at, :], gob[at, :]
-                    probs = jnp.exp(dot(key, query, NN) + bias[...] - lse_t[h : h + 1, :])
-                    grad_value = grad_value + dot(probs.astype(BF), gob_h, NT)
-                    grad_scores = (probs * (dot(value, gob_h, NN) - delta_t[h : h + 1, :])).astype(BF)
-                    grad_key = grad_key + dot(grad_scores, query, NT)
-                    gq[at, :] += dot(key, grad_scores, TN)
+                at = pl.ds(pl.multiple_of(t * 128 + u * 64, 64), 64)
+                query, gob_h = q_ref[at, :], gob[at, :]
+                probs = jnp.exp(dot(key, query, NN) + bias[...] - lse_t[u : u + 1, :])
+                grad_value = dot(probs.astype(BF), gob_h, NT)
+                grad_scores = (probs * (dot(value, gob_h, NN) - delta_t[u : u + 1, :])).astype(BF)
+                grad_key = dot(grad_scores, query, NT)
+                gq[at, :] += dot(key, grad_scores, TN)
                 grad_keys.append(grad_key)
                 grad_values.append(grad_value)
             gkv[slot, :, key_at] = jnp.concatenate(grad_keys, axis=1).astype(BF)
@@ -1199,14 +1203,15 @@
     def four_grads(h):
         kind = 0 if h < HEADS else 1
         if kind == 0:
-            four = gq[pl.ds(h * HEAD_DIM, 4 * HEAD_DIM), :] * HEAD_DIM ** (-0.5)
+            heads = [gq[paired(h + i, count)] * HEAD_DIM ** (-0.5) for i in range(4)]
         else:
             four = grad_kv[:, pl.ds((h - HEADS) * HEAD_DIM, 4 * HEAD_DIM)].T
+            heads = [four[i * HEAD_DIM : (i + 1) * HEAD_DIM] for i in range(4)]
         recips = recip_s[h // 4]
         results = []
         for i in range(4):
             unit = unit_s[pl.ds((h + i) * HEAD_DIM, HEAD_DIM), :]
-            grad = turned(four[i * HEAD_DIM : (i + 1) * HEAD_DIM], cosine, sine)
+            grad = turned(heads[i], cosine, sine)
             scaled = grad * (gain_k if kind else gain_q)
             inner = jnp.mean(scaled * unit, axis=0, keepdims=True)
             results.append(recips[i : i + 1, :] * (scaled - unit * inner))
@@ -1361,12 +1366,12 @@
         scratch_shapes=[pltpu.VMEM(a.shape, a.dtype) for a in (wo_all, kv_all, unit, recip, wq_all, wkv_all, xat)]
         + [
             pltpu.VMEM((count, D), BF),
-            pltpu.VMEM((HQ, count), F32),
+            pltpu.VMEM((HK, 2 * count), F32),
             pltpu.VMEM((count, 2 * HK), F32),
             pltpu.VMEM((count, D), F32),
-            pltpu.VMEM((count, count), F32),
-            pltpu.VMEM((HQ, count), BF),
-            pltpu.VMEM((GROUPS, 4, count), F32),
+            pltpu.VMEM((count, 2 * count), F32),
+            pltpu.VMEM((HK, 2 * count), BF),
+            pltpu.VMEM((GROUPS, 2, 2 * count), F32),
             pltpu.VMEM((turns + 1, count, 2 * HK), BF),
             pltpu.VMEM((half, count, 2 * HK), BF),
             pltpu.VMEM((half, count, 2 * HK), BF),

time: 257 us -> 251 us (0.977)
  Pallas kernels: 252 us -> 246 us
    pallas_call x1, Pallas kernels: 91.3 us -> 88.1 us  [home(): pl.pallas_call(functools.partial(home_kernel, planes, depth, turns, n_gai...]
    pallas_call x1, Pallas kernels: 154 us -> 151 us  [fore(): pl.pallas_call(functools.partial(fore_kernel, planes, depth, turns, n_gai...]
where the time goes in v7:
time: 251 us; the launch traced here: 250 us
  Pallas kernels  246 us (98%)
    pallas_call x1, Pallas kernels, fore(): pl.pallas_call(functools.partial(fore_kernel, planes, depth, turns, n_gai...  151 us
    pallas_call x1, Pallas kernels, home(): pl.pallas_call(functools.partial(home_kernel, planes, depth, turns, n_gai...  88.1 us
    pallas_call x1, Pallas kernels, adam(): pl.pallas_call(functools.partial(adam_kernel, rates), out_shape=tuple(sha...  6.76 us

profile of v7, /device:TPU:0, one launch (start us, length us, event | category | flops | bytes accessed | tf_op | source)
XLA Modules:
  0.0 250.0 jit_solution(17299939415109739521)
XLA Ops:
  0.7 151.4 %shard_map.345 = (bf16[512,512]{1,0:T(8,128)(2,1)}, bf16[5,256,1024]{2,1,0:T(8,128)(2,1)}, bf16[4,4,2,32,1024]{4,3,2,1,0:T(8,128)(2,1)}, bf16[4,4,2,32,1024]{4,3...) custom-call(bf16[256,1024]{1,0:T(8,128)(2,1)} %bitcast.11, ...), custom_call_target="tpu_custom_call" | custom-call | flops 21743271936 | bytes 31457280 | tf_op jit(solution)/shard_map/pallas_call | solution.py:864
  152.1 0.0 copy-start.2
  152.1 0.0 copy-start.3
  152.1 0.0 copy-start.4
  152.1 88.1 %shard_map.346 = (bf16[256,1024]{1,0:T(8,128)(2,1)}, f32[256,1024]{1,0:T(8,128)}, f32[32,1024]{1,0:T(8,128)}, f32[32,2048]{1,0:T(8,128)}, f32[8,128]{1,0:T(8,128...) custom-call(f32[256,1024]{1,0:T(8,128)} %get-tuple-element.64.gn_ref, f32[256,1024]{1,0:T(8,128)} %get-tuple-element.65.mixed_ref, ...), custom_call_target="tpu_custom_call" | custom-call | flops 64424509440 | bytes 8388608 | tf_op jit(solution)/shard_map/pallas_call | solution.py:1353
  240.2 0.0 copy-done.2
  240.2 0.0 copy-done.3
  240.3 0.0 copy-done.4
  240.3 1.2 multiply_subtract_fusion
  241.5 0.0 copy-start.1
  241.5 0.0 copy-start
  241.5 6.8 %shard_map.347 = (f32[32,2048]{1,0:T(8,128)}, f32[32,2048]{1,0:T(8,128)}, f32[32,2048]{1,0:T(8,128)}, f32[32,2048]{1,0:T(8,128)}, f32[32,1024]{1,0:T(8,128)}, /*...) custom-call(f32[32,2048]{1,0:T(8,128)} %refs_0_.1, ...), custom_call_target="tpu_custom_call" | custom-call | tf_op jit(solution)/shard_map/pallas_call | solution.py:1425
  248.2 0.0 copy-done.1
  248.3 0.8 copy.42
  249.1 0.0 copy-done
  249.1 1.0 copy.43
Async XLA Ops:
  152.1 88.2 %copy-start.2 = (f32[68]{0:T(128)S(1)}, f32[68]{0:T(128)}, u32[]{:S(2)}) copy-start(f32[68]{0:T(128)} %param.25) | copy-start | bytes 820
  152.1 88.2 %copy-start.3 = (f32[68]{0:T(128)S(1)}, f32[68]{0:T(128)}, u32[]{:S(2)}) copy-start(f32[68]{0:T(128)} %param.30) | copy-start | bytes 820
  152.1 88.2 %copy-start.4 = (f32[68]{0:T(128)S(1)}, f32[68]{0:T(128)}, u32[]{:S(2)}) copy-start(f32[68]{0:T(128)} %param.35) | copy-start | bytes 820
  241.5 6.8 %copy-start.1 = (bf16[256,1024]{1,0:T(8,128)(2,1)S(1)}, bf16[256,1024]{1,0:T(8,128)(2,1)}, u32[]{:S(2)}) copy-start(bf16[256,1024]{1,0:T(8,128)(2,1)} %get-tuple-element.83) | copy-start | bytes 1572868
  241.5 7.6 %copy-start = (f32[256,1024]{1,0:T(8,128)S(1)}, f32[256,1024]{1,0:T(8,128)}, u32[]{:S(2)}) copy-start(f32[256,1024]{1,0:T(8,128)} %get-tuple-element.84) | copy-start | bytes 3145732

commit v8 on v7

--- a/solution.py
+++ b/solution.py
@@ -789,6 +789,8 @@
         pass_second.step(s)
     pass_second.arrive()
     ffn_part(1)
+    for k in range(2, EARLY):
+        fold.step(k)
     total = gn_out[...]
     for o in (1, 2) if square else range(1, planes):
         gn_copy(o).wait_recv()
@@ -1084,7 +1086,8 @@
         copy.start()
     greet(me.plane() + me.line() + [me.sibling()])
     loads[8].wait()
-    folds[0].send(EARLY)
+    if depth - 1 > EARLY:
+        folds[0].send(EARLY)
     folds[1].first()
 
     def c_copy(i):
@@ -1251,8 +1254,8 @@
     for h in range(HEADS, HEADS + KV_HEADS, 4):
         four_grads(h)
     gproj[:, pl.ds(HQ + HK, HK)] = grad_kv[:, pl.ds(HK, HK)].astype(BF)
+    value_o = collect.third()
     gather_grads(pl.ds(HQ, 2 * HK), partial_kv, collect_kv)
-    value_o = collect.third()
     value_q = collect_q.third()
     for i in (6, 7):
         loads[i].wait()
@@ -1265,7 +1268,8 @@
     dga = jnp.sum(grad * unit, axis=0, keepdims=True)
     for k in range(2, depth - 1):
         folds[1].step(k)
-    folds[0].settle(depth - 2)
+    if depth - 1 > EARLY:
+        folds[0].settle(depth - 2)
     swaps[0].start(mine_first[me.z])
     lane = lax.broadcasted_iota(jnp.int32, (HEAD_DIM, 128), 1)
     entry = lax.broadcasted_iota(jnp.int32, (HEAD_DIM, 128), 0)
@@ -1293,10 +1297,11 @@
     gains_p[...] = jnp.broadcast_to(table[:, None, :], (devices, 8, 128)).reshape(gains_p.shape)
     for o in order:
         small.first(o)
+    value_kv = collect_kv.third()
     for o in order:
         small.second(o)
-    value_kv = collect_kv.third()
-    little = small.third()
+    folds[1].settle(depth - 2)
+    swaps[1].start(mine_second[me.z])
     total = mixed_ref[...]
     loads[5].wait()
     total = total + own_part[...].astype(F32)
@@ -1304,8 +1309,7 @@
         p_copy(o).wait_recv()
         total = total + from_plane[o - 1].astype(F32)
     block_out[...] = total.astype(BF)
-    folds[1].settle(depth - 2)
-    swaps[1].start(mine_second[me.z])
+    little = small.third()
     shard_out[...] = collect.last(value_o)
     shard_qkv[:, :HQ] = collect_q.last(value_q)
     shard_qkv[:, HQ:] = collect_kv.last(value_kv)

time: 251 us -> 250 us (level)
  no operation moved by 1% of the time
where the time goes in v8:
time: 250 us
  Pallas kernels  246 us (98%)
    pallas_call x1, Pallas kernels, fore(): pl.pallas_call(functools.partial(fore_kernel, planes, depth, turns, n_gai...  151 us
    pallas_call x1, Pallas kernels, home(): pl.pallas_call(functools.partial(home_kernel, planes, depth, turns, n_gai...  88 us
    pallas_call x1, Pallas kernels, adam(): pl.pallas_call(functools.partial(adam_kernel, rates), out_shape=tuple(sha...  6.76 us

profile of v8, /device:TPU:0, one launch (start us, length us, event | category | flops | bytes accessed | tf_op | source)
XLA Modules:
  0.0 249.9 jit_solution(9652416046701351768)
XLA Ops:
  0.7 151.4 %shard_map.345 = (bf16[512,512]{1,0:T(8,128)(2,1)}, bf16[5,256,1024]{2,1,0:T(8,128)(2,1)}, bf16[4,4,2,32,1024]{4,3,2,1,0:T(8,128)(2,1)}, bf16[4,4,2,32,1024]{4,3...) custom-call(bf16[256,1024]{1,0:T(8,128)(2,1)} %bitcast.11, ...), custom_call_target="tpu_custom_call" | custom-call | flops 21743271936 | bytes 31457280 | tf_op jit(solution)/shard_map/pallas_call | solution.py:866
  152.1 0.0 copy-start.2
  152.1 0.0 copy-start.3
  152.1 0.0 copy-start.4
  152.1 88.0 %shard_map.346 = (bf16[256,1024]{1,0:T(8,128)(2,1)}, f32[256,1024]{1,0:T(8,128)}, f32[32,1024]{1,0:T(8,128)}, f32[32,2048]{1,0:T(8,128)}, f32[8,128]{1,0:T(8,128...) custom-call(f32[256,1024]{1,0:T(8,128)} %get-tuple-element.64.gn_ref, f32[256,1024]{1,0:T(8,128)} %get-tuple-element.65.mixed_ref, ...), custom_call_target="tpu_custom_call" | custom-call | flops 64424509440 | bytes 8388608 | tf_op jit(solution)/shard_map/pallas_call | solution.py:1357
  240.1 0.0 copy-done.2
  240.1 0.0 copy-done.3
  240.1 0.0 copy-done.4
  240.1 1.2 multiply_subtract_fusion
  241.3 0.0 copy-start.1
  241.3 0.0 copy-start
  241.3 6.8 %shard_map.347 = (f32[32,2048]{1,0:T(8,128)}, f32[32,2048]{1,0:T(8,128)}, f32[32,2048]{1,0:T(8,128)}, f32[32,2048]{1,0:T(8,128)}, f32[32,1024]{1,0:T(8,128)}, /*...) custom-call(f32[32,2048]{1,0:T(8,128)} %refs_0_.1, ...), custom_call_target="tpu_custom_call" | custom-call | tf_op jit(solution)/shard_map/pallas_call | solution.py:1429
  248.1 0.0 copy-done.1
  248.1 0.8 copy.42
  248.9 0.0 copy-done
  248.9 1.0 copy.43
Async XLA Ops:
  152.1 88.0 %copy-start.2 = (f32[68]{0:T(128)S(1)}, f32[68]{0:T(128)}, u32[]{:S(2)}) copy-start(f32[68]{0:T(128)} %param.25) | copy-start | bytes 820
  152.1 88.0 %copy-start.3 = (f32[68]{0:T(128)S(1)}, f32[68]{0:T(128)}, u32[]{:S(2)}) copy-start(f32[68]{0:T(128)} %param.30) | copy-start | bytes 820
  152.1 88.0 %copy-start.4 = (f32[68]{0:T(128)S(1)}, f32[68]{0:T(128)}, u32[]{:S(2)}) copy-start(f32[68]{0:T(128)} %param.35) | copy-start | bytes 820
  241.3 6.8 %copy-start.1 = (bf16[256,1024]{1,0:T(8,128)(2,1)S(1)}, bf16[256,1024]{1,0:T(8,128)(2,1)}, u32[]{:S(2)}) copy-start(bf16[256,1024]{1,0:T(8,128)(2,1)} %get-tuple-element.83) | copy-start | bytes 1572868
  241.3 7.6 %copy-start = (f32[256,1024]{1,0:T(8,128)S(1)}, f32[256,1024]{1,0:T(8,128)}, u32[]{:S(2)}) copy-start(f32[256,1024]{1,0:T(8,128)} %get-tuple-element.84) | copy-start | bytes 3145732
